TPU v7x, 32 devices: a whole 2x2x4 slice. The times are simulated.
32 devices in a mesh: dp: 8 (over y, x, core), tensor: 4 (over z).
Axes of the slice: x: 2, y: 2, z: 4, core: 2. Of those that a mesh axis runs over, the one named last changes fastest.
Arguments:
- layer_in: bfloat16 [16, 1024, 1024], P('dp', 'tensor'), may hold values from -6 to 6
- seq_lengths: int32 [16], P('dp'), may hold values from 256 to 1024, as said below
- out_grad: bfloat16 [16, 1024, 1024], P('dp', 'tensor'), may hold values from -6 to 6
- norm_gain: float32 [1024], replicated, may hold values from 0.5 to 1.5
- mixer_weight: bfloat16 [1024, 2, 1536], P('dp', None, 'tensor'), may hold values from -0.1875 to 0.1875
- step_weight: bfloat16 [1024, 24], P('dp', 'tensor'), may hold values from -0.09375 to 0.09375
- state_weight: bfloat16 [1024, 2, 128], P('dp'), may hold values from -0.1875 to 0.1875
- query_weight: bfloat16 [1024, 512], P('dp', 'tensor'), may hold values from -0.1875 to 0.1875
- key_value_weight: bfloat16 [1024, 2, 128], P('dp'), may hold values from -0.1875 to 0.1875
- conv_channels: float32 [4, 1536], P(None, 'tensor'), may hold values from -3 to 3
- conv_states: float32 [4, 2, 128], replicated, may hold values from -3 to 3
- step_bias: float32 [24], P('tensor'), may hold values from -7 to -3
- decay_log: float32 [24], P('tensor'), may hold values from 0 to 1.5
- skip_scale: float32 [24], P('tensor'), may hold values from 0.5 to 1.5
- group_gain: float32 [1536], P('tensor'), may hold values from 0.5 to 1.5
- mamba_proj: bfloat16 [1536, 1024], P('tensor', 'dp'), may hold values from -0.15625 to 0.15625
- attn_proj: bfloat16 [512, 1024], P('tensor', 'dp'), may hold values from -1 to 1
- ffn_gain: float32 [1024], replicated, may hold values from 0.5 to 1.5
- ffn_weight: bfloat16 [1024, 2, 2048], P('dp', None, 'tensor'), may hold values from -0.1875 to 0.1875
- ffn_down: bfloat16 [2048, 1024], P('tensor', 'dp'), may hold values from -0.125 to 0.125
Outputs:
- layer_out: bfloat16 [16, 1024, 1024], P('dp', 'tensor')
- input_grad: bfloat16 [16, 1024, 1024], P('dp', 'tensor')
- grad_norm_gain: float32 [1024], replicated
- grad_mixer_weight: float32 [1024, 2, 1536], P('dp', None, 'tensor')
- grad_step_weight: float32 [1024, 24], P('dp', 'tensor')
- grad_state_weight: float32 [1024, 2, 128], P('dp')
- grad_query_weight: float32 [1024, 512], P('dp', 'tensor')
- grad_keyval_weight: float32 [1024, 2, 128], P('dp')
- grad_conv_channels: float32 [4, 1536], P(None, 'tensor')
- grad_conv_states: float32 [4, 2, 128], replicated
- grad_step_bias: float32 [24], P('tensor')
- grad_decay_log: float32 [24], P('tensor')
- grad_skip_scale: float32 [24], P('tensor')
- grad_group_gain: float32 [1536], P('tensor')
- grad_mamba_proj: float32 [1536, 1024], P('tensor', 'dp')
- grad_attn_proj: float32 [512, 1024], P('tensor', 'dp')
- grad_ffn_gain: float32 [1024], replicated
- grad_ffn_weight: float32 [1024, 2, 2048], P('dp', None, 'tensor')
- grad_ffn_down: float32 [2048, 1024], P('tensor', 'dp')
Inputs may be any that keep to these rules, and one draw needn't show every extreme that they name: `seq_lengths`: among the 2 sequences of each index of dp, one has the full length 1024.
All inputs are finite; a program needn't handle non-finite values.
Results may differ from a plain program's by a relative error of at most 0.018.
Values may be sent and summed in bfloat16 or wider, within the bound.
A program may use at most 192 MiB of HBM per device.

v0:
```python
from functools import partial

import jax
import jax.numpy as jnp
from jax import lax
from jax.sharding import PartitionSpec as P

HEAD_SIZE = 64
N = 128
KCONV = 4
QUERY_HEADS = 8
KEY_VALUE_HEADS = 2
GH = 6


EPS = 1e-05
THETA = 10000.0
MASKED = -1e30


def product(left, right):
    return jnp.dot(left, right, preferred_element_type=jnp.float32)


def silu_act(values):
    return values / (1.0 + jnp.exp(-values))


def softplus(values):
    return jnp.log1p(jnp.exp(-jnp.abs(values))) + jnp.maximum(values, 0.0)


def rms_norm(values, gain_vec):
    return values * lax.rsqrt(jnp.mean(values * values, axis=-1, keepdims=True) + EPS) * gain_vec


def causal_conv(values, kernel):
    seq_count = values.shape[0]
    padded = jnp.concatenate(
        [jnp.zeros((KCONV - 1, values.shape[1]), values.dtype), values], axis=0
    )
    summed = jnp.zeros_like(values)
    for offset in range(KCONV):
        summed = summed + padded[offset : offset + seq_count] * kernel[offset]
    return summed


def rotary(values):
    seq_count = values.shape[0]
    head_count = values.shape[1] // HEAD_SIZE
    half_dim = HEAD_SIZE // 2
    freqs = THETA ** (-jnp.arange(half_dim, dtype=jnp.float32) * 2.0 / HEAD_SIZE)
    angles = jnp.arange(seq_count, dtype=jnp.float32)[:, None] * freqs[None, :]
    cosine = jnp.cos(angles)[:, None, :]
    sine = jnp.sin(angles)[:, None, :]
    shaped = values.reshape(seq_count, head_count, HEAD_SIZE)
    first_half = shaped[..., :half_dim]
    second_half = shaped[..., half_dim:]
    turned = jnp.concatenate(
        [first_half * cosine - second_half * sine, second_half * cosine + first_half * sine],
        axis=-1,
    )
    return turned.reshape(seq_count, head_count * HEAD_SIZE)


def attention_front(query_proj, key_part):
    return (rotary(query_proj) * HEAD_SIZE ** (-0.5), rotary(key_part))


def mamba_front(chan_in, state_in, step_in, conv_chan, conv_state, bias_vec, decay_vec):
    chan_act = silu_act(causal_conv(chan_in, conv_chan))
    state_act = silu_act(causal_conv(state_in, conv_state))
    step_act = softplus(step_in + bias_vec)
    cumul = jnp.cumsum(-jnp.exp(decay_vec) * step_act, axis=0)
    return (chan_act, state_act, step_act, cumul)


def head_mix(gram_mat, cumul_head, step_head, chan_head):
    seq_count = gram_mat.shape[0]
    causal = jnp.arange(seq_count)[:, None] >= jnp.arange(seq_count)[None, :]
    spread = jnp.where(causal, cumul_head[:, None] - cumul_head[None, :], 0.0)
    mixing = jnp.where(causal, gram_mat * jnp.exp(spread), 0.0)
    return (mixing, chan_head * step_head[:, None])


def mamba_tail(state_out, chan_act, gate_val, skip_vec, gain_vec):
    seq_count, columns = chan_act.shape
    skipped = state_out + chan_act * jnp.repeat(skip_vec, HEAD_SIZE)
    gated = skipped * silu_act(gate_val)
    grouped = gated.reshape(seq_count, columns // (GH * HEAD_SIZE), GH * HEAD_SIZE)
    normed = grouped * lax.rsqrt(jnp.mean(grouped * grouped, axis=-1, keepdims=True) + EPS)
    return normed.reshape(seq_count, columns) * gain_vec


def swiglu(gate_up):
    half_cols = gate_up.shape[1] // 2
    return silu_act(gate_up[:, :half_cols]) * gate_up[:, half_cols:]


def head_forward(gram_mat, items):
    cumul_head, step_head, chan_head = items
    mixing, inputs = head_mix(gram_mat, cumul_head, step_head, chan_head)
    return product(mixing.astype(jnp.bfloat16), inputs.astype(jnp.bfloat16))


def head_backward(gram_mat, gram_grad, items):
    cumul_head, step_head, chan_head, grad_head = items
    mixed_pair, pull = jax.vjp(head_mix, gram_mat, cumul_head, step_head, chan_head)
    mixing_low = mixed_pair[0].astype(jnp.bfloat16)
    inputs_low = mixed_pair[1].astype(jnp.bfloat16)
    grad_inputs = product(mixing_low.T, grad_head)
    grad_mixing = product(grad_head, inputs_low.T)
    grad_gram, grad_cumul, grad_step, grad_chan = pull((grad_mixing, grad_inputs))
    return (gram_grad + grad_gram, (grad_cumul, grad_step, grad_chan))


def score_block(query_block, start, keys_low, seq_len):
    block_rows = query_block.shape[0]
    scores = product(query_block, keys_low.T)
    row_pos = start + jnp.arange(block_rows, dtype=jnp.int32)[:, None]
    col_pos = jnp.arange(keys_low.shape[0], dtype=jnp.int32)[None, :]
    allowed = (col_pos <= row_pos) & (col_pos < seq_len)
    return jnp.where(allowed, scores, MASKED)


def attention_forward(queries, keys_low, values_low, seq_len):
    seq_count, head_count, head_dim = queries.shape
    block_rows = min(512, seq_count)
    block_count = seq_count // block_rows
    flat_queries = queries.transpose(1, 0, 2).reshape(
        head_count * block_count, block_rows, head_dim
    )
    starts = jnp.tile(jnp.arange(block_count, dtype=jnp.int32) * block_rows, head_count)

    def forward_block(items):
        query_block, start = items
        scores = score_block(query_block, start, keys_low, seq_len)
        row_peak = jnp.max(scores, axis=-1, keepdims=True)
        exp_scores = jnp.exp(scores - row_peak)
        row_total = jnp.sum(exp_scores, axis=-1, keepdims=True)
        probs = (exp_scores / row_total).astype(jnp.bfloat16)
        return (product(probs, values_low), (row_peak + jnp.log(row_total))[:, 0])

    block_out, log_sums = lax.map(forward_block, (flat_queries, starts))
    merged = (
        block_out.reshape(head_count, seq_count, head_dim)
        .transpose(1, 0, 2)
        .reshape(seq_count, head_count * head_dim)
    )
    return (merged, log_sums)


def attention_backward(queries, keys_low, values_low, grad_out, log_sums, seq_len):
    seq_count, head_count, head_dim = queries.shape
    block_rows = min(512, seq_count)
    block_count = seq_count // block_rows
    flat_queries = queries.transpose(1, 0, 2).reshape(
        head_count * block_count, block_rows, head_dim
    )
    flat_grads = (
        grad_out.reshape(seq_count, head_count, head_dim)
        .transpose(1, 0, 2)
        .reshape(head_count * block_count, block_rows, head_dim)
    )
    starts = jnp.tile(jnp.arange(block_count, dtype=jnp.int32) * block_rows, head_count)

    def backward_block(carry, items):
        key_grad, value_grad = carry
        query_block, start, grad_block, log_block = items
        scores = score_block(query_block, start, keys_low, seq_len)
        probs = jnp.exp(scores - log_block[:, None])
        value_grad = value_grad + product(probs.astype(jnp.bfloat16).T, grad_block)
        grad_probs = product(grad_block, values_low.T)
        inner = jnp.sum(probs * grad_probs, axis=-1, keepdims=True)
        grad_scores = (probs * (grad_probs - inner)).astype(jnp.bfloat16)
        key_grad = key_grad + product(grad_scores.T, query_block)
        return ((key_grad, value_grad), product(grad_scores, keys_low))

    empty = jnp.zeros((seq_count, head_dim), jnp.float32)
    (key_grad, value_grad), query_grad = lax.scan(
        backward_block, (empty, empty), (flat_queries, starts, flat_grads, log_sums)
    )
    query_grad = (
        query_grad.reshape(head_count, seq_count, head_dim)
        .transpose(1, 0, 2)
        .reshape(seq_count, head_count * head_dim)
    )
    return (query_grad, key_grad, value_grad)


def add_tuples(first_tuple, second_tuple):
    if first_tuple is None:
        return second_tuple
    return tuple((left + right for left, right in zip(first_tuple, second_tuple)))


def body(
    layer_in,
    seq_lengths,
    out_grad,
    norm_gain,
    mixer_weight,
    step_weight,
    state_weight,
    query_weight,
    key_value_weight,
    conv_channels,
    conv_states,
    step_bias,
    decay_log,
    skip_scale,
    group_gain,
    mamba_proj,
    attn_proj,
    ffn_gain,
    ffn_weight,
    ffn_down,
):
    gathered = (
        lax.all_gather(mixer_weight, "dp", axis=0, tiled=True),
        lax.all_gather(step_weight, "dp", axis=0, tiled=True),
        lax.all_gather(state_weight, "dp", axis=0, tiled=True),
        lax.all_gather(query_weight, "dp", axis=0, tiled=True),
        lax.all_gather(key_value_weight, "dp", axis=0, tiled=True),
        lax.all_gather(mamba_proj, "dp", axis=1, tiled=True),
        lax.all_gather(attn_proj, "dp", axis=1, tiled=True),
        lax.all_gather(ffn_weight, "dp", axis=0, tiled=True),
        lax.all_gather(ffn_down, "dp", axis=1, tiled=True),
    )
    (
        mixer_full,
        step_full,
        state_full,
        query_full,
        keyval_full,
        mamba_full,
        attn_full,
        ffn_full,
        down_full,
    ) = gathered
    model_dim = mixer_full.shape[0]
    chans = mixer_full.shape[2]
    heads_dev = step_full.shape[1]
    query_head_count = query_full.shape[1] // HEAD_SIZE
    hidden_dev = ffn_full.shape[2]
    rows_dev = layer_in.shape[1]
    seq_total = rows_dev * lax.axis_size("tensor")
    tensor_position = lax.axis_index("tensor")
    key_value_head = tensor_position * query_head_count // (QUERY_HEADS // KEY_VALUE_HEADS)
    mixer_mat = mixer_full.reshape(model_dim, 2 * chans)
    state_mat = state_full.reshape(model_dim, 2 * N)
    kv_mat = lax.dynamic_slice_in_dim(
        keyval_full, key_value_head * HEAD_SIZE, HEAD_SIZE, 2
    ).reshape(model_dim, 2 * HEAD_SIZE)
    ffn_mat = ffn_full.reshape(model_dim, 2 * hidden_dev)
    conv_state_mat = conv_states.reshape(KCONV, 2 * N)
    positions = tensor_position * rows_dev + jnp.arange(rows_dev, dtype=jnp.int32)
    layer_rows = []
    input_rows = []
    small_sums = None
    reduced = None
    for micro_step in range(layer_in.shape[0]):
        rows_in = layer_in[micro_step].astype(jnp.float32)
        seq_len = seq_lengths[micro_step]
        valid_rows = (positions < seq_len).astype(jnp.float32)[:, None]
        normed_one, norm_one_pull = jax.vjp(rms_norm, rows_in, norm_gain)
        whole_one = lax.all_gather(normed_one.astype(jnp.bfloat16), "tensor", axis=0, tiled=True)
        gate_chan = product(whole_one, mixer_mat)
        step_in = product(whole_one, step_full)
        state_in = product(whole_one, state_mat)
        query_proj = product(whole_one, query_full)
        keyval_proj = product(whole_one, kv_mat)
        front_out, front_pull = jax.vjp(
            mamba_front,
            gate_chan[:, chans:],
            state_in,
            step_in,
            conv_channels,
            conv_state_mat,
            step_bias,
            decay_log,
        )
        chan_act, state_act, step_act, cumul = front_out
        state_low = state_act.astype(jnp.bfloat16)
        state_b = state_low[:, :N]
        state_c = state_low[:, N:]
        gram_mat = product(state_c, state_b.T)
        per_head = (
            cumul.T,
            step_act.T,
            chan_act.reshape(seq_total, heads_dev, HEAD_SIZE).transpose(1, 0, 2),
        )
        head_out = lax.map(partial(head_forward, gram_mat), per_head)
        state_out = head_out.transpose(1, 0, 2).reshape(seq_total, chans)
        tail_out, tail_pull = jax.vjp(
            mamba_tail, state_out, chan_act, gate_chan[:, :chans], skip_scale, group_gain
        )
        tail_low = tail_out.astype(jnp.bfloat16)
        rotated, rotate_pull = jax.vjp(attention_front, query_proj, keyval_proj[:, :HEAD_SIZE])
        query_low = rotated[0].astype(jnp.bfloat16).reshape(seq_total, query_head_count, HEAD_SIZE)
        key_low = rotated[1].astype(jnp.bfloat16)
        value_low = keyval_proj[:, HEAD_SIZE:].astype(jnp.bfloat16)
        attn_out, log_sums = attention_forward(query_low, key_low, value_low, seq_len)
        attn_low = attn_out.astype(jnp.bfloat16)
        mixed = lax.psum_scatter(
            product(tail_low, mamba_full) + product(attn_low, attn_full),
            "tensor",
            scatter_dimension=0,
            tiled=True,
        )
        hidden = rows_in + mixed
        normed_two, norm_two_pull = jax.vjp(rms_norm, hidden, ffn_gain)
        whole_two = lax.all_gather(normed_two.astype(jnp.bfloat16), "tensor", axis=0, tiled=True)
        gate_up = product(whole_two, ffn_mat)
        act_value, act_pull = jax.vjp(swiglu, gate_up)
        act_low = act_value.astype(jnp.bfloat16)
        ffn_out = lax.psum_scatter(
            product(act_low, down_full).astype(jnp.bfloat16),
            "tensor",
            scatter_dimension=0,
            tiled=True,
        ).astype(jnp.float32)
        layer_rows.append((valid_rows * (hidden + ffn_out)).astype(jnp.bfloat16))
        grad_rows = valid_rows * out_grad[micro_step].astype(jnp.float32)
        grad_whole = lax.all_gather(grad_rows.astype(jnp.bfloat16), "tensor", axis=0, tiled=True)
        grad_down = product(act_low.T, grad_whole)
        (grad_gate_up,) = act_pull(product(grad_whole, down_full.T))
        gate_up_low = grad_gate_up.astype(jnp.bfloat16)
        grad_ffn = product(whole_two.T, gate_up_low)
        grad_normed_two = lax.psum_scatter(
            product(gate_up_low, ffn_mat.T), "tensor", scatter_dimension=0, tiled=True
        )
        grad_hidden, grad_fgain = norm_two_pull(grad_normed_two)
        grad_hidden = grad_hidden + grad_rows
        grad_mixed = lax.all_gather(grad_hidden.astype(jnp.bfloat16), "tensor", axis=0, tiled=True)
        grad_mamba = product(tail_low.T, grad_mixed)
        grad_state_out, grad_chan_tail, grad_gate, grad_skip, grad_ggain = tail_pull(
            product(grad_mixed, mamba_full.T)
        )
        state_grad_low = (
            grad_state_out.astype(jnp.bfloat16)
            .reshape(seq_total, heads_dev, HEAD_SIZE)
            .transpose(1, 0, 2)
        )
        gram_grad, head_grads = lax.scan(
            partial(head_backward, gram_mat),
            jnp.zeros(gram_mat.shape, jnp.float32),
            per_head + (state_grad_low,),
        )
        grad_cumul, grad_step, grad_chan_heads = head_grads
        grad_chan = grad_chan_tail + grad_chan_heads.transpose(1, 0, 2).reshape(seq_total, chans)
        gram_low = gram_grad.astype(jnp.bfloat16)
        grad_state = jnp.concatenate(
            [product(gram_low.T, state_c), product(gram_low, state_b)], axis=1
        )
        (
            grad_chan_in,
            grad_state_in,
            grad_step_in,
            grad_conv_c,
            grad_conv_s,
            grad_bias,
            grad_decay,
        ) = front_pull((grad_chan, grad_state, grad_step.T, grad_cumul.T))
        grad_attn = product(attn_low.T, grad_mixed)
        attn_grad_low = product(grad_mixed, attn_full.T).astype(jnp.bfloat16)
        grad_query_rot, grad_key_rot, grad_value = attention_backward(
            query_low, key_low, value_low, attn_grad_low, log_sums, seq_len
        )
        grad_query_proj, grad_key_proj = rotate_pull((grad_query_rot, grad_key_rot))
        proj_grad_low = jnp.concatenate([grad_gate, grad_chan_in], axis=1).astype(jnp.bfloat16)
        step_grad_low = grad_step_in.astype(jnp.bfloat16)
        state_in_low = grad_state_in.astype(jnp.bfloat16)
        query_grad_low = grad_query_proj.astype(jnp.bfloat16)
        kv_grad_low = jnp.concatenate([grad_key_proj, grad_value], axis=1).astype(jnp.bfloat16)
        batch_grads = (
            product(whole_one.T, proj_grad_low),
            product(whole_one.T, step_grad_low),
            product(whole_one.T, state_in_low),
            product(whole_one.T, query_grad_low),
            product(whole_one.T, kv_grad_low),
            grad_mamba,
            grad_attn,
            grad_ffn,
            grad_down,
        )
        summed = product(proj_grad_low, mixer_mat.T) + product(step_grad_low, step_full.T)
        summed = summed + product(state_in_low, state_mat.T) + product(query_grad_low, query_full.T)
        grad_normed_one = lax.psum_scatter(
            summed + product(kv_grad_low, kv_mat.T), "tensor", scatter_dimension=0, tiled=True
        )
        grad_input, grad_ngain = norm_one_pull(grad_normed_one)
        input_rows.append((grad_input + grad_hidden).astype(jnp.bfloat16))
        small_sums = add_tuples(
            small_sums,
            (
                grad_conv_c,
                grad_conv_s,
                grad_bias,
                grad_decay,
                grad_skip,
                grad_ggain,
                grad_ngain,
                grad_fgain,
            ),
        )
        (
            grad_mixer,
            grad_step_w,
            grad_state_w,
            grad_query_w,
            grad_kv_w,
            grad_mamba_w,
            grad_attn_w,
            grad_ffn_w,
            grad_down_w,
        ) = batch_grads
        kv_whole = lax.dynamic_update_slice_in_dim(
            jnp.zeros(keyval_full.shape, jnp.float32),
            grad_kv_w.reshape(model_dim, 2, HEAD_SIZE),
            key_value_head * HEAD_SIZE,
            2,
        )
        reduced = add_tuples(
            reduced,
            (
                lax.psum_scatter(
                    grad_mixer.reshape(mixer_full.shape), "dp", scatter_dimension=0, tiled=True
                ),
                lax.psum_scatter(grad_step_w, "dp", scatter_dimension=0, tiled=True),
                lax.psum_scatter(
                    grad_state_w.reshape(state_full.shape), "dp", scatter_dimension=0, tiled=True
                ),
                lax.psum_scatter(grad_query_w, "dp", scatter_dimension=0, tiled=True),
                lax.psum_scatter(kv_whole, "dp", scatter_dimension=0, tiled=True),
                lax.psum_scatter(grad_mamba_w, "dp", scatter_dimension=1, tiled=True),
                lax.psum_scatter(grad_attn_w, "dp", scatter_dimension=1, tiled=True),
                lax.psum_scatter(
                    grad_ffn_w.reshape(ffn_full.shape), "dp", scatter_dimension=0, tiled=True
                ),
                lax.psum_scatter(grad_down_w, "dp", scatter_dimension=1, tiled=True),
            ),
        )
    small = lax.psum(small_sums, "dp")
    shared = (
        lax.psum(reduced[2].astype(jnp.bfloat16), "tensor").astype(jnp.float32),
        lax.psum(reduced[4].astype(jnp.bfloat16), "tensor").astype(jnp.float32),
        lax.psum(small[1].astype(jnp.bfloat16), "tensor").astype(jnp.float32),
        lax.psum(small[6].astype(jnp.bfloat16), "tensor").astype(jnp.float32),
        lax.psum(small[7].astype(jnp.bfloat16), "tensor").astype(jnp.float32),
    )
    return (
        jnp.stack(layer_rows),
        jnp.stack(input_rows),
        shared[3],
        reduced[0],
        reduced[1],
        shared[0],
        reduced[3],
        shared[1],
        small[0],
        shared[2].reshape(conv_states.shape),
        small[2],
        small[3],
        small[4],
        small[5],
        reduced[5],
        reduced[6],
        shared[4],
        reduced[7],
        reduced[8],
    )


def solution(mesh):
    return jax.shard_map(
        body,
        mesh=mesh,
        in_specs=(
            P("dp", "tensor", None),
            P("dp"),
            P("dp", "tensor", None),
            P(),
            P("dp", None, "tensor"),
            P("dp", "tensor"),
            P("dp", None, None),
            P("dp", "tensor"),
            P("dp", None, None),
            P(None, "tensor"),
            P(),
            P("tensor"),
            P("tensor"),
            P("tensor"),
            P("tensor"),
            P("tensor", "dp"),
            P("tensor", "dp"),
            P(),
            P("dp", None, "tensor"),
            P("tensor", "dp"),
        ),
        out_specs=(
            P("dp", "tensor", None),
            P("dp", "tensor", None),
            P(),
            P("dp", None, "tensor"),
            P("dp", "tensor"),
            P("dp", None, None),
            P("dp", "tensor"),
            P("dp", None, None),
            P(None, "tensor"),
            P(),
            P("tensor"),
            P("tensor"),
            P("tensor"),
            P("tensor"),
            P("tensor", "dp"),
            P("tensor", "dp"),
            P(),
            P("dp", None, "tensor"),
            P("tensor", "dp"),
        ),
        check_vma=False,
    )
```

profile of v0, /device:TPU:0, one launch (start us, length us, event | category | flops | bytes accessed | tf_op | source)
XLA Modules:
  0.0 2092.7 jit_solution(523727424495722480)
XLA Ops:
  91.0 43.0 %all-gather.12.cloned.1.call-done = bf16[1024,1024]{1,0:T(8,128)(2,1)} async-done(((bf16[256,1024]{1,0:T(8,128)(2,1)}), bf16[1024,1024]{1,0:T(8,128)(2,1)}) %all-gather.12.cloned.1.call-update) | async-done | bytes 2097168 | tf_op jit(solution)/shard_map/all_gather | solution.py:267
  327.8 46.4 %reduce-scatter.18.cloned.1.call-done = f32[256,1024]{1,0:T(8,128)} async-done(((f32[1024,1024]{1,0:T(8,128)}), f32[256,1024]{1,0:T(8,128)}) %reduce-scatter.18.cloned.1.call-update) | async-done | bytes 1048592 | tf_op jit(solution)/shard_map/reduce_scatter | solution.py:305
  374.2 79.5 %reduce-scatter.14.cloned.1.call-done = f32[256,1024]{1,0:T(8,128)} async-done(((f32[1024,1024]{1,0:T(8,128)}), f32[256,1024]{1,0:T(8,128)}) %reduce-scatter.14.cloned.1.call-update) | async-done | bytes 1048592 | tf_op jit(solution)/shard_map/reduce_scatter | solution.py:305
  487.4 44.6 %all-gather.16.cloned.1.call-done = bf16[1024,1024]{1,0:T(8,128)(2,1)} async-done(((bf16[256,1024]{1,0:T(8,128)(2,1)}), bf16[1024,1024]{1,0:T(8,128)(2,1)}) %all-gather.16.cloned.1.call-update) | async-done | bytes 2097168 | tf_op jit(solution)/shard_map/all_gather | solution.py:313
  556.2 47.5 %all-gather.26.cloned.1.call-done = bf16[1024,1024]{1,0:T(8,128)(2,1)} async-done(((bf16[256,1024]{1,0:T(8,128)(2,1)}), bf16[1024,1024]{1,0:T(8,128)(2,1)}) %all-gather.26.cloned.1.call-update) | async-done | bytes 2097168 | tf_op jit(solution)/shard_map/all_gather | solution.py:325
  616.9 75.6 %reduce-scatter.22.cloned.1.call-done = f32[256,1024]{1,0:T(8,128)} async-done(((f32[1024,1024]{1,0:T(8,128)}), f32[256,1024]{1,0:T(8,128)}) %reduce-scatter.22.cloned.1.call-update) | async-done | bytes 1048592 | tf_op jit(solution)/shard_map/reduce_scatter | solution.py:330
  696.6 45.8 %all-gather.24.cloned.1.call-done = bf16[1024,1024]{1,0:T(8,128)(2,1)} async-done(((bf16[256,1024]{1,0:T(8,128)(2,1)}), bf16[1024,1024]{1,0:T(8,128)(2,1)}) %all-gather.24.cloned.1.call-update) | async-done | bytes 2097168 | tf_op jit(solution)/shard_map/all_gather | solution.py:313
  749.0 39.6 %all-gather.30.cloned.1.call-done = bf16[1024,1024]{1,0:T(8,128)(2,1)} async-done(((bf16[256,1024]{1,0:T(8,128)(2,1)}), bf16[1024,1024]{1,0:T(8,128)(2,1)}) %all-gather.30.cloned.1.call-update) | async-done | bytes 2097168 | tf_op jit(solution)/shard_map/all_gather | solution.py:325
  810.6 66.6 %reduce-scatter.26.cloned.1.call-done = f32[256,1024]{1,0:T(8,128)} async-done(((f32[1024,1024]{1,0:T(8,128)}), f32[256,1024]{1,0:T(8,128)}) %reduce-scatter.26.cloned.1.call-update) | async-done | bytes 1048592 | tf_op jit(solution)/shard_map/reduce_scatter | solution.py:330
  879.3 44.5 %reduce-scatter.16.cloned.1.call-done = bf16[256,1024]{1,0:T(8,128)(2,1)} async-done(((bf16[1024,1024]{1,0:T(8,128)(2,1)}), bf16[256,1024]{1,0:T(8,128)(2,1)}) %reduce-scatter.16.cloned.1.call-update) | async-done | bytes 524304 | tf_op jit(solution)/shard_map/reduce_scatter | solution.py:317
  923.8 45.5 %reduce-scatter.20.cloned.1.call-done = bf16[256,1024]{1,0:T(8,128)(2,1)} async-done(((bf16[1024,1024]{1,0:T(8,128)(2,1)}), bf16[256,1024]{1,0:T(8,128)(2,1)}) %reduce-scatter.20.cloned.1.call-update) | async-done | bytes 524304 | tf_op jit(solution)/shard_map/reduce_scatter | solution.py:317
  975.3 44.7 %all-gather.32.cloned.1.call-done = bf16[1024,1024]{1,0:T(8,128)(2,1)} async-done(((bf16[256,1024]{1,0:T(8,128)(2,1)}), bf16[1024,1024]{1,0:T(8,128)(2,1)}) %all-gather.32.cloned.1.call-update) | async-done | bytes 2097168 | tf_op jit(solution)/shard_map/all_gather | solution.py:335
  1024.2 42.5 %all-gather.28.cloned.1.call-done = bf16[1024,1024]{1,0:T(8,128)(2,1)} async-done(((bf16[256,1024]{1,0:T(8,128)(2,1)}), bf16[1024,1024]{1,0:T(8,128)(2,1)}) %all-gather.28.cloned.1.call-update) | async-done | bytes 2097168 | tf_op jit(solution)/shard_map/all_gather | solution.py:335
  1080.2 61.6 %while.112 = (s32[]{:T(128)}, f32[1024,1024]{1,0:T(8,128)}, f32[6,1024]{1,0:T(8,128)S(1)}, f32[6,1024]{1,0:T(8,128)S(1)}, f32[6,1024,64]{1,2,0:T(8,128)S(1)}, /*...) while((s32[]{:T(128)}, f32[1024,1024]{1,0:T(8,128)}, ...), condition=%wide.region_33.34_spmd.clone, body=%wide.region_29.33_spmd.clone.sunk | while | flops 287636480 | bytes 26822796 | solution.py:345
  1148.3 61.7 %while.114 = (s32[]{:T(128)}, f32[1024,1024]{1,0:T(8,128)}, f32[6,1024]{1,0:T(8,128)S(1)}, f32[6,1024]{1,0:T(8,128)S(1)}, f32[6,1024,64]{1,2,0:T(8,128)S(1)}, /*...) while((s32[]{:T(128)}, f32[1024,1024]{1,0:T(8,128)}, ...), condition=%wide.region_48.49_spmd.clone, body=%wide.region_44.48_spmd.clone.sunk | while | flops 287636480 | bytes 26822796 | solution.py:345
  1218.7 48.8 %while.115 = (s32[]{:T(128)}, f32[1024,64]{0,1:T(8,128)}, f32[1024,64]{0,1:T(8,128)}, f32[4,512,64]{1,2,0:T(8,128)}, s32[4]{0:T(128)}, /*index=5*/s32[]{:T(128)}...) while((s32[]{:T(128)}, f32[1024,64]{0,1:T(8,128)}, ...), condition=%wide.region_53.54_spmd.clone, body=%wide.region_51.53_spmd.clone.sunk | while | flops 341050368 | bytes 17975968 | solution.py:180
  1274.4 44.3 %while.113 = (s32[]{:T(128)}, f32[1024,64]{0,1:T(8,128)}, f32[1024,64]{0,1:T(8,128)}, f32[4,512,64]{1,2,0:T(8,128)}, s32[4]{0:T(128)}, /*index=5*/s32[]{:T(128)}...) while((s32[]{:T(128)}, f32[1024,64]{0,1:T(8,128)}, ...), condition=%wide.region_38.39_spmd.clone, body=%wide.region_36.38_spmd.clone.sunk | while | flops 341050368 | bytes 20596992 | solution.py:180
  1536.3 84.2 %all-reduce.63 = (bf16[1024]{0:T(1024)(128)(2,1)S(1)}, bf16[1024,2,128]{2,1,0:T(2,128)(2,1)S(1)}, bf16[1024,2,128]{2,1,0:T(2,128)(2,1)S(1)}, f32[4,384]{1,0:T(4,...) all-reduce(f32[1024]{0:T(1024)S(1)} %add.662, ...), channel_id=1, replica_groups=mesh['dp'=8,'tensor'=4] {'dp'}, use_global_device_ids=true, to_apply=%region_58.59 | all-reduce | flops 529298 | bytes 3179664 | tf_op jit(solution)/shard_map/psum | solution.py:444
  1648.2 34.0 %all-reduce.60.cloned.1.call-done = (f32[1024,2,384]{2,1,0:T(2,128)}, f32[1024,2,512]{2,1,0:T(2,128)}) async-done(((f32[1024,2,384]{2,1,0:T(2,128)}, f32[1024,2,512]{2,1,0:T(2,128)}), (f32[1024,2,384]{2,1,0:T(2,128)}, f32[1024,2,512]{2,1,0:T(2,128)})) %all-reduce.60.cloned.1.call-update) | async-done | bytes 7340048
  1685.9 209.2 %all-reduce.54 = (bf16[1024]{0:T(1024)(128)(2,1)S(1)}, bf16[4,2,128]{2,1,0:T(2,128)(2,1)S(1)}, bf16[1024]{0:T(1024)(128)(2,1)S(1)}) all-reduce(bf16[1024]{0:T(1024)(128)(2,1)S(1)} %get-tuple-element.1205, bf16[4,2,128]{2,1,0:T(2,128)(2,1)S(1)} %reshape.829, ...), channel_id=1, replica_groups=mesh['dp'=8,'tensor'=4] {'tensor'}, use_global_device_ids=true, to_apply=%region_59.60 | all-reduce | flops 3072 | bytes 12288 | tf_op jit(solution)/shard_map/psum | solution.py:449
  1932.9 35.1 %reduce-scatter.30.cloned.1.call-done = f32[128,6]{0,1:T(8,128)} async-done(((f32[1024,6]{0,1:T(8,128)}), f32[128,6]{0,1:T(8,128)}) %reduce-scatter.30.cloned.1.call-update) | async-done | bytes 3088 | tf_op jit(solution)/shard_map/reduce_scatter | solution.py:430
  1968.0 37.7 %reduce-scatter.32.cloned.1.call-done = f32[128,128]{1,0:T(8,128)} async-done(((f32[1024,128]{1,0:T(8,128)}), f32[128,128]{1,0:T(8,128)}) %reduce-scatter.32.cloned.1.call-update) | async-done | bytes 65552 | tf_op jit(solution)/shard_map/reduce_scatter | solution.py:434
  2005.7 38.1 %reduce-scatter.36.cloned.1.call-done = f32[128,128]{1,0:T(8,128)} async-done(((f32[128,1024]{1,0:T(8,128)}), f32[128,128]{1,0:T(8,128)}) %reduce-scatter.36.cloned.1.call-update) | async-done | bytes 65552 | tf_op jit(solution)/shard_map/reduce_scatter | solution.py:437
  2043.8 42.2 %reduce-scatter.34.cloned.1.call-done = f32[384,128]{1,0:T(8,128)} async-done(((f32[384,1024]{1,0:T(8,128)}), f32[384,128]{1,0:T(8,128)}) %reduce-scatter.34.cloned.1.call-update) | async-done | bytes 196624 | tf_op jit(solution)/shard_map/reduce_scatter | solution.py:436
  (1126 shorter events, 1038.8 us)
Async XLA Ops:
  12.7 121.4 %all-gather.12.cloned.1.call-start = ((), (), s32[]{:S(2)}) async-start(), calls=%async_computation.13 | async-start | bytes 2621440 | tf_op jit(solution)/shard_map/all_gather | solution.py:267
  13.4 360.8 %reduce-scatter.18.cloned.1.call-start = ((), (), s32[]{:S(2)}) async-start(), calls=%async_computation.21 | async-start | bytes 5242880 | tf_op jit(solution)/shard_map/reduce_scatter | solution.py:305
  298.6 155.2 %reduce-scatter.14.cloned.1.call-start = ((), (), s32[]{:S(2)}) async-start(), calls=%async_computation.15 | async-start | bytes 5242880 | tf_op jit(solution)/shard_map/reduce_scatter | solution.py:305
  327.0 156.9 %all-gather.18.cloned.1.call-start = ((), (), s32[]{:S(2)}) async-start(), calls=%async_computation.17 | async-start | bytes 2359296 | tf_op jit(solution)/shard_map/all_gather | solution.py:227
  327.6 204.4 %all-gather.16.cloned.1.call-start = ((), (), s32[]{:S(2)}) async-start(), calls=%async_computation.16 | async-start | bytes 2621440 | tf_op jit(solution)/shard_map/all_gather | solution.py:313
  458.5 97.7 %all-gather.20.cloned.1.call-start = ((), (), s32[]{:S(2)}) async-start(), calls=%async_computation.18 | async-start | bytes 1179648 | tf_op jit(solution)/shard_map/all_gather | solution.py:228
  459.3 144.5 %all-gather.26.cloned.1.call-start = ((), (), s32[]{:S(2)}) async-start(), calls=%async_computation.24 | async-start | bytes 2621440 | tf_op jit(solution)/shard_map/all_gather | solution.py:325
  461.9 230.5 %reduce-scatter.22.cloned.1.call-start = ((), (), s32[]{:S(2)}) async-start(), calls=%async_computation.25 | async-start | bytes 5242880 | tf_op jit(solution)/shard_map/reduce_scatter | solution.py:330
  616.8 125.5 %all-gather.24.cloned.1.call-start = ((), (), s32[]{:S(2)}) async-start(), calls=%async_computation.22 | async-start | bytes 2621440 | tf_op jit(solution)/shard_map/all_gather | solution.py:313
  695.7 92.8 %all-gather.30.cloned.1.call-start = ((), (), s32[]{:S(2)}) async-start(), calls=%async_computation.28 | async-start | bytes 2621440 | tf_op jit(solution)/shard_map/all_gather | solution.py:325
  696.3 180.9 %reduce-scatter.26.cloned.1.call-start = ((), (), s32[]{:S(2)}) async-start(), calls=%async_computation.29 | async-start | bytes 5242880 | tf_op jit(solution)/shard_map/reduce_scatter | solution.py:330
  801.6 122.2 %reduce-scatter.16.cloned.1.call-start = ((), (), s32[]{:S(2)}) async-start(), calls=%async_computation.19 | async-start | bytes 2621440 | tf_op jit(solution)/shard_map/reduce_scatter | solution.py:317
  805.8 163.4 %reduce-scatter.20.cloned.1.call-start = ((), (), s32[]{:S(2)}) async-start(), calls=%async_computation.23 | async-start | bytes 2621440 | tf_op jit(solution)/shard_map/reduce_scatter | solution.py:317
  810.5 209.5 %all-gather.32.cloned.1.call-start = ((), (), s32[]{:S(2)}) async-start(), calls=%async_computation.30 | async-start | bytes 2621440 | tf_op jit(solution)/shard_map/all_gather | solution.py:335
  974.6 92.1 %all-gather.28.cloned.1.call-start = ((), (), s32[]{:S(2)}) async-start(), calls=%async_computation.26 | async-start | bytes 2621440 | tf_op jit(solution)/shard_map/all_gather | solution.py:335
  975.2 544.0 %reduce-scatter.28.cloned.1.call-start = ((), (), s32[]{:S(2)}) async-start(), calls=%async_computation.31 | async-start | bytes 5242880 | tf_op jit(solution)/shard_map/reduce_scatter | solution.py:389
  1378.6 155.5 %reduce-scatter.24.cloned.1.call-start = ((), (), s32[]{:S(2)}) async-start(), calls=%async_computation.27 | async-start | bytes 5242880 | tf_op jit(solution)/shard_map/reduce_scatter | solution.py:389
  1393.5 288.6 %all-reduce.60.cloned.1.call-start = ((), (), s32[]{:S(2)}) async-start(), calls=%async_computation.37 | async-start | bytes 14680064
  1425.5 474.7 %all-reduce.62.cloned.1.call-start = ((), (), s32[]{:S(2)}) async-start(), calls=%async_computation.38 | async-start | bytes 262144 | tf_op jit(solution)/shard_map/psum | solution.py:446
  1621.9 311.0 %reduce-scatter.38.cloned.1.call-start = ((), (), s32[]{:S(2)}) async-start(), calls=%async_computation.36 | async-start | bytes 2359296 | tf_op jit(solution)/shard_map/reduce_scatter | solution.py:441
  1627.1 340.9 %reduce-scatter.30.cloned.1.call-start = ((), (), s32[]{:S(2)}) async-start(), calls=%async_computation.32 | async-start | bytes 36864 | tf_op jit(solution)/shard_map/reduce_scatter | solution.py:430
  1630.8 374.9 %reduce-scatter.32.cloned.1.call-start = ((), (), s32[]{:S(2)}) async-start(), calls=%async_computation.33 | async-start | bytes 589824 | tf_op jit(solution)/shard_map/reduce_scatter | solution.py:434
  1635.2 408.6 %reduce-scatter.36.cloned.1.call-start = ((), (), s32[]{:S(2)}) async-start(), calls=%async_computation.35 | async-start | bytes 589824 | tf_op jit(solution)/shard_map/reduce_scatter | solution.py:437
  1640.3 445.7 %reduce-scatter.34.cloned.1.call-start = ((), (), s32[]{:S(2)}) async-start(), calls=%async_computation.34 | async-start | bytes 1769472 | tf_op jit(solution)/shard_map/reduce_scatter | solution.py:436
  (260 other events, 7598.2 us)
Sparse Core Ops, SparseCore 0:
  9.9 29.1 all-gather.13
  41.2 45.9 all-gather.21
  89.3 44.6 all-gather.11
  298.7 75.4 reduce-scatter.17
  376.4 77.2 reduce-scatter.13
  486.1 45.9 all-gather.15
  557.8 45.9 all-gather.25
  616.9 75.4 reduce-scatter.21
  695.9 46.4 all-gather.23
  743.8 44.6 all-gather.29
  801.7 75.4 reduce-scatter.25
  879.3 44.3 reduce-scatter.15
  926.0 43.1 reduce-scatter.19
  974.7 45.2 all-gather.31
  1022.0 44.6 all-gather.27
  1378.7 75.4 reduce-scatter.27
  1456.6 77.4 reduce-scatter.23
  1537.2 144.8 all-reduce.59
  1685.2 202.7 all-reduce.61
  1891.9 40.9 reduce-scatter.37
  1936.7 31.2 reduce-scatter.29
  1971.5 34.1 reduce-scatter.31
  2009.6 34.1 reduce-scatter.35
  2047.5 38.4 reduce-scatter.33
  (2 shorter events, 50.6 us)
where the time goes:
time: 2100 us; the launch traced here: 2090 us
  waiting for transfers between devices  948 us (45%)
  matrix products  393 us (19%)
  blocking collectives  352 us (17%)
  local copies, waits for them, and re-layouts  233 us (11%)
  other arithmetic  144 us (7%)
    dot_general x152, matrix products, product(): return jnp.dot(left, right, preferred_element_type=jnp.float32)  393 us
    psum x1, blocking collectives, body(): lax.psum(small[6].astype(jnp.bfloat16), 'tensor').astype(jnp.float32)  209 us
    reduce_scatter x2, waiting for transfers between devices, body(): lax.psum_scatter(product(gate_up_low, ffn_mat.T), 'tensor', scatter_dimen...  142 us
    reduce_scatter x2, waiting for transfers between devices, body(): lax.psum_scatter(product(tail_low, mamba_full) + product(attn_low, attn_f...  126 us
    all_gather x2, waiting for transfers between devices, body(): lax.all_gather(normed_two.astype(jnp.bfloat16), 'tensor', axis=0, tiled=T...  90.4 us
    reduce_scatter x2, waiting for transfers between devices, body(): lax.psum_scatter(product(act_low, down_full).astype(jnp.bfloat16), 'tenso...  89.9 us
    all_gather x2, waiting for transfers between devices, body(): lax.all_gather(grad_hidden.astype(jnp.bfloat16), 'tensor', axis=0, tiled=...  87.2 us
    all_gather x2, waiting for transfers between devices, body(): lax.all_gather(grad_rows.astype(jnp.bfloat16), 'tensor', axis=0, tiled=True)  87.1 us
  transfers between devices with their start and end apart: 26, of which 23 were waited for; matrix products, arithmetic and copies ran while one was open for 12% of the time, Pallas kernels for 0%

commit v1 on v0

v1 whole, which is shorter than its diff:
```python
import jax
import jax.numpy as jnp
from jax import lax
from jax.experimental import pallas as pl
from jax.experimental.pallas import tpu as pltpu
from jax.sharding import Mesh
from jax.sharding import PartitionSpec as P

HEAD_SIZE = 64
N = 128
KCONV = 4
GH = 6
EPS = 1e-05
THETA = 10000.0
MASKED = -1e30
SWAP = [(0, 1), (1, 0)]


def low(values):
    return values.astype(jnp.bfloat16)


def wide(values):
    return values.astype(jnp.float32)


def dot(left, right):
    return jnp.dot(left, right, preferred_element_type=jnp.float32)


def dot_nt(left, right):
    return lax.dot_general(
        left, right, (((1,), (1,)), ((), ())), preferred_element_type=jnp.float32
    )


def dot_tn(left, right):
    return lax.dot_general(
        left, right, (((0,), (0,)), ((), ())), preferred_element_type=jnp.float32
    )


def dot_fine(left, right):
    high = low(right)
    rest = right - wide(high)
    mid = low(rest)
    last = low(rest - wide(mid))
    return dot(left, high) + dot(left, mid) + dot(left, last)


def dot_by(left, right):
    high = low(left)
    rest = left - wide(high)
    mid = low(rest)
    last = low(rest - wide(mid))
    return dot(high, right) + dot(mid, right) + dot(last, right)


def sigmoid(values):
    return 1.0 / (1.0 + jnp.exp(-values))


def turn(values, cosine, sine):
    lane = lax.broadcasted_iota(jnp.int32, values.shape, 1)
    half = HEAD_SIZE // 2
    up = pltpu.roll(values, 128 - half, 1)
    down = pltpu.roll(values, half, 1)
    return values * cosine + jnp.where(lane % HEAD_SIZE < half, up, down) * sine


def turn_back(values, cosine, sine):
    lane = lax.broadcasted_iota(jnp.int32, values.shape, 1)
    half = HEAD_SIZE // 2
    turned = values * sine
    up = pltpu.roll(turned, 128 - half, 1)
    down = pltpu.roll(turned, half, 1)
    return values * cosine + jnp.where(lane % HEAD_SIZE < half, up, down)


SCALE = HEAD_SIZE ** (-0.5)
ROWS = 256


def key_value_parts(kv, cosine, sine):
    lane = lax.broadcasted_iota(jnp.int32, kv.shape, 1)
    key = jnp.where(lane < HEAD_SIZE, turn(kv, cosine, sine), 0.0)
    value = jnp.where(lane < HEAD_SIZE, 0.0, kv)
    keys = (low(key), low(pltpu.roll(key, HEAD_SIZE, 1)))
    values = (low(pltpu.roll(value, HEAD_SIZE, 1)), low(value))
    return keys, values


def block_scores(query, keys, begin, seq_len):
    scores = dot_nt(query, keys)
    row = lax.broadcasted_iota(jnp.int32, (scores.shape[0], 1), 0) + begin
    col = lax.broadcasted_iota(jnp.int32, scores.shape, 1)
    return jnp.where(col < jnp.minimum(row + 1, seq_len), scores, MASKED)


def attention_forward_kernel(len_ref, q_ref, kv_ref, cos_ref, sin_ref, out_ref, sum_ref):
    seq_len = len_ref[0]
    cosine, sine = cos_ref[...], sin_ref[...]
    keys, values = key_value_parts(kv_ref[...], cosine, sine)
    query = low(turn(q_ref[...], cosine, sine) * SCALE)
    rows = query.shape[0]
    lane = lax.broadcasted_iota(jnp.int32, (ROWS, 128), 1)
    for begin in range(0, rows, ROWS):
        end = begin + ROWS
        outs, sums = [], []
        for head in range(2):
            scores = block_scores(query[begin:end], keys[head][:end], begin, seq_len)
            peak = jnp.max(scores, axis=1, keepdims=True)
            exps = jnp.exp(scores - peak)
            total = jnp.sum(exps, axis=1, keepdims=True)
            probs = low(exps * (1.0 / total))
            outs.append(dot(probs, values[head][:end]))
            sums.append(peak + jnp.log(total))
        out_ref[begin:end, :] = low(outs[0] + outs[1])
        sum_ref[begin:end, :] = jnp.where(lane < HEAD_SIZE, sums[0], sums[1])


def attention_backward_kernel(
    len_ref, q_ref, kv_ref, cos_ref, sin_ref, sum_ref, grad_ref, dq_ref, dkv_ref, dk_acc, dv_acc
):
    seq_len = len_ref[0]
    cosine, sine = cos_ref[...], sin_ref[...]
    keys, values = key_value_parts(kv_ref[...], cosine, sine)
    query = low(turn(q_ref[...], cosine, sine) * SCALE)
    query_t = query.T
    rows = query.shape[0]
    group = pl.program_id(0)
    grad = low(grad_ref[...])
    grad_t = grad.T

    @pl.when(group == 0)
    def _():
        dk_acc[...] = jnp.zeros_like(dk_acc)
        dv_acc[...] = jnp.zeros_like(dv_acc)

    for begin in range(0, rows, ROWS):
        end = begin + ROWS
        dq = jnp.zeros((ROWS, 128), jnp.float32)
        for head in range(2):
            lanes = slice(head * HEAD_SIZE, (head + 1) * HEAD_SIZE)
            scores = block_scores(query[begin:end], keys[head][:end], begin, seq_len)
            at = head * HEAD_SIZE
            probs = jnp.exp(scores - sum_ref[begin:end, at : at + 1])
            dv_acc[:, :end] += dot(grad_t[lanes, begin:end], low(probs))
            dp = dot_nt(grad[begin:end], values[head][:end])
            inner = jnp.sum(probs * dp, axis=1, keepdims=True)
            ds = low(probs * (dp - inner))
            dq = dq + dot(ds, keys[head][:end])
            dk_acc[:, :end] += dot(query_t[lanes, begin:end], ds)
        dq = turn_back(dq * SCALE, cosine[begin:end], sine[begin:end])
        dq_ref[begin:end, :] = low(dq)

    @pl.when(group == pl.num_programs(0) - 1)
    def _():
        both = jnp.concatenate([dk_acc[...], dv_acc[...]], axis=0).T
        lane = lax.broadcasted_iota(jnp.int32, both.shape, 1)
        dkv_ref[...] = low(jnp.where(lane < HEAD_SIZE, turn_back(both, cosine, sine), both))


def attention_specs(rows, group_cols):
    whole = pl.BlockSpec((rows, 128), lambda g: (0, 0))
    return [
        pl.BlockSpec(memory_space=pltpu.SMEM),
        pl.BlockSpec((rows, 128), lambda g: (0, g * (group_cols // 128) + 6)),
        pl.BlockSpec((rows, 128), lambda g: (0, 2 * (group_cols // 128) + 2)),
        whole,
        whole,
    ]


BIG = 60 * 1024 * 1024


def attention_forward(seq_len, proj, cosine, sine, group_cols):
    rows = proj.shape[0]
    pairs = pl.BlockSpec((rows, 128), lambda g: (0, g))
    return pl.pallas_call(
        attention_forward_kernel,
        grid=(2,),
        in_specs=attention_specs(rows, group_cols),
        out_specs=[pairs, pairs],
        out_shape=[
            jax.ShapeDtypeStruct((rows, 256), jnp.bfloat16),
            jax.ShapeDtypeStruct((rows, 256), jnp.float32),
        ],
        compiler_params=pltpu.CompilerParams(vmem_limit_bytes=BIG),
        name="attention_forward",
    )(seq_len, proj, proj, cosine, sine)


def attention_backward(seq_len, proj, cosine, sine, sums, grad, group_cols, grad_at):
    rows = proj.shape[0]
    pairs = pl.BlockSpec((rows, 128), lambda g: (0, g))
    return pl.pallas_call(
        attention_backward_kernel,
        grid=(2,),
        in_specs=attention_specs(rows, group_cols)
        + [pairs, pl.BlockSpec((rows, 128), lambda g: (0, grad_at + g))],
        out_specs=[pairs, pl.BlockSpec((rows, 128), lambda g: (0, 0))],
        out_shape=[
            jax.ShapeDtypeStruct((rows, 256), jnp.bfloat16),
            jax.ShapeDtypeStruct((rows, 128), jnp.bfloat16),
        ],
        scratch_shapes=[
            pltpu.VMEM((HEAD_SIZE, rows), jnp.float32),
            pltpu.VMEM((HEAD_SIZE, rows), jnp.float32),
        ],
        compiler_params=pltpu.CompilerParams(vmem_limit_bytes=BIG),
        name="attention_backward",
    )(seq_len, proj, proj, cosine, sine, sums, grad)


CHUNK = 128
GROUP = GH * HEAD_SIZE
PAIRS = GH // 2
CONV = 2 * GROUP + 2 * N
SHARED = 2048


def triangle():
    row = lax.broadcasted_iota(jnp.int32, (CHUNK, CHUNK), 0)
    col = lax.broadcasted_iota(jnp.int32, (CHUNK, CHUNK), 1)
    return col <= row


def pair_lanes(values, pair):
    lane = lax.broadcasted_iota(jnp.int32, (values.shape[0], 128), 1)
    at = 2 * pair
    return jnp.where(lane < HEAD_SIZE, values[:, at : at + 1], values[:, at + 1 : at + 2])


def split_pair(values):
    lane = lax.broadcasted_iota(jnp.int32, values.shape, 1)
    empty = jnp.zeros_like(values)
    return jnp.concatenate(
        [jnp.where(lane < HEAD_SIZE, values, empty), jnp.where(lane < HEAD_SIZE, empty, values)],
        axis=0,
    )


def conv_pre(buf_ref, taps_ref, begin, size):
    total = buf_ref[5 : 5 + CHUNK, begin : begin + size] * taps_ref[0:1, begin : begin + size]
    for tap in range(1, KCONV):
        total = total + (
            buf_ref[5 + tap : 5 + tap + CHUNK, begin : begin + size]
            * taps_ref[tap : tap + 1, begin : begin + size]
        )
    return total


def load_conv(buf_ref, proj_ref):
    for group in range(2):
        at = group * 1024 + GROUP
        buf_ref[8:, group * GROUP : (group + 1) * GROUP] = proj_ref[:, at : at + GROUP]
    buf_ref[8:, 2 * GROUP :] = proj_ref[:, SHARED : SHARED + 2 * N]


def group_steps(proj_ref, bias_ref, decay_ref, group, lower):
    at = group * 1024 + 896
    raw = proj_ref[:, at : at + 128] + bias_ref[group : group + 1, :]
    step = jnp.log1p(jnp.exp(-jnp.abs(raw))) + jnp.maximum(raw, 0.0)
    rate = -jnp.exp(decay_ref[group : group + 1, :])
    cumul = dot_fine(lower, rate * step)
    return raw, step, rate, cumul


def head_decay(cumul, cumul_t, head, mask):
    spread = cumul[:, head : head + 1] - cumul_t[head : head + 1, :]
    return jnp.exp(jnp.where(mask, spread, MASKED))


def mamba_forward_kernel(
    proj_ref,
    attn_ref,
    taps_ref,
    bias_ref,
    decay_ref,
    skip_ref,
    gain_ref,
    both_ref,
    out_ref,
    states_ref,
    buf_ref,
    state_ref,
):
    chunk = pl.program_id(0)

    @pl.when(chunk == 0)
    def _():
        buf_ref[0:8, :] = jnp.zeros((8, CONV), jnp.float32)
        state_ref[...] = jnp.zeros_like(state_ref)

    load_conv(buf_ref, proj_ref)
    mask = triangle()
    lower = mask.astype(jnp.bfloat16)
    pre = conv_pre(buf_ref, taps_ref, 2 * GROUP, 2 * N)
    state_act = low(pre * sigmoid(pre))
    b_rows, c_rows = state_act[:, :N], state_act[:, N:]
    gram = dot_nt(c_rows, b_rows)
    b_cols = b_rows.T
    for group in range(2):
        cols = slice(group * GROUP, (group + 1) * GROUP)
        _, step, _, cumul = group_steps(proj_ref, bias_ref, decay_ref, group, lower)
        cumul_t = cumul.T
        last = cumul[CHUNK - 1 : CHUNK, :]
        state = state_ref[:, cols]
        states_ref[0, :, cols] = state
        from_state = dot(c_rows, low(state))
        gated = []
        for pair in range(PAIRS):
            at = group * GROUP + pair * 128
            pre = conv_pre(buf_ref, taps_ref, at, 128)
            chan = pre * sigmoid(pre)
            inputs = low(chan * pair_lanes(step, pair))
            mixing = jnp.concatenate(
                [
                    low(gram * head_decay(cumul, cumul_t, 2 * pair + side, mask))
                    for side in range(2)
                ],
                axis=1,
            )
            lanes = slice(pair * 128, (pair + 1) * 128)
            inner = pair_lanes(cumul, pair)
            out = dot(mixing, split_pair(inputs)) + jnp.exp(inner) * from_state[:, lanes]
            out_ref[:, at : at + 128] = out
            last_lanes = pair_lanes(last, pair)
            x_end = low(jnp.exp(last_lanes - inner) * wide(inputs))
            state_ref[:, at : at + 128] = jnp.exp(last_lanes) * state[:, lanes] + dot(
                b_cols, x_end
            )
            gate = proj_ref[:, group * 1024 + pair * 128 : group * 1024 + pair * 128 + 128]
            skipped = out + chan * skip_ref[:, at : at + 128]
            gated.append(skipped * (gate * sigmoid(gate)))
        square = sum(jnp.sum(part * part, axis=1, keepdims=True) for part in gated)
        scale = lax.rsqrt(square * (1.0 / GROUP) + EPS)
        for pair in range(PAIRS):
            at = group * GROUP + pair * 128
            to = group * 512 + pair * 128
            both_ref[:, to : to + 128] = low(gated[pair] * scale * gain_ref[:, at : at + 128])
        to = group * 512 + GROUP
        both_ref[:, to : to + 128] = attn_ref[:, group * 128 : (group + 1) * 128]
    buf_ref[0:8, :] = buf_ref[CHUNK : CHUNK + 8, :]


def mamba_forward(proj, attn, taps, bias, decay, skip, gain):
    rows, columns = proj.shape
    chunks = rows // CHUNK

    def whole(value):
        return pl.BlockSpec(value.shape, lambda k: (0, 0))

    return pl.pallas_call(
        mamba_forward_kernel,
        grid=(chunks,),
        in_specs=[
            pl.BlockSpec((CHUNK, columns), lambda k: (k, 0)),
            pl.BlockSpec((CHUNK, 256), lambda k: (k, 0)),
        ]
        + [whole(value) for value in (taps, bias, decay, skip, gain)],
        out_specs=[
            pl.BlockSpec((CHUNK, 1024), lambda k: (k, 0)),
            pl.BlockSpec((CHUNK, 2 * GROUP), lambda k: (k, 0)),
            pl.BlockSpec((1, N, 2 * GROUP), lambda k: (k, 0, 0)),
        ],
        out_shape=[
            jax.ShapeDtypeStruct((rows, 1024), jnp.bfloat16),
            jax.ShapeDtypeStruct((rows, 2 * GROUP), jnp.float32),
            jax.ShapeDtypeStruct((chunks, N, 2 * GROUP), jnp.float32),
        ],
        scratch_shapes=[
            pltpu.VMEM((CHUNK + 8, CONV), jnp.float32),
            pltpu.VMEM((N, 2 * GROUP), jnp.float32),
        ],
        compiler_params=pltpu.CompilerParams(vmem_limit_bytes=BIG),
        name="mamba_forward",
    )(proj, attn, taps, bias, decay, skip, gain)


def silu_slope(values, sig):
    return sig * (1.0 + values * (1.0 - sig))


def mamba_backward_kernel(
    proj_ref,
    before_ref,
    out_ref,
    states_ref,
    back_ref,
    dq_ref,
    dkv_ref,
    taps_ref,
    bias_ref,
    decay_ref,
    skip_ref,
    gain_ref,
    dproj_ref,
    dtaps_ref,
    dgain_ref,
    dskip_ref,
    dbias_ref,
    ddecay_ref,
    buf_ref,
    grad_buf,
    after_ref,
    flow_ref,
):
    step_at = pl.program_id(0)

    @pl.when(step_at == 0)
    def _():
        for ref in (dtaps_ref, dgain_ref, dskip_ref, dbias_ref, ddecay_ref, after_ref, flow_ref):
            ref[...] = jnp.zeros_like(ref)
        grad_buf[CHUNK:, :] = jnp.zeros((8, CONV), jnp.float32)

    inside = jnp.where(step_at == pl.num_programs(0) - 1, 0.0, 1.0)
    for group in range(2):
        at = group * 1024 + GROUP
        buf_ref[0:8, group * GROUP : (group + 1) * GROUP] = before_ref[:, at : at + GROUP] * inside
    buf_ref[0:8, 2 * GROUP :] = before_ref[:, SHARED : SHARED + 2 * N] * inside
    load_conv(buf_ref, proj_ref)
    mask = triangle()
    lower = mask.astype(jnp.bfloat16)
    row = lax.broadcasted_iota(jnp.int32, (CHUNK, CHUNK), 0)
    col = lax.broadcasted_iota(jnp.int32, (CHUNK, CHUNK), 1)
    upper = (row <= col).astype(jnp.bfloat16)
    pre_state = conv_pre(buf_ref, taps_ref, 2 * GROUP, 2 * N)
    sig_state = sigmoid(pre_state)
    state_act = low(pre_state * sig_state)
    b_rows, c_rows = state_act[:, :N], state_act[:, N:]
    gram = dot_nt(c_rows, b_rows)
    c_cols = c_rows.T
    dgram = jnp.zeros((CHUNK, CHUNK), jnp.float32)
    d_c = jnp.zeros((CHUNK, N), jnp.float32)
    d_b = jnp.zeros((CHUNK, N), jnp.float32)
    for group in range(2):
        raw, step, rate, cumul = group_steps(proj_ref, bias_ref, decay_ref, group, lower)
        cumul_t = cumul.T
        last = cumul[CHUNK - 1 : CHUNK, :]
        pres, sigs, chans, gates, gate_sigs, skips, gated = [], [], [], [], [], [], []
        for pair in range(PAIRS):
            at = group * GROUP + pair * 128
            pre = conv_pre(buf_ref, taps_ref, at, 128)
            sig = sigmoid(pre)
            chan = pre * sig
            gate = proj_ref[:, group * 1024 + pair * 128 : group * 1024 + pair * 128 + 128]
            gate_sig = sigmoid(gate)
            skipped = out_ref[:, at : at + 128] + chan * skip_ref[:, at : at + 128]
            pres.append(pre)
            sigs.append(sig)
            chans.append(chan)
            gates.append(gate)
            gate_sigs.append(gate_sig)
            skips.append(skipped)
            gated.append(skipped * (gate * gate_sig))
        square = sum(jnp.sum(part * part, axis=1, keepdims=True) for part in gated)
        scale = lax.rsqrt(square * (1.0 / GROUP) + EPS)
        grads = []
        cross = jnp.zeros((CHUNK, 1), jnp.float32)
        for pair in range(PAIRS):
            at = group * GROUP + pair * 128
            grad = back_ref[:, group * 512 + pair * 128 : group * 512 + pair * 128 + 128]
            dgain_ref[:, at : at + 128] += jnp.sum(grad * gated[pair] * scale, axis=0, keepdims=True)
            grad = grad * gain_ref[:, at : at + 128]
            cross = cross + jnp.sum(gated[pair] * grad, axis=1, keepdims=True)
            grads.append(grad)
        cross = cross * (1.0 / GROUP) * scale * scale * scale
        dstep = jnp.zeros((CHUNK, 128), jnp.float32)
        flow = jnp.zeros((CHUNK, 128), jnp.float32)
        flow_end = flow_ref[group : group + 1, :]
        flow_next = jnp.zeros((1, 128), jnp.float32)
        for pair in range(PAIRS):
            at = group * GROUP + pair * 128
            head_of_lane = lax.broadcasted_iota(jnp.int32, (128, 128), 0) // HEAD_SIZE + 2 * pair
            lane = lax.broadcasted_iota(jnp.int32, (128, 128), 1)
            pick = (head_of_lane == lane).astype(jnp.bfloat16)
            chan = chans[pair]
            grad = scale * grads[pair] - gated[pair] * cross
            gate, gate_sig = gates[pair], gate_sigs[pair]
            dgate = grad * skips[pair] * silu_slope(gate, gate_sig)
            to = group * 1024 + pair * 128
            dproj_ref[:, to : to + 128] = low(dgate)
            grad = grad * (gate * gate_sig)
            dskip_ref[:, at : at + 128] += jnp.sum(grad * chan, axis=0, keepdims=True)
            dchan = grad * skip_ref[:, at : at + 128]
            dout = low(grad)
            step_lanes = pair_lanes(step, pair)
            inputs = low(chan * step_lanes)
            halves = split_pair(inputs)
            decays = [head_decay(cumul, cumul_t, 2 * pair + side, mask) for side in range(2)]
            mixing = jnp.concatenate([low(gram * decay) for decay in decays], axis=1)
            dmix = dot_nt(dout, halves)
            dgram = dgram + dmix[:, :CHUNK] * decays[0] + dmix[:, CHUNK:] * decays[1]
            dinputs = dot_tn(mixing, dout)
            lane = lax.broadcasted_iota(jnp.int32, (CHUNK, 128), 1)
            dinputs = jnp.where(lane < HEAD_SIZE, dinputs[:CHUNK], dinputs[CHUNK:])
            inner = pair_lanes(cumul, pair)
            last_lanes = pair_lanes(last, pair)
            to_end = jnp.exp(last_lanes - inner)
            after = after_ref[:, at : at + 128]
            after_low = low(after)
            dinputs = dinputs + to_end * dot(b_rows, after_low)
            x_end = low(to_end * wide(inputs))
            g_start = low(jnp.exp(inner) * wide(dout))
            state = states_ref[0, :, at : at + 128]
            d_c = d_c + dot_nt(g_start, low(state))
            d_b = d_b + dot_nt(x_end, after_low)
            after = jnp.exp(last_lanes) * after + dot(c_cols, g_start)
            after_ref[:, at : at + 128] = after
            through = jnp.sum(after * state, axis=0, keepdims=True)
            flow_next = flow_next + dot_by(jnp.broadcast_to(through, (8, 128)), pick)[0:1]
            flow = flow + dot_by(
                wide(dout) * out_ref[:, at : at + 128] - wide(inputs) * dinputs, pick
            )
            dstep = dstep + dot_by(dinputs * chan, pick)
            dchan = dchan + dinputs * step_lanes
            grad_buf[0:CHUNK, at : at + 128] = dchan * silu_slope(pres[pair], sigs[pair])
        dcumul = dot_fine(upper, flow) + flow_end
        flow_ref[group : group + 1, :] = flow_next
        dstep = dstep + rate * dcumul
        ddecay_ref[group : group + 1, :] += jnp.sum(rate * step * dcumul, axis=0, keepdims=True)
        draw = dstep * sigmoid(raw)
        dbias_ref[group : group + 1, :] += jnp.sum(draw, axis=0, keepdims=True)
        to = group * 1024 + 896
        lane = lax.broadcasted_iota(jnp.int32, (CHUNK, 128), 1)
        dproj_ref[:, to : to + 128] = low(jnp.where(lane < GH, draw, 0.0))
        to = group * 1024 + 2 * GROUP
        dproj_ref[:, to : to + 128] = dq_ref[:, group * 128 : (group + 1) * 128]
    dgram_low = low(dgram)
    d_c = d_c + dot(dgram_low, b_rows)
    d_b = d_b + dot_tn(dgram_low, c_rows)
    slope = silu_slope(pre_state, sig_state)
    grad_buf[0:CHUNK, 2 * GROUP : 2 * GROUP + N] = d_b * slope[:, :N]
    grad_buf[0:CHUNK, 2 * GROUP + N :] = d_c * slope[:, N:]
    for at in range(0, CONV, 128):
        grad = jnp.zeros((CHUNK, 128), jnp.float32)
        here = grad_buf[0:CHUNK, at : at + 128]
        for tap in range(KCONV):
            shift = KCONV - 1 - tap
            grad = grad + (
                grad_buf[shift : shift + CHUNK, at : at + 128] * taps_ref[tap : tap + 1, at : at + 128]
            )
            dtaps_ref[tap : tap + 1, at : at + 128] += jnp.sum(
                here * buf_ref[5 + tap : 5 + tap + CHUNK, at : at + 128], axis=0, keepdims=True
            )
        if at < 2 * GROUP:
            to = (at // GROUP) * 1024 + GROUP + at % GROUP
        else:
            to = SHARED + at - 2 * GROUP
        dproj_ref[:, to : to + 128] = low(grad)
    dproj_ref[:, SHARED + 2 * N :] = dkv_ref[...]
    grad_buf[CHUNK:, :] = grad_buf[0:8, :]


def mamba_backward(proj, out, states, back, dq, dkv, taps, bias, decay, skip, gain):
    rows, columns = proj.shape
    chunks = rows // CHUNK

    def whole(value):
        return pl.BlockSpec(value.shape, lambda k: (0, 0))

    def rows_of(width):
        return pl.BlockSpec((CHUNK, width), lambda k: (chunks - 1 - k, 0))

    params = (taps, bias, decay, skip, gain)
    return pl.pallas_call(
        mamba_backward_kernel,
        grid=(chunks,),
        in_specs=[
            rows_of(columns),
            pl.BlockSpec(
                (8, columns),
                lambda k: (jnp.maximum((chunks - 1 - k) * (CHUNK // 8) - 1, 0), 0),
            ),
            rows_of(2 * GROUP),
            pl.BlockSpec((1, N, 2 * GROUP), lambda k: (chunks - 1 - k, 0, 0)),
            rows_of(1024),
            rows_of(256),
            rows_of(128),
        ]
        + [whole(value) for value in params],
        out_specs=[rows_of(columns)]
        + [whole(value) for value in (taps, gain, skip, bias, decay)],
        out_shape=[jax.ShapeDtypeStruct((rows, columns), jnp.bfloat16)]
        + [
            jax.ShapeDtypeStruct(value.shape, jnp.float32)
            for value in (taps, gain, skip, bias, decay)
        ],
        scratch_shapes=[
            pltpu.VMEM((CHUNK + 8, CONV), jnp.float32),
            pltpu.VMEM((CHUNK + 8, CONV), jnp.float32),
            pltpu.VMEM((N, 2 * GROUP), jnp.float32),
            pltpu.VMEM((8, 128), jnp.float32),
        ],
        compiler_params=pltpu.CompilerParams(vmem_limit_bytes=BIG),
        name="mamba_backward",
    )(proj, proj, out, states, back, dq, dkv, *params)


def rms_norm(values, gain_vec):
    return values * lax.rsqrt(jnp.mean(values * values, axis=-1, keepdims=True) + EPS) * gain_vec


def turn_tables(seq_count, head_count):
    half_dim = HEAD_SIZE // 2
    freqs = THETA ** (-jnp.arange(half_dim, dtype=jnp.float32) * 2.0 / HEAD_SIZE)
    angles = jnp.arange(seq_count, dtype=jnp.float32)[:, None] * freqs[None, :]
    cosine, sine = jnp.cos(angles), jnp.sin(angles)
    return (
        jnp.tile(jnp.concatenate([cosine, cosine], axis=1), (1, head_count)),
        jnp.tile(jnp.concatenate([-sine, sine], axis=1), (1, head_count)),
    )


def swiglu(gate_up):
    half_cols = gate_up.shape[1] // 2
    gate = gate_up[:, :half_cols]
    return gate * sigmoid(gate) * gate_up[:, half_cols:]


def swapped(values):
    return lax.ppermute(values, "core", SWAP)


def body(
    layer_in,
    seq_lengths,
    out_grad,
    norm_gain,
    mixer_weight,
    step_weight,
    state_weight,
    query_weight,
    key_value_weight,
    conv_channels,
    conv_states,
    step_bias,
    decay_log,
    skip_scale,
    group_gain,
    mamba_proj,
    attn_proj,
    ffn_gain,
    ffn_weight,
    ffn_down,
):
    core = lax.axis_index("core")
    place = lax.axis_index("tensor")
    first = core == 0
    seq_dev, rows_dev, model_dim = layer_in.shape
    groups = lax.axis_size("tensor")
    seq_total = rows_dev * groups
    half_rows = rows_dev // 2
    share = mixer_weight.shape[0]
    chans_dev = mixer_weight.shape[2]
    heads_dev = step_weight.shape[1]
    query_dev = query_weight.shape[1]
    hidden_dev = ffn_weight.shape[2]
    held = groups // 2
    step_pad = 128

    def mine(values):
        return lax.dynamic_slice_in_dim(values, core * held, held, 0)

    def other(values):
        return lax.dynamic_slice_in_dim(values, (1 - core) * held, held, 0)

    def in_order(own, others, axis):
        return jnp.where(
            first,
            jnp.concatenate([own, others], axis=axis),
            jnp.concatenate([others, own], axis=axis),
        )

    def flat(values):
        return values.transpose(1, 0, 2).reshape(values.shape[1], -1)

    def positions_in(values):
        shaped = values.reshape(seq_dev, 2, half_rows, model_dim)
        keep = lax.dynamic_index_in_dim(shaped, core, 1, False)
        send = lax.dynamic_index_in_dim(shaped, 1 - core, 1, False)
        four = in_order(keep, swapped(send), 0)
        own = lax.all_to_all(four, "tensor", 0, 0, tiled=True)
        both = in_order(own[:, None], swapped(own)[:, None], 1)
        return both.reshape(seq_total, model_dim)

    def positions_out(own):
        four = lax.all_to_all(own, "tensor", 0, 0, tiled=True)
        keep = lax.dynamic_slice_in_dim(four, core * seq_dev, seq_dev, 0)
        send = lax.dynamic_slice_in_dim(four, (1 - core) * seq_dev, seq_dev, 0)
        both = in_order(keep[:, None], swapped(send)[:, None], 1)
        return both.reshape(seq_dev, rows_dev, model_dim)

    def own_half(values):
        shaped = values.reshape(groups, 2, half_rows, -1)
        return lax.dynamic_index_in_dim(shaped, core, 1, False)

    def other_half(values):
        shaped = values.reshape(groups, 2, half_rows, -1)
        return lax.dynamic_index_in_dim(shaped, 1 - core, 1, False)

    x_low = positions_in(layer_in)
    pack_one = jnp.concatenate(
        [
            mixer_weight.reshape(share, 2 * chans_dev),
            query_weight,
            jnp.pad(step_weight, ((0, 0), (0, step_pad - heads_dev))),
        ],
        axis=1,
    )
    all_one = lax.all_gather(pack_one, "tensor", axis=0)
    kv_heads = key_value_weight.reshape(share, 2, 2, HEAD_SIZE)

    def lay_one(pack, at):
        return jnp.concatenate(
            [
                flat(pack),
                state_weight.reshape(share, 2 * N),
                lax.dynamic_index_in_dim(kv_heads, at, 2, False).reshape(share, 2 * HEAD_SIZE),
            ],
            axis=1,
        )

    own_one = lay_one(mine(all_one), core)
    their_one = lay_one(other(all_one), 1 - core)
    weight_one = lax.all_gather(
        in_order(own_one, swapped(their_one), 0), "plane", axis=0, tiled=True
    )

    pack_two = jnp.concatenate(
        [mamba_proj.T, attn_proj.T, ffn_weight.reshape(share, 2 * hidden_dev), ffn_down.T], axis=1
    )
    all_two = lax.all_gather(pack_two, "tensor", axis=0)
    out_dev = chans_dev + query_dev

    def lay_two(pack):
        cut = out_dev + hidden_dev
        return jnp.concatenate(
            [
                flat(pack[:, :, :out_dev]),
                flat(pack[:, :, out_dev:cut]),
                flat(pack[:, :, cut : cut + hidden_dev]),
                flat(pack[:, :, cut + hidden_dev :]),
            ],
            axis=1,
        )

    rows_two = in_order(lay_two(mine(all_two)), swapped(lay_two(other(all_two))), 0)
    edges = (0, held * out_dev, held * (out_dev + 2 * hidden_dev), held * (out_dev + 3 * hidden_dev))
    weight_two, gate_up_weight, down_weight = (
        lax.all_gather(rows_two[:, begin:end], "plane", axis=0, tiled=True)
        for begin, end in zip(edges[:-1], edges[1:])
    )

    small_in = jnp.concatenate(
        [conv_channels.reshape(-1), step_bias, decay_log, skip_scale, group_gain]
    )
    small_mine = mine(lax.all_gather(small_in, "tensor", axis=0))
    cuts = []
    at = 0
    for size in (KCONV * chans_dev, heads_dev, heads_dev, heads_dev, chans_dev):
        cuts.append(small_mine[:, at : at + size])
        at += size
    taps = cuts[0].reshape(held, KCONV, chans_dev).transpose(1, 0, 2).reshape(KCONV, -1)
    taps = jnp.concatenate([taps, conv_states.reshape(KCONV, 2 * N)], axis=1)
    bias = jnp.pad(cuts[1], ((0, 0), (0, step_pad - heads_dev)))
    decay = jnp.pad(cuts[2], ((0, 0), (0, step_pad - heads_dev)))
    skip = jnp.repeat(cuts[3].reshape(1, -1), HEAD_SIZE, axis=1)
    gain = cuts[4].reshape(1, -1)

    lengths = lax.all_gather(seq_lengths, "core", axis=0).reshape(-1)
    seq_len = lengths[place]
    len_one = seq_len.reshape(1)
    valid_rows = (jnp.arange(seq_total, dtype=jnp.int32) < seq_len).astype(jnp.float32)[:, None]

    x_rows = wide(x_low)
    normed = low(rms_norm(x_rows, norm_gain))
    proj = dot(normed, weight_one)
    group_cols = 2 * chans_dev + query_dev + step_pad
    cosine, sine = turn_tables(seq_total, 2)
    attn, log_sums = attention_forward(len_one, proj, cosine, sine, group_cols)
    both_low, state_out, states = mamba_forward(proj, attn, taps, bias, decay, skip, gain)

    mixed_part = low(dot_nt(both_low, weight_two))
    mixed = wide(mixed_part) + wide(swapped(mixed_part))
    hidden = x_rows + mixed
    normed_two = low(rms_norm(hidden, ffn_gain))
    gate_up = dot(normed_two, gate_up_weight)
    act, act_pull = jax.vjp(swiglu, gate_up)
    act_low = low(act)
    ffn_part = low(dot_nt(act_low, down_weight))
    ffn_own = wide(own_half(ffn_part)) + wide(swapped(other_half(ffn_part)))
    out_own = own_half(valid_rows) * (own_half(hidden) + ffn_own)
    layer_out = positions_out(low(out_own))

    grad_rows = valid_rows * wide(positions_in(out_grad))
    grad_low = low(grad_rows)
    grad_down = low(dot_tn(grad_low, act_low))
    (grad_gate_up,) = act_pull(dot(grad_low, down_weight))
    gate_up_low = low(grad_gate_up)
    grad_gate_up_weight = low(dot_tn(normed_two, gate_up_low))
    grad_two_part = low(dot_nt(gate_up_low, gate_up_weight))
    grad_two = wide(grad_two_part) + wide(swapped(grad_two_part))
    r_two = lax.rsqrt(jnp.mean(hidden * hidden, axis=-1, keepdims=True) + EPS)
    scaled = grad_two * ffn_gain
    grad_hidden = (
        grad_rows
        + r_two * scaled
        - hidden * (r_two**3 * jnp.mean(hidden * scaled, axis=-1, keepdims=True))
    )
    grad_ffn_gain = jnp.sum(own_half(hidden * r_two * grad_two), axis=(0, 1))
    grad_mixed = low(grad_hidden)

    def scatter(values):
        part = lax.psum_scatter(values, "plane", scatter_dimension=0, tiled=True)
        part = part.reshape(2, share, -1)
        return (
            lax.dynamic_index_in_dim(part, core, 0, False),
            lax.dynamic_index_in_dim(part, 1 - core, 0, False),
        )

    def by_group(values, widths):
        pieces = []
        at = 0
        for width in widths:
            piece = values[:, at : at + held * width]
            pieces.append(piece.reshape(share, held, width).transpose(1, 0, 2))
            at += held * width
        return jnp.concatenate(pieces, axis=2)

    def to_groups(own, theirs):
        whole = in_order(own, theirs, 0)
        return lax.psum_scatter(whole, "tensor", scatter_dimension=0, tiled=True)[0]

    def sum_rest(parts, widths):
        both = [scatter(part) for part in parts]
        own = by_group(jnp.concatenate([pair[0] for pair in both], axis=1), widths)
        theirs = by_group(jnp.concatenate([pair[1] for pair in both], axis=1), widths)
        return to_groups(own, swapped(theirs))

    sum_three = sum_rest((grad_gate_up_weight, grad_down), (hidden_dev,) * 3)
    grad_both = low(dot_tn(grad_mixed, both_low))
    sum_two = sum_rest((grad_both,), (out_dev,))

    back = dot(grad_mixed, weight_two)
    attn_back = jnp.concatenate(
        [low(back[:, chans_dev:out_dev]), low(back[:, out_dev + chans_dev :])], axis=1
    )
    grad_q, grad_kv = attention_backward(
        len_one, proj, cosine, sine, log_sums, attn_back, group_cols, 0
    )
    proj_grad, grad_taps, grad_gain, grad_skip_cols, grad_bias, grad_decay = mamba_backward(
        proj, state_out, states, back, grad_q, grad_kv, taps, bias, decay, skip, gain
    )
    grad_one = low(dot_tn(normed, proj_grad))
    own_grad, their_grad = scatter(grad_one)
    their_grad = swapped(their_grad)
    edge = held * group_cols
    shared_own = wide(own_grad[:, edge : edge + 2 * N]) + wide(their_grad[:, edge : edge + 2 * N])
    kv_both = in_order(
        own_grad[:, None, edge + 2 * N :], their_grad[:, None, edge + 2 * N :], 1
    )
    kv_both = kv_both.reshape(share, 2, 2, HEAD_SIZE).transpose(0, 2, 1, 3)
    shared_low = jnp.concatenate([low(shared_own), kv_both.reshape(share, -1)], axis=1)
    shared_sum = jnp.sum(wide(lax.all_gather(shared_low, "tensor", axis=0)), axis=0)
    sum_one = to_groups(
        by_group(own_grad[:, :edge], (group_cols,)), by_group(their_grad[:, :edge], (group_cols,))
    )

    grad_norm_part = low(dot_nt(proj_grad, weight_one))
    grad_norm_own = wide(own_half(grad_norm_part)) + wide(swapped(other_half(grad_norm_part)))
    x_own = wide(own_half(x_low))
    r_one = lax.rsqrt(jnp.mean(x_own * x_own, axis=-1, keepdims=True) + EPS)
    scaled = grad_norm_own * norm_gain
    grad_x = (
        own_half(grad_hidden)
        + r_one * scaled
        - x_own * (r_one**3 * jnp.mean(x_own * scaled, axis=-1, keepdims=True))
    )
    grad_norm_gain = jnp.sum(x_own * r_one * grad_norm_own, axis=(0, 1))
    input_grad = positions_out(low(grad_x))

    grad_skip = jnp.sum(grad_skip_cols.reshape(held, heads_dev, HEAD_SIZE), axis=-1)
    chan_taps = grad_taps[:, : held * chans_dev].reshape(KCONV, held, chans_dev)
    group_small = jnp.concatenate(
        [
            chan_taps.transpose(1, 0, 2).reshape(held, -1),
            grad_bias[:, :heads_dev],
            grad_decay[:, :heads_dev],
            grad_skip,
            grad_gain.reshape(held, -1),
        ],
        axis=1,
    )
    small_groups = in_order(group_small, jnp.zeros_like(group_small), 0)
    small_out = jnp.concatenate(
        [
            grad_norm_gain,
            grad_ffn_gain,
            grad_taps[:, held * chans_dev :].reshape(-1),
            small_groups.reshape(-1),
        ]
    )
    small_sum = lax.psum(small_out, ("plane", "core", "tensor"))
    group_sum = lax.dynamic_index_in_dim(
        small_sum[2 * model_dim + KCONV * 2 * N :].reshape(groups, -1), place, 0, False
    )
    pieces = []
    at = 0
    for size in (KCONV * chans_dev, heads_dev, heads_dev, heads_dev, chans_dev):
        pieces.append(group_sum[at : at + size])
        at += size

    one, two, three = wide(sum_one), wide(sum_two), wide(sum_three)
    return (
        layer_out,
        input_grad,
        small_sum[:model_dim],
        one[:, : 2 * chans_dev].reshape(share, 2, chans_dev),
        one[:, 2 * chans_dev + query_dev :][:, :heads_dev],
        shared_sum[:, : 2 * N].reshape(share, 2, N),
        one[:, 2 * chans_dev : 2 * chans_dev + query_dev],
        shared_sum[:, 2 * N :].reshape(share, 2, 2 * HEAD_SIZE),
        pieces[0].reshape(KCONV, chans_dev),
        small_sum[2 * model_dim : 2 * model_dim + KCONV * 2 * N].reshape(KCONV, 2, N),
        pieces[1],
        pieces[2],
        pieces[3],
        pieces[4],
        two[:, :chans_dev].T,
        two[:, chans_dev:].T,
        small_sum[model_dim : 2 * model_dim],
        three[:, : 2 * hidden_dev].reshape(share, 2, hidden_dev),
        three[:, 2 * hidden_dev :].T,
    )


def solution(mesh):
    rows, columns = mesh.devices.shape
    fine = Mesh(mesh.devices.reshape(rows // 2, 2, columns), ("plane", "core", "tensor"))
    dp = ("plane", "core")
    return jax.shard_map(
        body,
        mesh=fine,
        in_specs=(
            P(dp, "tensor", None),
            P(dp),
            P(dp, "tensor", None),
            P(),
            P(dp, None, "tensor"),
            P(dp, "tensor"),
            P(dp, None, None),
            P(dp, "tensor"),
            P(dp, None, None),
            P(None, "tensor"),
            P(),
            P("tensor"),
            P("tensor"),
            P("tensor"),
            P("tensor"),
            P("tensor", dp),
            P("tensor", dp),
            P(),
            P(dp, None, "tensor"),
            P("tensor", dp),
        ),
        out_specs=(
            P(dp, "tensor", None),
            P(dp, "tensor", None),
            P(),
            P(dp, None, "tensor"),
            P(dp, "tensor"),
            P(dp, None, None),
            P(dp, "tensor"),
            P(dp, None, None),
            P(None, "tensor"),
            P(),
            P("tensor"),
            P("tensor"),
            P("tensor"),
            P("tensor"),
            P("tensor", dp),
            P("tensor", dp),
            P(),
            P(dp, None, "tensor"),
            P("tensor", dp),
        ),
        check_vma=False,
    )
```

time: 2100 us -> 602 us (0.29)
  waiting for transfers between devices: 948 us -> 158 us
  matrix products: 393 us -> 100 us
  blocking collectives: 352 us -> 82.7 us
  local copies, waits for them, and re-layouts: 233 us -> 75.2 us
  other arithmetic: 144 us -> 59.4 us
  Pallas kernels: 0 us -> 80 us
    reduce_scatter x13 -> x7, waiting for transfers between devices: 556 us -> 4.24 us  [the longest x3 4.24 us: to_groups(): return lax.psum_scatter(whole, 'tensor', scatter_dimension=0, tiled=True)[0]]
    dot_general x152 -> x12, matrix products: 393 us -> 100 us  [the longest x4 41.7 us: dot(): return jnp.dot(left, right, preferred_element_type=jnp.float32)]
    all_gather x11 -> x6, waiting for transfers between devices: 355 us -> 98.2 us  [the longest x1 42.3 us: body(): all_two = lax.all_gather(pack_two, 'tensor', axis=0)]
    psum x2 -> x1, blocking collectives: 293 us -> 39.1 us  [body(): small_sum = lax.psum(small_out, ('plane', 'core', 'tensor'))]
    pallas_call x0 -> x4, Pallas kernels: none -> 80 us  [the longest x1 36.3 us: mamba_backward(): pl.pallas_call(mamba_backward_kernel, grid=(chunks,), in_specs=[rows_of(c...]
    add x4 -> x0, local copies, waits for them, and re-layouts: 48.3 us -> none  [add_tuples(): left + right]
    dynamic_slice x73 -> x11, local copies, waits for them, and re-layouts: 57.9 us -> 13.2 us  [the longest x6 7.92 us: scatter(): lax.dynamic_index_in_dim(part, core, 0, False)]
    all_to_all x0 -> x4, waiting for transfers between devices: none -> 43.4 us  [the longest x2 21.8 us: positions_in(): own = lax.all_to_all(four, 'tensor', 0, 0, tiled=True)]
  transfers between devices with their start and end apart: 26 -> 32, of which waited for: 23 -> 12; matrix products, arithmetic and copies ran while one was open for 12% -> 34% of each run, Pallas kernels for 0% -> 13%
where the time goes in v1:
time: 602 us; the launch traced here: 594 us
  waiting for transfers between devices  158 us (26%)
  matrix products  100 us (17%)
  blocking collectives  82.7 us (14%)
  Pallas kernels  80 us (13%)
  local copies, waits for them, and re-layouts  75.2 us (12%)
  other arithmetic  59.4 us (10%)
  starting transfers between devices  22.3 us (4%)
  between operations  16.4 us (3%)
    all_gather x1, waiting for transfers between devices, body(): all_two = lax.all_gather(pack_two, 'tensor', axis=0)  42.3 us
    dot_general x4, matrix products, dot(): return jnp.dot(left, right, preferred_element_type=jnp.float32)  41.7 us
    psum x1, blocking collectives, body(): small_sum = lax.psum(small_out, ('plane', 'core', 'tensor'))  39.1 us
    pallas_call x1, Pallas kernels, mamba_backward(): pl.pallas_call(mamba_backward_kernel, grid=(chunks,), in_specs=[rows_of(c...  36.3 us
    all_gather x3, waiting for transfers between devices, body(): lax.all_gather(rows_two[:, begin:end], 'plane', axis=0, tiled=True)  30.3 us
    dot_general x4, matrix products, dot_tn(): lax.dot_general(left, right, (((0,), (0,)), ((), ())), preferred_element_...  29.8 us
    dot_general x4, matrix products, dot_nt(): lax.dot_general(left, right, (((1,), (1,)), ((), ())), preferred_element_...  28.9 us
    all_gather x1, waiting for transfers between devices, body(): all_one = lax.all_gather(pack_one, 'tensor', axis=0)  25.6 us
  transfers between devices with their start and end apart: 32, of which 12 were waited for; matrix products, arithmetic and copies ran while one was open for 34% of the time, Pallas kernels for 13%

profile of v1, /device:TPU:0, one launch (start us, length us, event | category | flops | bytes accessed | tf_op | source)
XLA Modules:
  0.0 594.3 jit_solution(15957394475318264146)
XLA Ops:
  15.7 25.6 %all-gather.20.cloned.1.call-done = bf16[512,1024]{1,0:T(8,128)(2,1)} async-done(((bf16[128,1024]{1,0:T(8,128)(2,1)}), bf16[512,1024]{1,0:T(8,128)(2,1)}) %all-gather.20.cloned.1.call-update) | async-done | bytes 1048592 | tf_op jit(solution)/shard_map/all_gather | solution.py:714
  46.6 42.3 %all-gather.22.cloned.1.call-done = bf16[512,2048]{1,0:T(8,128)(2,1)} async-done(((bf16[128,2048]{1,0:T(8,128)(2,1)}), bf16[512,2048]{1,0:T(8,128)(2,1)}) %all-gather.22.cloned.1.call-update) | async-done | bytes 2097168 | tf_op jit(solution)/shard_map/all_gather | solution.py:736
  94.2 4.8 maximum_select_fusion.1
  113.9 21.8 %all-to-all-done = bf16[4,128,1024]{2,1,0:T(8,128)(2,1)S(1)} async-done(((bf16[4,128,1024]{2,1,0:T(8,128)(2,1)}), bf16[4,128,1024]{2,1,0:T(8,128)(2,1)S(1)}, u32[]{:S(2)}, u32[]{:S(2)}) %all-to-all-start) | async-done | bytes 1048608 | tf_op jit(solution)/shard_map/all_to_all | solution.py:686
  140.2 17.1 %all-reduce.9 = f32[4,1938]{1,0:T(4,128)S(1)} all-reduce(f32[4,1938]{1,0:T(4,128)S(1)} %reshape.454), channel_id=4, replica_groups=mesh['plane'=4,'core'=2,'tensor'=4] {'tensor'}, use_global_device_ids=true, to_apply=%add.8 | all-reduce | flops 7752 | bytes 62016
  175.8 10.9 %fusion.46.q_ref.kv_ref.proj_ref.before_ref = f32[1024,2432]{1,0:T(8,128)} fusion(bf16[1024,1024]{1,0:T(8,128)(2,1)} %fusion.1, bf16[1024,2432]{0,1:T(8,128)(2,1)} %all-gather.12.cloned.1.call-done), kind=kOutput, calls=%fused_computation.157 | convolution fusion | flops 5100273664 | bytes 17039360 | tf_op jit(solution)/shard_map/dot_general | solution.py:28
  186.7 11.2 %attention_forward.1 = (bf16[1024,256]{1,0:T(8,128)(2,1)}, f32[1024,256]{1,0:T(8,128)}) custom-call(s32[1]{0:T(128)} %dynamic-slice.len_ref, f32[1024,2432]{1,0:T(8,128)} %fusion.46.q_ref.kv_ref.proj_ref.before_ref, f32[1024,2432]{1,0:T(8,128)} %fusion.46.q_ref.kv_ref.proj_ref.before_ref, f32[1024,128]{1,0:T(8,128)} %copy.197.cos_ref, f32[1024,128]{1,0:T(8,128)} %copy.198.sin_ref), custom_call_target="tpu_custom_call" | custom-call | tf_op jit(solution)/shard_map/attention_forward/pallas_call | solution.py:181
  197.9 14.4 %mamba_forward.1 = (bf16[1024,1024]{1,0:T(8,128)(2,1)}, f32[1024,768]{1,0:T(8,128)}, f32[8,128,768]{2,1,0:T(8,128)}) custom-call(f32[1024,2432]{1,0:T(8,128)} %fusion.46.q_ref.kv_ref.proj_ref.before_ref, bf16[1024,256]{1,0:T(8,128)(2,1)} %get-tuple-element.32.attn_ref, f32[4,1024]{1,0:T(4,128)} %pad_maximum_fusion.9.taps_ref, f32[2,128]{1,0:T(2,128)} %pad.20.bias_ref, ...), custom_call_target="tpu_custom_call" | custom-call | tf_op jit(solution)/shard_map/mamba_forward/pallas_call | solution.py:356
  212.3 5.9 convolution_convert_fusion.7
  230.7 5.0 multiply_reduce_fusion.1
  240.4 11.3 %fusion.37 = f32[1024,2048]{1,0:T(8,128)} fusion(bf16[1024,2048]{0,1:T(8,128)(2,1)} %all-gather.16.cloned.1.call-done, f32[1024,1024]{1,0:T(8,128)} %get-tuple-element.143, f32[1024]{0:T(1024)S(1)} %copy-done.14, f32[1024]{0:T(1024)S(1)} %add_rsqrt_fusion), kind=kOutput, calls=%fused_computation.148 | convolution fusion | flops 4298113024 | bytes 16785408 | tf_op jit(solution)/shard_map/dot_general | solution.py:28
  251.7 25.6 %all-gather.18.cloned.1.call-done = bf16[1024,1024]{0,1:T(8,128)(2,1)} async-done(((bf16[256,1024]{0,1:T(8,128)(2,1)}), bf16[1024,1024]{0,1:T(8,128)(2,1)}) %all-gather.18.cloned.1.call-update) | async-done | bytes 2097168 | tf_op jit(solution)/shard_map/all_gather | solution.py:754
  277.2 12.3 %fusion.23 = (f32[1024,1024]{1,0:T(8,128)}, f32[1024,1024]{1,0:T(8,128)}, bf16[1024,1024]{1,0:T(8,128)(2,1)S(1)}) fusion(f32[1024,2048]{1,0:T(8,128)} %fusion.37, bf16[1024,1024]{1,0:T(8,128)(2,1)} %fusion.7, bf16[1024,1024]{0,1:T(8,128)(2,1)} %all-gather.18.cloned.1.call-done), kind=kOutput, calls=%fused_computation.81 | convolution fusion | flops 2165309440 | bytes 23068672 | tf_op jit(solution)/shard_map/dot_general | solution.py:28
  294.9 9.3 %convolution_convert_fusion.5 = bf16[1024,1024]{1,0:T(8,128)(2,1)S(1)} fusion(bf16[1024,2048]{0,1:T(8,128)(2,1)} %all-gather.16.cloned.1.call-done, f32[1024,1024]{1,0:T(8,128)} %get-tuple-element.147, f32[1024,1024]{1,0:T(8,128)} %get-tuple-element.146), kind=kOutput, calls=%fused_computation.48 | convolution fusion | flops 4300210176 | bytes 14680064 | tf_op jit(solution)/shard_map/dot_general | solution.py:32
  318.8 11.7 %convolution_convert_fusion.1 = bf16[1024,2048]{1,0:T(8,128)(2,1)} fusion(f32[1024,1024]{1,0:T(8,128)} %get-tuple-element.147, f32[1024,1024]{1,0:T(8,128)} %get-tuple-element.146, f32[1024,1024]{1,0:T(8,128)} %get-tuple-element.143, f32[1024]{0:T(1024)S(1)} %copy-done.14, f32[1024]{0:T(1024)S(1)} %add_rsqrt_fusion), kind=kOutput, calls=%fused_computation.22 | convolution fusion | flops 4304404480 | bytes 16785408 | tf_op jit(solution)/shard_map/dot_general | solution.py:38
  330.8 7.2 %fusion.45 = (bf16[1024,1024]{1,0:T(8,128)(2,1)S(1)}, f32[1024,1024]{1,0:T(8,128)}) fusion(bf16[1024,1024]{0,1:T(8,128)(2,1)} %all-gather.14.cloned.1.call-done, f32[1024,1024]{1,0:T(8,128)} %copy-done.6), kind=kOutput, calls=%fused_computation.156 | convolution fusion | flops 2149580800 | bytes 12582912 | tf_op jit(solution)/shard_map/dot_general | solution.py:28
  338.9 18.1 %attention_backward.1 = (bf16[1024,256]{1,0:T(8,128)(2,1)}, bf16[1024,128]{1,0:T(8,128)(2,1)}) custom-call(s32[1]{0:T(128)} %dynamic-slice.len_ref, f32[1024,2432]{1,0:T(8,128)} %fusion.46.q_ref.kv_ref.proj_ref.before_ref, f32[1024,2432]{1,0:T(8,128)} %fusion.46.q_ref.kv_ref.proj_ref.before_ref, f32[1024,128]{1,0:T(8,128)} %copy.197.cos_ref, ...), custom_call_target="tpu_custom_call" | custom-call | tf_op jit(solution)/shard_map/attention_backward/pallas_call | solution.py:198
  357.1 36.3 %mamba_backward.1 = (bf16[1024,2432]{1,0:T(8,128)(2,1)}, f32[4,1024]{1,0:T(4,128)}, f32[1,768]{1,0:T(1,128)}, f32[1,768]{1,0:T(1,128)}, f32[2,128]{1,0:T(2,128)}, /*index=5*/f32[2,128]{1,0:T(2,128)}) custom-call(f32[1024,2432]{1,0:T(8,128)} %fusion.46.q_ref.kv_ref.proj_ref.before_ref, f32[1024,2432]{1,0:T(8,128)} %fusion.46.q_ref.kv_ref.proj_ref.before_ref, ...), custom_call_target="tpu_custom_call" | custom-call | tf_op jit(solution)/shard_map/mamba_backward/pallas_call | solution.py:569
  393.3 10.6 %convolution_convert_fusion = bf16[1024,2432]{1,0:T(8,128)(2,1)} fusion(bf16[1024,1024]{1,0:T(8,128)(2,1)} %fusion.1, bf16[1024,2432]{1,0:T(8,128)(2,1)} %get-tuple-element.39), kind=kOutput, calls=%fused_computation.1 | convolution fusion | flops 5102764032 | bytes 12058624 | tf_op jit(solution)/shard_map/dot_general | solution.py:38
  417.6 9.0 %convolution_convert_fusion.4 = bf16[1024,1024]{1,0:T(8,128)(2,1)S(1)} fusion(bf16[1024,2432]{1,0:T(8,128)(2,1)} %get-tuple-element.39, bf16[1024,2432]{0,1:T(8,128)(2,1)} %all-gather.12.cloned.1.call-done), kind=kOutput, calls=%fused_computation.47 | convolution fusion | flops 5101322240 | bytes 12058624 | tf_op jit(solution)/shard_map/dot_general | solution.py:32
  463.9 5.0 all-to-all-start.3
  473.8 21.5 %all-to-all-done.3 = bf16[4,128,1024]{2,1,0:T(8,128)(2,1)S(1)} async-done(((bf16[4,128,1024]{2,1,0:T(8,128)(2,1)}), bf16[4,128,1024]{2,1,0:T(8,128)(2,1)S(1)}, u32[]{:S(2)}, u32[]{:S(2)}) %all-to-all-start.3) | async-done | bytes 1048608 | tf_op jit(solution)/shard_map/all_to_all | solution.py:691
  499.2 39.1 %psum.7 = f32[10824]{0:T(1024)S(1)} all-reduce(f32[10824]{0:T(1024)S(1)} %pad_maximum_fusion.8), channel_id=1, replica_groups=mesh['plane'=4,'core'=2,'tensor'=4] {'plane','core','tensor'}, use_global_device_ids=true, to_apply=%region_8.9 | all-reduce | flops 10824 | bytes 86592 | tf_op jit(solution)/shard_map/psum | solution.py:907
  552.9 24.7 %all-gather.4 = bf16[512,512]{0,1:T(8,128)(2,1)S(1)} all-gather(bf16[128,512]{0,1:T(8,128)(2,1)S(1)} %pad_maximum_fusion.7), channel_id=6, replica_groups=mesh['plane'=4,'core'=2,'tensor'=4] {'tensor'}, dimensions={0}, use_global_device_ids=true | all-gather | bytes 655360 | tf_op jit(solution)/shard_map/all_gather | solution.py:868
  (295 shorter events, 177.2 us)
Async XLA Ops:
  7.2 34.1 %all-gather.20.cloned.1.call-start = ((), (), s32[]{:S(2)}) async-start(), calls=%async_computation.22 | async-start | bytes 1310720 | tf_op jit(solution)/shard_map/all_gather | solution.py:714
  10.5 78.4 %all-gather.22.cloned.1.call-start = ((), (), s32[]{:S(2)}) async-start(), calls=%async_computation.23 | async-start | bytes 2621440 | tf_op jit(solution)/shard_map/all_gather | solution.py:736
  15.4 160.5 %all-gather.12.cloned.1.call-start = ((), (), s32[]{:S(2)}) async-start(), calls=%async_computation.11 | async-start | bytes 6225920 | tf_op jit(solution)/shard_map/all_gather | solution.py:729
  46.5 165.8 %all-gather.14.cloned.1.call-start = ((), (), s32[]{:S(2)}) async-start(), calls=%async_computation.12 | async-start | bytes 2621440 | tf_op jit(solution)/shard_map/all_gather | solution.py:754
  100.1 140.3 %all-gather.16.cloned.1.call-start = ((), (), s32[]{:S(2)}) async-start(), calls=%async_computation.13 | async-start | bytes 5242880 | tf_op jit(solution)/shard_map/all_gather | solution.py:754
  105.7 30.0 %all-to-all-start = ((bf16[4,128,1024]{2,1,0:T(8,128)(2,1)}), bf16[4,128,1024]{2,1,0:T(8,128)(2,1)S(1)}, u32[]{:S(2)}, u32[]{:S(2)}) async-start(bf16[4,128,1024]{2,1,0:T(8,128)(2,1)} %maximum_select_fusion.5), calls=%async_computation | async-start | bytes 2097152 | tf_op jit(solution)/shard_map/all_to_all | solution.py:686
  111.6 49.6 %collective-permute-start.7 = (bf16[2,128,1024]{2,1,0:T(8,128)(2,1)}, bf16[2,128,1024]{2,1,0:T(8,128)(2,1)}, u32[]{:S(2)}, u32[]{:S(2)}) collective-permute-start(bf16[2,128,1024]{2,1,0:T(8,128)(2,1)} %get-tuple-element.170), channel_id=1, source_target_pairs={{0,4},{4,0},{1,5},{5,1},{2,6},{6,2},{3,7},{7,3},{8,12},{12,8},{9,1... | collective-permute-start | bytes 1572872 | tf_op jit(solution)/shard_map/ppermute | solution.py:625
  135.7 32.6 %collective-permute-start.1 = (bf16[4,128,1024]{2,1,0:T(8,128)(2,1)S(1)}, bf16[4,128,1024]{2,1,0:T(8,128)(2,1)S(1)}, u32[]{:S(2)}, u32[]{:S(2)}) collective-permute-start(bf16[4,128,1024]{2,1,0:T(8,128)(2,1)S(1)} %all-to-all-done), channel_id=1, source_target_pairs={{0,4},{4,0},{1,5},{5,1},{2,6},{6,2},{3,7},{7,3},{8,12},{12,8},{9,1... | collective-permute-start | bytes 3145736 | tf_op jit(solution)/shard_map/ppermute | solution.py:625
  163.6 54.5 %all-to-all-start.2 = ((bf16[4,128,1024]{2,1,0:T(8,128)(2,1)}), bf16[4,128,1024]{2,1,0:T(8,128)(2,1)}, u32[]{:S(2)}, u32[]{:S(2)}) async-start(bf16[4,128,1024]{2,1,0:T(8,128)(2,1)} %maximum_select_fusion.7), calls=%async_computation.2 | async-start | bytes 2097152 | tf_op jit(solution)/shard_map/all_to_all | solution.py:686
  167.9 109.4 %all-gather.18.cloned.1.call-start = ((), (), s32[]{:S(2)}) async-start(), calls=%async_computation.14 | async-start | bytes 2621440 | tf_op jit(solution)/shard_map/all_gather | solution.py:754
  218.2 11.2 %collective-permute-start.4 = (bf16[1024,1024]{1,0:T(8,128)(2,1)}, bf16[1024,1024]{1,0:T(8,128)(2,1)}, u32[]{:S(2)}, u32[]{:S(2)}) collective-permute-start(bf16[1024,1024]{1,0:T(8,128)(2,1)} %convolution_convert_fusion.7), channel_id=1, source_target_pairs={{0,4},{4,0},{1,5},{5,1},{2,6},{6,2},{3,7},{7,3},{8,12},{12,8},{9,1... | collective-permute-start | bytes 6291464 | tf_op jit(solution)/shard_map/ppermute | solution.py:625
  218.7 210.2 %reduce-scatter.18.cloned.1.call-start = ((), (), s32[]{:S(2)}) async-start(), calls=%async_computation.20 | async-start | bytes 2621440 | tf_op jit(solution)/shard_map/reduce_scatter | solution.py:818
  294.7 137.8 %reduce-scatter.12.cloned.1.call-start = ((), (), s32[]{:S(2)}) async-start(), calls=%async_computation.17 | async-start | bytes 2621440 | tf_op jit(solution)/shard_map/reduce_scatter | solution.py:818
  318.7 119.7 %reduce-scatter.16.cloned.1.call-start = ((), (), s32[]{:S(2)}) async-start(), calls=%async_computation.19 | async-start | bytes 5242880 | tf_op jit(solution)/shard_map/reduce_scatter | solution.py:818
  330.5 165.7 %reduce-scatter.8.cloned.1.call-start = ((), (), s32[]{:S(2)}) async-start(), calls=%async_computation.15 | async-start | bytes 6225920 | tf_op jit(solution)/shard_map/reduce_scatter | solution.py:818
  412.8 51.1 %all-to-all-start.1 = ((bf16[4,128,1024]{2,1,0:T(8,128)(2,1)}), bf16[4,128,1024]{2,1,0:T(8,128)(2,1)}, u32[]{:S(2)}, u32[]{:S(2)}) async-start(bf16[4,128,1024]{2,1,0:T(8,128)(2,1)} %fusion.17), calls=%async_computation.1 | async-start | bytes 2097152 | tf_op jit(solution)/shard_map/all_to_all | solution.py:691
  417.5 130.2 %reduce-scatter.14.cloned.1.call-start = ((), (), s32[]{:S(2)}) async-start(), calls=%async_computation.18 | async-start | bytes 655360 | tf_op jit(solution)/shard_map/reduce_scatter | solution.py:836
  428.9 20.4 %collective-permute-start.10 = (bf16[4,128,1024]{2,1,0:T(8,128)(2,1)}, bf16[4,128,1024]{2,1,0:T(8,128)(2,1)S(1)}, u32[]{:S(2)}, u32[]{:S(2)}) collective-permute-start(bf16[4,128,1024]{2,1,0:T(8,128)(2,1)} %dynamic-slice_bitcast_fusion), channel_id=1, source_target_pairs={{0,4},{4,0},{1,5},{5,1},{2,6},{6,2},{3,7},{7,3},{8,12},{12,8},{9,1... | collective-permute-start | bytes 3145736 | tf_op jit(solution)/shard_map/ppermute | solution.py:625
  449.2 100.8 %reduce-scatter.20.cloned.1.call-start = ((), (), s32[]{:S(2)}) async-start(), calls=%async_computation.21 | async-start | bytes 1966080 | tf_op jit(solution)/shard_map/reduce_scatter | solution.py:836
  463.9 31.4 %all-to-all-start.3 = ((bf16[4,128,1024]{2,1,0:T(8,128)(2,1)}), bf16[4,128,1024]{2,1,0:T(8,128)(2,1)S(1)}, u32[]{:S(2)}, u32[]{:S(2)}) async-start(bf16[4,128,1024]{2,1,0:T(8,128)(2,1)} %fusion.11), calls=%async_computation.3 | async-start | bytes 2097152 | tf_op jit(solution)/shard_map/all_to_all | solution.py:691
  468.9 115.3 %reduce-scatter.10.cloned.1.call-start = ((), (), s32[]{:S(2)}) async-start(), calls=%async_computation.16 | async-start | bytes 1310720 | tf_op jit(solution)/shard_map/reduce_scatter | solution.py:836
  473.5 66.9 %collective-permute-start.6 = (bf16[2,128,1024]{2,1,0:T(8,128)(2,1)}, bf16[2,128,1024]{2,1,0:T(8,128)(2,1)}, u32[]{:S(2)}, u32[]{:S(2)}) collective-permute-start(bf16[2,128,1024]{2,1,0:T(8,128)(2,1)} %get-tuple-element.172), channel_id=1, source_target_pairs={{0,4},{4,0},{1,5},{5,1},{2,6},{6,2},{3,7},{7,3},{8,12},{12,8},{9,1... | collective-permute-start | bytes 1572872 | tf_op jit(solution)/shard_map/ppermute | solution.py:625
  496.3 47.1 %collective-permute-start.11 = (bf16[2,128,1024]{2,1,0:T(8,128)(2,1)}, bf16[2,128,1024]{2,1,0:T(8,128)(2,1)}, u32[]{:S(2)}, u32[]{:S(2)}) collective-permute-start(bf16[2,128,1024]{2,1,0:T(8,128)(2,1)} %get-tuple-element.168), channel_id=1, source_target_pairs={{0,4},{4,0},{1,5},{5,1},{2,6},{6,2},{3,7},{7,3},{8,12},{12,8},{9,1... | collective-permute-start | bytes 1572872 | tf_op jit(solution)/shard_map/ppermute | solution.py:625
  498.7 47.5 %collective-permute-start.12 = (bf16[128,2432]{0,1:T(8,128)(2,1)}, bf16[128,2432]{0,1:T(8,128)(2,1)S(1)}, u32[]{:S(2)}, u32[]{:S(2)}) collective-permute-start(bf16[128,2432]{0,1:T(8,128)(2,1)} %bitcast.283), channel_id=1, source_target_pairs={{0,4},{4,0},{1,5},{5,1},{2,6},{6,2},{3,7},{7,3},{8,12},{12,8},{9,1... | collective-permute-start | bytes 1867784 | tf_op jit(solution)/shard_map/ppermute | solution.py:625
  (39 other events, 370.9 us)
Sparse Core Ops, SparseCore 0:
  10.7 30.6 all-gather.19
  43.5 45.4 all-gather.21
  90.8 57.8 all-gather.11
  150.3 35.1 all-gather.13
  187.8 52.5 all-gather.15
  242.0 35.1 all-gather.17
  294.8 35.1 reduce-scatter.17
  333.2 35.2 reduce-scatter.11
  371.5 52.6 reduce-scatter.15
  427.4 59.2 reduce-scatter.7
  489.0 21.5 reduce-scatter.13
  513.0 33.7 reduce-scatter.19
  549.2 35.0 reduce-scatter.9

commit v2 on v1

--- a/solution.py
+++ b/solution.py
@@ -600,6 +600,291 @@
     )(proj, proj, out, states, back, dq, dkv, *params)
 
 
+MESH = pl.DeviceIdType.MESH
+
+
+def landed(ref, sem):
+    pltpu.make_async_copy(ref, ref, sem).wait()
+
+
+def spread_kernel(
+    pack_ref,
+    next_ref,
+    shared_ref,
+    x_ref,
+    small_ref,
+    w_ref,
+    v_ref,
+    full_ref,
+    params_ref,
+    near_sem,
+    out_sem,
+    part_sem,
+    fromx_sem,
+    fromy_sem,
+    overx_sem,
+    overy_sem,
+    tox_sem,
+    toy_sem,
+    relx_sem,
+    rely_sem,
+    row_sem,
+    row_out,
+    pair_sem,
+    pair_out,
+    param_sem,
+    param_out,
+):
+    plane = lax.axis_index("plane")
+    core = lax.axis_index("core")
+    place = lax.axis_index("tensor")
+    xside = plane + 1 - 2 * (plane % 2)
+    yside = plane + 2 - 4 * (plane // 2)
+    across = xside + 2 - 4 * (xside // 2)
+    target = place // 2
+    column = place % 2
+    share, width = pack_ref.shape
+    narrow = next_ref.shape[1]
+    rest = shared_ref.shape[2]
+    half = share
+    rows_dev = x_ref.shape[1]
+
+    barrier = pltpu.get_barrier_semaphore()
+    for step in range(4):
+        for side in range(2):
+            if step or side:
+                pl.semaphore_signal(
+                    barrier,
+                    inc=1,
+                    device_id={"core": (core + side) % 2, "tensor": (place + step) % 4},
+                    device_id_type=MESH,
+                )
+    for neighbour in (xside, yside):
+        pl.semaphore_signal(
+            barrier, inc=1, device_id={"plane": neighbour}, device_id_type=MESH
+        )
+    pl.semaphore_wait(barrier, 9)
+
+    def block(at, part):
+        return pl.ds(pl.multiple_of(at * 2 * share + part * share, share), share)
+
+    def piece(at, part, col):
+        return w_ref.at[block(at, part), pl.ds(pl.multiple_of(col * width, width), width)]
+
+    def next_piece(at, part, col):
+        return v_ref.at[block(at, part), pl.ds(pl.multiple_of(col * narrow, narrow), narrow)]
+
+    def rest_piece(at, part):
+        return w_ref.at[block(at, part), pl.ds(2 * width, rest)]
+
+    started = []
+
+    def send(src, dst, send_sem, recv_sem, device):
+        copy = pltpu.make_async_remote_copy(
+            src_ref=src,
+            dst_ref=dst,
+            send_sem=send_sem,
+            recv_sem=recv_sem,
+            device_id=device,
+            device_id_type=MESH,
+        )
+        copy.start()
+        started.append((src, send_sem))
+
+    mine = piece(plane, core, column)
+    slot = core * 2 + column
+    mine_next = next_piece(plane, core, column)
+
+    def send_parts(src, dst, at, recv_sem):
+        for step in (2, 1, 3):
+            send(
+                src,
+                dst,
+                out_sem.at[at + step],
+                recv_sem,
+                {"core": target, "tensor": (place + step) % 4},
+            )
+
+    send_parts(pack_ref, mine, 0, part_sem.at[slot])
+
+    params = params_ref.at[column]
+
+    @pl.when(target == core)
+    def _():
+        pltpu.make_async_copy(pack_ref, mine, part_sem.at[slot]).start()
+        pltpu.make_async_copy(next_ref, mine_next, part_sem.at[6 + slot]).start()
+        pltpu.make_async_copy(small_ref, params, param_sem.at[column]).start()
+        for step in range(1, 4):
+            pltpu.make_async_remote_copy(
+                src_ref=small_ref,
+                dst_ref=params,
+                send_sem=param_out.at[step],
+                recv_sem=param_sem.at[column],
+                device_id={"tensor": (place + step) % 4},
+                device_id_type=MESH,
+            ).start()
+
+    @pl.when(target != core)
+    def _():
+        pltpu.make_async_remote_copy(
+            src_ref=pack_ref,
+            dst_ref=mine,
+            send_sem=out_sem.at[0],
+            recv_sem=part_sem.at[slot],
+            device_id={"core": 1 - core},
+            device_id_type=MESH,
+        ).start()
+        pltpu.make_async_remote_copy(
+            src_ref=next_ref,
+            dst_ref=mine_next,
+            send_sem=out_sem.at[4],
+            recv_sem=part_sem.at[6 + slot],
+            device_id={"core": 1 - core},
+            device_id_type=MESH,
+        ).start()
+
+    own_rest = rest_piece(plane, core)
+    near = pltpu.make_async_copy(shared_ref.at[core], own_rest, part_sem.at[4 + core])
+    near.start()
+    send(
+        shared_ref.at[1 - core],
+        own_rest,
+        near_sem.at[0],
+        part_sem.at[4 + core],
+        {"core": 1 - core},
+    )
+
+    def rows_at(at, side):
+        return full_ref.at[pl.ds(pl.multiple_of(at * rows_dev + side * half, half), half)]
+
+    for seq in range(2):
+        for side in range(2):
+            goal = 2 * core + seq
+            src = x_ref.at[seq, pl.ds(side * half, half)]
+            dst = rows_at(place, side)
+            here = jnp.logical_and(core == side, goal == place)
+
+            @pl.when(here)
+            def _():
+                pltpu.make_async_copy(src, dst, row_sem.at[place]).start()
+
+            @pl.when(jnp.logical_not(here))
+            def _():
+                pltpu.make_async_remote_copy(
+                    src_ref=src,
+                    dst_ref=dst,
+                    send_sem=row_out.at[seq * 2 + side],
+                    recv_sem=row_sem.at[place],
+                    device_id={"core": side, "tensor": goal},
+                    device_id_type=MESH,
+                ).start()
+
+    send_parts(next_ref, mine_next, 4, part_sem.at[6 + slot])
+
+    first_col = jnp.where(place // 2 == core, place % 2, 1 - core)
+    order = [(0, None, 0), (0, None, 1)]
+    for kind in (1, 2):
+        for turn in range(2):
+            for part in range(2):
+                order.append((kind, (first_col + turn) % 2, part))
+
+    def at_piece(at, item):
+        kind, col, part = item
+        if kind == 0:
+            return rest_piece(at, part)
+        return piece(at, part, col) if kind == 1 else next_piece(at, part, col)
+
+    def index(item):
+        kind, col, part = item
+        return 4 + part if kind == 0 else (kind - 1) * 6 + part * 2 + col
+
+    def relay(item):
+        at = index(item)
+        if item[2] == 0:
+            landed(at_piece(xside, item), fromx_sem.at[at])
+            ref = at_piece(xside, item)
+            send(ref, ref, rely_sem.at[at], overy_sem.at[at], {"plane": yside})
+        else:
+            landed(at_piece(yside, item), fromy_sem.at[at])
+            ref = at_piece(yside, item)
+            send(ref, ref, relx_sem.at[at], overx_sem.at[at], {"plane": xside})
+
+    for number, item in enumerate(order):
+        at = index(item)
+        ref = at_piece(plane, item)
+        landed(ref, part_sem.at[at])
+        send(ref, ref, tox_sem.at[at], fromx_sem.at[at], {"plane": xside})
+        send(ref, ref, toy_sem.at[at], fromy_sem.at[at], {"plane": yside})
+        if number >= 2:
+            relay(order[number - 2])
+        if number == 5:
+            for step in range(4):
+                at = (place + step) % 4
+                ref = rows_at(at, core)
+                landed(ref, row_sem.at[at])
+                send(ref, ref, pair_out.at[at], pair_sem.at[at], {"core": 1 - core})
+    for item in order[-2:]:
+        relay(item)
+    for step in range(4):
+        at = (place + step) % 4
+        landed(rows_at(at, 1 - core), pair_sem.at[at])
+    for item in order:
+        at = index(item)
+        if item[2] == 0:
+            landed(at_piece(yside, item), fromy_sem.at[at])
+            landed(at_piece(across, item), overy_sem.at[at])
+        else:
+            landed(at_piece(xside, item), fromx_sem.at[at])
+            landed(at_piece(across, item), overx_sem.at[at])
+
+    for src, sem in started:
+        landed(src, sem)
+
+    for at in range(2):
+        landed(params_ref.at[at], param_sem.at[at])
+
+    @pl.when(target == core)
+    def _():
+        for step in range(1, 4):
+            landed(small_ref, param_out.at[step])
+
+    @pl.when(target != core)
+    def _():
+        landed(pack_ref, out_sem.at[0])
+        landed(next_ref, out_sem.at[4])
+
+    for seq in range(2):
+        for side in range(2):
+            here = jnp.logical_and(core == side, 2 * core + seq == place)
+
+            @pl.when(jnp.logical_not(here))
+            def _():
+                landed(x_ref.at[seq, pl.ds(side * half, half)], row_out.at[seq * 2 + side])
+
+
+def spread(pack, following, shared, x_rows, small):
+    share, width = pack.shape
+    narrow = following.shape[1]
+    rest = shared.shape[2]
+    rows = x_rows.shape[1] * 4
+    dma = pltpu.SemaphoreType.DMA
+    any_space = pl.BlockSpec(memory_space=pl.ANY)
+    return pl.pallas_call(
+        spread_kernel,
+        in_specs=[any_space] * 5,
+        out_specs=[any_space] * 4,
+        out_shape=[
+            jax.ShapeDtypeStruct((8 * share, 2 * width + rest), pack.dtype),
+            jax.ShapeDtypeStruct((8 * share, 2 * narrow), pack.dtype),
+            jax.ShapeDtypeStruct((rows, x_rows.shape[2]), x_rows.dtype),
+            jax.ShapeDtypeStruct((2,) + small.shape, small.dtype),
+        ],
+        scratch_shapes=[dma((1,)), dma((8,))] + [dma((10,))] * 9 + [dma((4,))] * 6,
+        compiler_params=pltpu.CompilerParams(collective_id=1, has_side_effects=True),
+        name="spread",
+    )(pack, following, shared, x_rows, small)
+
+
 def rms_norm(values, gain_vec):
     return values * lax.rsqrt(jnp.mean(values * values, axis=-1, keepdims=True) + EPS) * gain_vec
 
@@ -702,7 +987,8 @@
         shaped = values.reshape(groups, 2, half_rows, -1)
         return lax.dynamic_index_in_dim(shaped, 1 - core, 1, False)
 
-    x_low = positions_in(layer_in)
+    out_dev = chans_dev + query_dev
+    pack_two = jnp.concatenate([mamba_proj.T, attn_proj.T], axis=1)
     pack_one = jnp.concatenate(
         [
             mixer_weight.reshape(share, 2 * chans_dev),
@@ -711,54 +997,58 @@
         ],
         axis=1,
     )
-    all_one = lax.all_gather(pack_one, "tensor", axis=0)
     kv_heads = key_value_weight.reshape(share, 2, 2, HEAD_SIZE)
 
-    def lay_one(pack, at):
+    def shared_for(at):
         return jnp.concatenate(
             [
-                flat(pack),
                 state_weight.reshape(share, 2 * N),
                 lax.dynamic_index_in_dim(kv_heads, at, 2, False).reshape(share, 2 * HEAD_SIZE),
             ],
             axis=1,
         )
 
-    own_one = lay_one(mine(all_one), core)
-    their_one = lay_one(other(all_one), 1 - core)
-    weight_one = lax.all_gather(
-        in_order(own_one, swapped(their_one), 0), "plane", axis=0, tiled=True
-    )
-
-    pack_two = jnp.concatenate(
-        [mamba_proj.T, attn_proj.T, ffn_weight.reshape(share, 2 * hidden_dev), ffn_down.T], axis=1
-    )
-    all_two = lax.all_gather(pack_two, "tensor", axis=0)
-    out_dev = chans_dev + query_dev
-
-    def lay_two(pack):
-        cut = out_dev + hidden_dev
-        return jnp.concatenate(
-            [
-                flat(pack[:, :, :out_dev]),
-                flat(pack[:, :, out_dev:cut]),
-                flat(pack[:, :, cut : cut + hidden_dev]),
-                flat(pack[:, :, cut + hidden_dev :]),
-            ],
-            axis=1,
-        )
-
-    rows_two = in_order(lay_two(mine(all_two)), swapped(lay_two(other(all_two))), 0)
-    edges = (0, held * out_dev, held * (out_dev + 2 * hidden_dev), held * (out_dev + 3 * hidden_dev))
-    weight_two, gate_up_weight, down_weight = (
-        lax.all_gather(rows_two[:, begin:end], "plane", axis=0, tiled=True)
-        for begin, end in zip(edges[:-1], edges[1:])
-    )
-
     small_in = jnp.concatenate(
         [conv_channels.reshape(-1), step_bias, decay_log, skip_scale, group_gain]
     )
-    small_mine = mine(lax.all_gather(small_in, "tensor", axis=0))
+    small_pad = -(-small_in.shape[0] // 1024) * 1024
+    small_in = jnp.pad(small_in, (0, small_pad - small_in.shape[0])).reshape(-1, 128)
+    if lax.axis_size("plane") == 4 and groups == 4 and share % 16 == 0:
+        shared = jnp.stack([shared_for(0), shared_for(1)])
+        weight_one, weight_two, x_low, small_mine = spread(
+            pack_one, pack_two, shared, layer_in, small_in
+        )
+    else:
+        x_low = positions_in(layer_in)
+        all_one = lax.all_gather(pack_one, "tensor", axis=0)
+        own_one = jnp.concatenate([flat(mine(all_one)), shared_for(core)], axis=1)
+        their_one = jnp.concatenate([flat(other(all_one)), shared_for(1 - core)], axis=1)
+        weight_one = lax.all_gather(
+            in_order(own_one, swapped(their_one), 0), "plane", axis=0, tiled=True
+        )
+        all_two = lax.all_gather(pack_two, "tensor", axis=0)
+        weight_two = lax.all_gather(
+            in_order(flat(mine(all_two)), swapped(flat(other(all_two))), 0),
+            "plane",
+            axis=0,
+            tiled=True,
+        )
+        small_mine = mine(lax.all_gather(small_in, "tensor", axis=0))
+    small_mine = small_mine.reshape(held, -1)
+
+    pack_three = jnp.concatenate([ffn_weight.reshape(share, 2 * hidden_dev), ffn_down.T], axis=1)
+    all_three = lax.all_gather(pack_three, "tensor", axis=0)
+    all_three, weight_one = lax.optimization_barrier((all_three, weight_one))
+
+    def lay_three(pack):
+        cuts = [pack[:, :, at * hidden_dev : (at + 1) * hidden_dev] for at in range(3)]
+        return jnp.concatenate([flat(cut) for cut in cuts], axis=1)
+
+    rows_three = in_order(lay_three(mine(all_three)), swapped(lay_three(other(all_three))), 0)
+    weight_three = lax.all_gather(rows_three, "plane", axis=0, tiled=True)
+    gate_up_weight = weight_three[:, : 2 * held * hidden_dev]
+    down_weight = weight_three[:, 2 * held * hidden_dev :]
+
     cuts = []
     at = 0
     for size in (KCONV * chans_dev, heads_dev, heads_dev, heads_dev, chans_dev):
@@ -771,7 +1061,7 @@
     skip = jnp.repeat(cuts[3].reshape(1, -1), HEAD_SIZE, axis=1)
     gain = cuts[4].reshape(1, -1)
 
-    lengths = lax.all_gather(seq_lengths, "core", axis=0).reshape(-1)
+    lengths = in_order(seq_lengths, swapped(seq_lengths), 0)
     seq_len = lengths[place]
     len_one = seq_len.reshape(1)
     valid_rows = (jnp.arange(seq_total, dtype=jnp.int32) < seq_len).astype(jnp.float32)[:, None]

time: 602 us -> 549 us (0.912)
  waiting for transfers between devices: 158 us -> 35.6 us
  Pallas kernels: 80 us -> 178 us
  blocking collectives: 82.7 us -> 63.9 us
  local copies, waits for them, and re-layouts: 75.2 us -> 66.6 us
  starting transfers between devices: 22.3 us -> 30.9 us
  matrix products: 100 us -> 93 us
    all_gather x6 -> x2, waiting for transfers between devices: 98.2 us -> 0.02 us  [the longest x1 0.02 us: body(): all_three = lax.all_gather(pack_three, 'tensor', axis=0)]
    pallas_call x0 -> x1, Pallas kernels: none -> 98.1 us  [spread(): pl.pallas_call(spread_kernel, in_specs=[any_space] * 5, out_specs=[any_sp...]
    all_to_all x2 -> x1, waiting for transfers between devices: 21.8 us -> 0.01 us  [positions_in(): own = lax.all_to_all(four, 'tensor', 0, 0, tiled=True)]
    unnamed x2 -> x0, blocking collectives: 18.9 us -> none
    ppermute x15 -> x13, starting transfers between devices: 3.19 us -> 11.5 us  [swapped(): return lax.ppermute(values, 'core', SWAP)]
    dot_general x4, matrix products: 41.7 us -> 34.4 us  [dot(): return jnp.dot(left, right, preferred_element_type=jnp.float32)]
    unnamed x85 -> x75, local copies, waits for them, and re-layouts: 22 us -> 17.7 us
    select_n x10 -> x9, other arithmetic: 21.4 us -> 19.1 us  [in_order(): jnp.where(first, jnp.concatenate([own, others], axis=axis), jnp.concatena...]
  transfers between devices with their start and end apart: 32 -> 25, of which waited for: 12 -> 6; matrix products, arithmetic and copies ran while one was open for 34% -> 33% of each run, Pallas kernels for 13% -> 33%
where the time goes in v2:
time: 549 us; the launch traced here: 541 us
  Pallas kernels  178 us (32%)
  matrix products  93 us (17%)
  local copies, waits for them, and re-layouts  66.6 us (12%)
  blocking collectives  63.9 us (12%)
  other arithmetic  57.5 us (10%)
  waiting for transfers between devices  35.6 us (6%)
  starting transfers between devices  30.9 us (6%)
  between operations  15.2 us (3%)
    pallas_call x1, Pallas kernels, spread(): pl.pallas_call(spread_kernel, in_specs=[any_space] * 5, out_specs=[any_sp...  98.1 us
    psum x1, blocking collectives, body(): small_sum = lax.psum(small_out, ('plane', 'core', 'tensor'))  39.1 us
    pallas_call x1, Pallas kernels, mamba_backward(): pl.pallas_call(mamba_backward_kernel, grid=(chunks,), in_specs=[rows_of(c...  36.3 us
    dot_general x4, matrix products, dot(): return jnp.dot(left, right, preferred_element_type=jnp.float32)  34.4 us
    dot_general x4, matrix products, dot_tn(): lax.dot_general(left, right, (((0,), (0,)), ((), ())), preferred_element_...  29.6 us
    dot_general x4, matrix products, dot_nt(): lax.dot_general(left, right, (((1,), (1,)), ((), ())), preferred_element_...  28.9 us
    all_gather x1, blocking collectives, body(): lax.all_gather(shared_low, 'tensor', axis=0)  24.8 us
    all_to_all x2, waiting for transfers between devices, positions_out(): four = lax.all_to_all(own, 'tensor', 0, 0, tiled=True)  20.8 us
  transfers between devices with their start and end apart: 25, of which 6 were waited for; matrix products, arithmetic and copies ran while one was open for 33% of the time, Pallas kernels for 33%

profile of v2, /device:TPU:0, one launch (start us, length us, event | category | flops | bytes accessed | tf_op | source)
XLA Modules:
  0.0 540.8 jit_solution(7830611551083525468)
XLA Ops:
  18.0 98.1 %spread.1 = (bf16[1024,2432]{1,0:T(8,128)(2,1)}, bf16[1024,1024]{1,0:T(8,128)(2,1)}, bf16[1024,1024]{1,0:T(8,128)(2,1)}, f32[2,16,128]{2,1,0:T(8,128)}) custom-call(bf16[128,1024]{1,0:T(8,128)(2,1)} %fusion.38.pack_ref, bf16[128,512]{1,0:T(8,128)(2,1)} %pad_maximum_fusion.7.next_ref, bf16[2,128,384]{2,1,0:T(8,128)(2,1)} %pad_maximum_fusion.6.shared_ref, ...), custom_call_target="tpu_custom_call" | custom-call | tf_op jit(solution)/shard_map/spread/pallas_call | solution.py:872
  118.3 8.2 %collective-permute-start.2 = (bf16[128,3072]{0,1:T(8,128)(2,1)S(1)}, bf16[128,3072]{0,1:T(8,128)(2,1)}, u32[]{:S(2)}, u32[]{:S(2)}) collective-permute-start(bf16[128,3072]{0,1:T(8,128)(2,1)S(1)} %pad_maximum_fusion), channel_id=1, source_target_pairs={{0,4},{4,0},{1,5},{5,1},{2,6},{6,2},{3,7},{7,3},{8,12},{12,8},{9,1... | collective-permute-start | bytes 2359304 | tf_op jit(solution)/shard_map/ppermute | solution.py:910
  128.5 7.2 %maximum_select_fusion.1 = bf16[256,3072]{0,1:T(8,128)(2,1)} fusion(bf16[128,3072]{0,1:T(8,128)(2,1)} %collective-permute-done.2, bf16[128,1024]{0,1:T(8,128)(2,1)S(1)} %bitcast.246, bf16[128,1024]{0,1:T(8,128)(2,1)S(1)} %bitcast.244, bf16[128,1024]{0,1:T(8,128)(2,1)S(1)} %bitcast.243, pred[]{:T(512)S(6)} %eq.3), kind=kLoop, calls=%fused_computation.57 | loop fusion | flops 13369344 | bytes 3145729 | tf_op jit(solution)/shard_map/jit(_where)/select_n | solution.py:957
  147.4 8.5 %all-to-all-start.1 = ((bf16[4,128,1024]{1,2,0:T(8,128)(2,1)}), bf16[4,128,1024]{1,2,0:T(8,128)(2,1)S(1)}, u32[]{:S(2)}, u32[]{:S(2)}) async-start(bf16[4,128,1024]{1,2,0:T(8,128)(2,1)} %maximum_select_fusion.4), calls=%async_computation.1 | async-start | bytes 2097152 | tf_op jit(solution)/shard_map/all_to_all | solution.py:971
  156.1 10.7 %fusion.34.q_ref.kv_ref.proj_ref.before_ref = f32[1024,2432]{1,0:T(8,128)} fusion(bf16[1024,2432]{1,0:T(8,128)(2,1)} %get-tuple-element.40, bf16[1024,1024]{1,0:T(8,128)(2,1)S(1)} %copy-done.3, f32[1024]{0:T(1024)S(1)} %copy-done.11, f32[1024]{0:T(1024)S(1)} %add_rsqrt_fusion.1), kind=kOutput, calls=%fused_computation.70 | convolution fusion | flops 5104467968 | bytes 17047552 | tf_op jit(solution)/shard_map/dot_general | solution.py:28
  166.7 11.2 %attention_forward.1 = (bf16[1024,256]{1,0:T(8,128)(2,1)}, f32[1024,256]{1,0:T(8,128)}) custom-call(s32[1]{0:T(128)} %dynamic_slice.96.len_ref, f32[1024,2432]{1,0:T(8,128)} %fusion.34.q_ref.kv_ref.proj_ref.before_ref, f32[1024,2432]{1,0:T(8,128)} %fusion.34.q_ref.kv_ref.proj_ref.before_ref, f32[1024,128]{1,0:T(8,128)} %copy.143.cos_ref, ...), custom_call_target="tpu_custom_call" | custom-call | tf_op jit(solution)/shard_map/attention_forward/pallas_call | solution.py:181
  178.0 14.4 %mamba_forward.1 = (bf16[1024,1024]{1,0:T(8,128)(2,1)}, f32[1024,768]{1,0:T(8,128)}, f32[8,128,768]{2,1,0:T(8,128)}) custom-call(f32[1024,2432]{1,0:T(8,128)} %fusion.34.q_ref.kv_ref.proj_ref.before_ref, bf16[1024,256]{1,0:T(8,128)(2,1)} %get-tuple-element.41.attn_ref, f32[4,1024]{1,0:T(4,128)} %pad_maximum_fusion.12.taps_ref, f32[2,128]{1,0:T(2,128)} %pad.25.bias_ref, ...), custom_call_target="tpu_custom_call" | custom-call | tf_op jit(solution)/shard_map/mamba_forward/pallas_call | solution.py:356
  192.3 5.9 %convolution_convert_fusion.6 = bf16[1024,1024]{1,0:T(8,128)(2,1)} fusion(bf16[1024,1024]{1,0:T(8,128)(2,1)} %get-tuple-element.43, bf16[1024,1024]{1,0:T(8,128)(2,1)} %get-tuple-element.44), kind=kOutput, calls=%fused_computation.53 | convolution fusion | flops 2148532224 | bytes 6291456 | tf_op jit(solution)/shard_map/dot_general | solution.py:32
  206.1 5.5 %copy.155 = f32[4,2,128,1024]{3,2,1,0:T(8,128)} copy(f32[4,2,128,1024]{2,3,0,1:T(8,128)} %fusion.19) | data formatting | bytes 8388608 | tf_op jit(solution)/shard_map/convert_element_type | solution.py:24
  215.4 5.1 multiply_reduce_fusion.1
  220.5 8.2 %fusion.11 = f32[1024,2048]{1,0:T(8,128)S(1)} fusion(bf16[1024,3072]{0,1:T(8,128)(2,1)} %all-gather.5.cloned.1.call-done, f32[1024,1024]{1,0:T(8,128)} %get-tuple-element.136, f32[1024]{0:T(1024)S(1)} %copy-done.10, f32[1024]{0:T(1024)S(1)} %add_rsqrt_fusion), kind=kOutput, calls=%fused_computation.26 | convolution fusion | flops 4298113024 | bytes 16785408 | tf_op jit(solution)/shard_map/dot_general | solution.py:28
  228.8 8.2 %fusion.37 = (f32[1024,1024]{1,0:T(8,128)}, f32[1024,1024]{1,0:T(8,128)}, bf16[1024,1024]{1,0:T(8,128)(2,1)S(1)}) fusion(f32[1024,2048]{1,0:T(8,128)S(1)} %fusion.11, bf16[1024,1024]{1,0:T(8,128)(2,1)S(1)} %copy-done.6, bf16[1024,3072]{0,1:T(8,128)(2,1)} %all-gather.5.cloned.1.call-done), kind=kOutput, calls=%fused_computation.79 | convolution fusion | flops 2165309440 | bytes 23068672 | tf_op jit(solution)/shard_map/dot_general | solution.py:28
  242.2 9.3 %fusion.24 = bf16[1024,1024]{1,0:T(8,128)(2,1)S(1)} fusion(bf16[1024,3072]{0,1:T(8,128)(2,1)} %all-gather.5.cloned.1.call-done, f32[1024,1024]{1,0:T(8,128)} %get-tuple-element.138, f32[1024,1024]{1,0:T(8,128)} %get-tuple-element.137), kind=kOutput, calls=%fused_computation.48 | convolution fusion | flops 4300210176 | bytes 14680064 | tf_op jit(solution)/shard_map/dot_general | solution.py:32
  266.2 11.7 %convolution_convert_fusion.1 = bf16[1024,2048]{1,0:T(8,128)(2,1)} fusion(f32[1024,1024]{1,0:T(8,128)} %get-tuple-element.138, f32[1024,1024]{1,0:T(8,128)} %get-tuple-element.137, f32[1024,1024]{1,0:T(8,128)} %get-tuple-element.136, f32[1024]{0:T(1024)S(1)} %copy-done.10, f32[1024]{0:T(1024)S(1)} %add_rsqrt_fusion), kind=kOutput, calls=%fused_computation.23 | convolution fusion | flops 4304404480 | bytes 16785408 | tf_op jit(solution)/shard_map/dot_general | solution.py:38
  278.0 7.3 %fusion.60 = (bf16[1024,1024]{1,0:T(8,128)(2,1)S(1)}, f32[1024,1024]{1,0:T(8,128)}) fusion(bf16[1024,1024]{1,0:T(8,128)(2,1)} %get-tuple-element.44, f32[1024,1024]{1,0:T(8,128)} %copy-done.4), kind=kOutput, calls=%fused_computation.161 | convolution fusion | flops 2149580800 | bytes 12582912 | tf_op jit(solution)/shard_map/dot_general | solution.py:28
  286.2 18.3 %attention_backward.1 = (bf16[1024,256]{1,0:T(8,128)(2,1)}, bf16[1024,128]{1,0:T(8,128)(2,1)}) custom-call(s32[1]{0:T(128)} %dynamic_slice.96.len_ref, f32[1024,2432]{1,0:T(8,128)} %fusion.34.q_ref.kv_ref.proj_ref.before_ref, f32[1024,2432]{1,0:T(8,128)} %fusion.34.q_ref.kv_ref.proj_ref.before_ref, f32[1024,128]{1,0:T(8,128)} %copy.143.cos_ref, ...), custom_call_target="tpu_custom_call" | custom-call | tf_op jit(solution)/shard_map/attention_backward/pallas_call | solution.py:198
  304.5 36.3 %mamba_backward.1 = (bf16[1024,2432]{1,0:T(8,128)(2,1)}, f32[4,1024]{1,0:T(4,128)}, f32[1,768]{1,0:T(1,128)}, f32[1,768]{1,0:T(1,128)}, f32[2,128]{1,0:T(2,128)}, /*index=5*/f32[2,128]{1,0:T(2,128)}) custom-call(f32[1024,2432]{1,0:T(8,128)} %fusion.34.q_ref.kv_ref.proj_ref.before_ref, f32[1024,2432]{1,0:T(8,128)} %fusion.34.q_ref.kv_ref.proj_ref.before_ref, ...), custom_call_target="tpu_custom_call" | custom-call | tf_op jit(solution)/shard_map/mamba_backward/pallas_call | solution.py:569
  340.8 10.4 %convolution_convert_fusion = bf16[1024,2432]{1,0:T(8,128)(2,1)} fusion(bf16[1024,2432]{1,0:T(8,128)(2,1)} %get-tuple-element.51, bf16[1024,1024]{1,0:T(8,128)(2,1)S(1)} %copy-done.3, f32[1024]{0:T(1024)S(1)} %copy-done.11, f32[1024]{0:T(1024)S(1)} %add_rsqrt_fusion.1), kind=kOutput, calls=%fused_computation.4 | convolution fusion | flops 5106958336 | bytes 12066816 | tf_op jit(solution)/shard_map/dot_general | solution.py:38
  360.1 5.1 all-to-all-start
  365.2 9.0 %convolution_convert_fusion.4 = bf16[1024,1024]{1,0:T(8,128)(2,1)S(1)} fusion(bf16[1024,2432]{1,0:T(8,128)(2,1)} %get-tuple-element.51, bf16[1024,2432]{1,0:T(8,128)(2,1)} %get-tuple-element.40), kind=kOutput, calls=%fused_computation.51 | convolution fusion | flops 5101322240 | bytes 12058624 | tf_op jit(solution)/shard_map/dot_general | solution.py:32
  411.9 5.0 all-to-all-start.2
  422.2 20.8 %all-to-all-done.2 = bf16[4,128,1024]{2,1,0:T(8,128)(2,1)S(1)} async-done(((bf16[4,128,1024]{2,1,0:T(8,128)(2,1)}), bf16[4,128,1024]{2,1,0:T(8,128)(2,1)S(1)}, u32[]{:S(2)}, u32[]{:S(2)}) %all-to-all-start.2) | async-done | bytes 1048608 | tf_op jit(solution)/shard_map/all_to_all | solution.py:976
  446.2 39.1 %psum.7 = f32[10824]{0:T(1024)S(1)} all-reduce(f32[10824]{0:T(1024)} %pad_maximum_fusion.11), channel_id=1, replica_groups=mesh['plane'=4,'core'=2,'tensor'=4] {'plane','core','tensor'}, use_global_device_ids=true, to_apply=%region_8.9 | all-reduce | flops 10824 | bytes 86592 | tf_op jit(solution)/shard_map/psum | solution.py:1197
  499.5 24.8 %all-gather.1 = bf16[512,512]{0,1:T(8,128)(2,1)S(1)} all-gather(bf16[128,512]{0,1:T(8,128)(2,1)S(1)} %pad_maximum_fusion.8), channel_id=3, replica_groups=mesh['plane'=4,'core'=2,'tensor'=4] {'tensor'}, dimensions={0}, use_global_device_ids=true | all-gather | bytes 655360 | tf_op jit(solution)/shard_map/all_gather | solution.py:1158
  (257 shorter events, 137.4 us)
Async XLA Ops:
  7.3 108.9 %all-gather.7.cloned.1.call-start = ((), (), s32[]{:S(2)}) async-start(), calls=%async_computation.18 | async-start | bytes 1966080 | tf_op jit(solution)/shard_map/all_gather | solution.py:1040
  10.1 210.4 %all-gather.5.cloned.1.call-start = ((), (), s32[]{:S(2)}) async-start(), calls=%async_computation.10 | async-start | bytes 7864320 | tf_op jit(solution)/shard_map/all_gather | solution.py:1048
  118.3 10.2 %collective-permute-start.2 = (bf16[128,3072]{0,1:T(8,128)(2,1)S(1)}, bf16[128,3072]{0,1:T(8,128)(2,1)}, u32[]{:S(2)}, u32[]{:S(2)}) collective-permute-start(bf16[128,3072]{0,1:T(8,128)(2,1)S(1)} %pad_maximum_fusion), channel_id=1, source_target_pairs={{0,4},{4,0},{1,5},{5,1},{2,6},{6,2},{3,7},{7,3},{8,12},{12,8},{9,1... | collective-permute-start | bytes 2359304 | tf_op jit(solution)/shard_map/ppermute | solution.py:910
  135.7 8.5 %collective-permute-start = (s32[2]{0:T(128)S(1)}, s32[2]{0:T(128)S(1)}, u32[]{:S(2)}, u32[]{:S(2)}) collective-permute-start(s32[2]{0:T(128)S(1)} %copy-done.24), channel_id=1, source_target_pairs={{0,4},{4,0},{1,5},{5,1},{2,6},{6,2},{3,7},{7,3},{8,12},{12,8},{9,1... | collective-permute-start | bytes 32 | tf_op jit(solution)/shard_map/ppermute | solution.py:910
  137.2 7.7 %collective-permute-start.5 = (bf16[2,128,1024]{1,2,0:T(8,128)(2,1)}, bf16[2,128,1024]{1,2,0:T(8,128)(2,1)}, u32[]{:S(2)}, u32[]{:S(2)}) collective-permute-start(bf16[2,128,1024]{1,2,0:T(8,128)(2,1)} %bitcast.38), channel_id=1, source_target_pairs={{0,4},{4,0},{1,5},{5,1},{2,6},{6,2},{3,7},{7,3},{8,12},{12,8},{9,1... | collective-permute-start | bytes 1572872 | tf_op jit(solution)/shard_map/ppermute | solution.py:910
  147.4 51.0 %all-to-all-start.1 = ((bf16[4,128,1024]{1,2,0:T(8,128)(2,1)}), bf16[4,128,1024]{1,2,0:T(8,128)(2,1)S(1)}, u32[]{:S(2)}, u32[]{:S(2)}) async-start(bf16[4,128,1024]{1,2,0:T(8,128)(2,1)} %maximum_select_fusion.4), calls=%async_computation.1 | async-start | bytes 2097152 | tf_op jit(solution)/shard_map/all_to_all | solution.py:971
  155.8 221.0 %reduce-scatter.18.cloned.1.call-start = ((), (), s32[]{:S(2)}) async-start(), calls=%async_computation.16 | async-start | bytes 2621440 | tf_op jit(solution)/shard_map/reduce_scatter | solution.py:1108
  198.3 17.1 %collective-permute-start.1 = (bf16[1024,1024]{1,0:T(8,128)(2,1)}, bf16[1024,1024]{1,0:T(8,128)(2,1)}, u32[]{:S(2)}, u32[]{:S(2)}) collective-permute-start(bf16[1024,1024]{1,0:T(8,128)(2,1)} %convolution_convert_fusion.6), channel_id=1, source_target_pairs={{0,4},{4,0},{1,5},{5,1},{2,6},{6,2},{3,7},{7,3},{8,12},{12,8},{9,1... | collective-permute-start | bytes 6291464 | tf_op jit(solution)/shard_map/ppermute | solution.py:910
  198.4 5.3 collective-permute-start.6
  242.1 138.3 %reduce-scatter.12.cloned.1.call-start = ((), (), s32[]{:S(2)}) async-start(), calls=%async_computation.13 | async-start | bytes 2621440 | tf_op jit(solution)/shard_map/reduce_scatter | solution.py:1108
  251.5 4.2 collective-permute-start.7
  266.1 120.2 %reduce-scatter.16.cloned.1.call-start = ((), (), s32[]{:S(2)}) async-start(), calls=%async_computation.15 | async-start | bytes 5242880 | tf_op jit(solution)/shard_map/reduce_scatter | solution.py:1108
  277.9 166.0 %reduce-scatter.8.cloned.1.call-start = ((), (), s32[]{:S(2)}) async-start(), calls=%async_computation.11 | async-start | bytes 6225920 | tf_op jit(solution)/shard_map/reduce_scatter | solution.py:1108
  360.1 51.9 %all-to-all-start = ((bf16[4,128,1024]{2,1,0:T(8,128)(2,1)}), bf16[4,128,1024]{2,1,0:T(8,128)(2,1)}, u32[]{:S(2)}, u32[]{:S(2)}) async-start(bf16[4,128,1024]{2,1,0:T(8,128)(2,1)} %fusion.22), calls=%async_computation | async-start | bytes 2097152 | tf_op jit(solution)/shard_map/all_to_all | solution.py:976
  365.2 129.1 %reduce-scatter.14.cloned.1.call-start = ((), (), s32[]{:S(2)}) async-start(), calls=%async_computation.14 | async-start | bytes 655360 | tf_op jit(solution)/shard_map/reduce_scatter | solution.py:1126
  376.7 20.7 %collective-permute-start.8 = (bf16[4,128,1024]{2,1,0:T(8,128)(2,1)}, bf16[4,128,1024]{2,1,0:T(8,128)(2,1)S(1)}, u32[]{:S(2)}, u32[]{:S(2)}) collective-permute-start(bf16[4,128,1024]{2,1,0:T(8,128)(2,1)} %dynamic-slice_bitcast_fusion), channel_id=1, source_target_pairs={{0,4},{4,0},{1,5},{5,1},{2,6},{6,2},{3,7},{7,3},{8,12},{12,8},{9,1... | collective-permute-start | bytes 3145736 | tf_op jit(solution)/shard_map/ppermute | solution.py:910
  384.2 11.0 %collective-permute-start.11 = (bf16[2,128,512]{1,2,0:T(8,128)(2,1)}, bf16[2,128,512]{1,2,0:T(8,128)(2,1)}, u32[]{:S(2)}, u32[]{:S(2)}) collective-permute-start(bf16[2,128,512]{1,2,0:T(8,128)(2,1)} %bitcast.258), channel_id=1, source_target_pairs={{0,4},{4,0},{1,5},{5,1},{2,6},{6,2},{3,7},{7,3},{8,12},{12,8},{9,1... | collective-permute-start | bytes 786440 | tf_op jit(solution)/shard_map/ppermute | solution.py:910
  394.9 10.1 %collective-permute-start.12 = (bf16[2,128,1536]{1,2,0:T(8,128)(2,1)}, bf16[2,128,1536]{1,2,0:T(8,128)(2,1)}, u32[]{:S(2)}, u32[]{:S(2)}) collective-permute-start(bf16[2,128,1536]{1,2,0:T(8,128)(2,1)} %pad_maximum_fusion.1), channel_id=1, source_target_pairs={{0,4},{4,0},{1,5},{5,1},{2,6},{6,2},{3,7},{7,3},{8,12},{12,8},{9,1... | collective-permute-start | bytes 2359304 | tf_op jit(solution)/shard_map/ppermute | solution.py:910
  397.3 99.3 %reduce-scatter.20.cloned.1.call-start = ((), (), s32[]{:S(2)}) async-start(), calls=%async_computation.17 | async-start | bytes 1966080 | tf_op jit(solution)/shard_map/reduce_scatter | solution.py:1126
  411.9 31.1 %all-to-all-start.2 = ((bf16[4,128,1024]{2,1,0:T(8,128)(2,1)}), bf16[4,128,1024]{2,1,0:T(8,128)(2,1)S(1)}, u32[]{:S(2)}, u32[]{:S(2)}) async-start(bf16[4,128,1024]{2,1,0:T(8,128)(2,1)} %fusion.16), calls=%async_computation.2 | async-start | bytes 2097152 | tf_op jit(solution)/shard_map/all_to_all | solution.py:976
  416.9 113.6 %reduce-scatter.10.cloned.1.call-start = ((), (), s32[]{:S(2)}) async-start(), calls=%async_computation.12 | async-start | bytes 1310720 | tf_op jit(solution)/shard_map/reduce_scatter | solution.py:1126
  421.6 64.4 %collective-permute-start.4 = (bf16[2,128,1024]{2,1,0:T(8,128)(2,1)}, bf16[2,128,1024]{2,1,0:T(8,128)(2,1)}, u32[]{:S(2)}, u32[]{:S(2)}) collective-permute-start(bf16[2,128,1024]{2,1,0:T(8,128)(2,1)} %get-tuple-element.159), channel_id=1, source_target_pairs={{0,4},{4,0},{1,5},{5,1},{2,6},{6,2},{3,7},{7,3},{8,12},{12,8},{9,1... | collective-permute-start | bytes 1572872 | tf_op jit(solution)/shard_map/ppermute | solution.py:910
  443.9 46.4 %collective-permute-start.9 = (bf16[2,128,1024]{2,1,0:T(8,128)(2,1)}, bf16[2,128,1024]{2,1,0:T(8,128)(2,1)}, u32[]{:S(2)}, u32[]{:S(2)}) collective-permute-start(bf16[2,128,1024]{2,1,0:T(8,128)(2,1)} %get-tuple-element.155), channel_id=1, source_target_pairs={{0,4},{4,0},{1,5},{5,1},{2,6},{6,2},{3,7},{7,3},{8,12},{12,8},{9,1... | collective-permute-start | bytes 1572872 | tf_op jit(solution)/shard_map/ppermute | solution.py:910
  445.6 47.5 %collective-permute-start.10 = (bf16[128,2432]{0,1:T(8,128)(2,1)S(1)}, bf16[128,2432]{0,1:T(8,128)(2,1)S(1)}, u32[]{:S(2)}, u32[]{:S(2)}) collective-permute-start(bf16[128,2432]{0,1:T(8,128)(2,1)S(1)} %bitcast.249), channel_id=1, source_target_pairs={{0,4},{4,0},{1,5},{5,1},{2,6},{6,2},{3,7},{7,3},{8,12},{12,8},{9,1... | collective-permute-start | bytes 1867784 | tf_op jit(solution)/shard_map/ppermute | solution.py:910
  (28 other events, 203.2 us)
Sparse Core Ops, SparseCore 0:
  10.2 75.5 all-gather.6
  135.8 73.1 all-gather.4
  242.2 34.7 reduce-scatter.17
  280.1 35.1 reduce-scatter.11
  318.1 52.6 reduce-scatter.15
  374.1 59.2 reduce-scatter.7
  435.7 21.6 reduce-scatter.13
  459.8 33.9 reduce-scatter.19
  496.2 34.2 reduce-scatter.9

commit v3 on v2

--- a/solution.py
+++ b/solution.py
@@ -610,11 +610,15 @@
 def spread_kernel(
     pack_ref,
     next_ref,
+    ups_ref,
+    downs_ref,
     shared_ref,
     x_ref,
     small_ref,
     w_ref,
     v_ref,
+    up_rows,
+    down_rows,
     full_ref,
     params_ref,
     near_sem,
@@ -634,6 +638,8 @@
     pair_out,
     param_sem,
     param_out,
+    ffn_sem,
+    ffn_out,
 ):
     plane = lax.axis_index("plane")
     core = lax.axis_index("core")
@@ -706,6 +712,7 @@
             )
 
     send_parts(pack_ref, mine, 0, part_sem.at[slot])
+    send_parts(next_ref, mine_next, 4, part_sem.at[6 + slot])
 
     params = params_ref.at[column]
 
@@ -779,7 +786,40 @@
                     device_id_type=MESH,
                 ).start()
 
-    send_parts(next_ref, mine_next, 4, part_sem.at[6 + slot])
+    wide_up, wide_down = ups_ref.shape[2], downs_ref.shape[2]
+    ffn_parts = []
+    for number, (src, dst, size) in enumerate(
+        ((ups_ref, up_rows, wide_up), (downs_ref, down_rows, wide_down))
+    ):
+        goal_ref = dst.at[
+            pl.ds(pl.multiple_of(core * share, share), share),
+            pl.ds(pl.multiple_of(place * size, size), size),
+        ]
+        for step in (2, 1, 3):
+            for side in range(2):
+                send(
+                    src.at[side],
+                    goal_ref,
+                    ffn_out.at[number, 2 * step + side],
+                    ffn_sem.at[number, 2 * place + core],
+                    {"core": side, "tensor": (place + step) % 4},
+                )
+        send(
+            src.at[1 - core],
+            goal_ref,
+            ffn_out.at[number, 0],
+            ffn_sem.at[number, 2 * place + core],
+            {"core": 1 - core},
+        )
+        pltpu.make_async_copy(src.at[core], goal_ref, ffn_sem.at[number, 2 * place + core]).start()
+        for at in range(4):
+            for part in range(2):
+                ffn_parts.append(
+                    (
+                        dst.at[pl.ds(part * share, share), pl.ds(at * size, size)],
+                        ffn_sem.at[number, 2 * at + part],
+                    )
+                )
 
     first_col = jnp.where(place // 2 == core, place % 2, 1 - core)
     order = [(0, None, 0), (0, None, 1)]
@@ -817,7 +857,7 @@
         send(ref, ref, toy_sem.at[at], fromy_sem.at[at], {"plane": yside})
         if number >= 2:
             relay(order[number - 2])
-        if number == 5:
+        if number == 9:
             for step in range(4):
                 at = (place + step) % 4
                 ref = rows_at(at, core)
@@ -842,6 +882,8 @@
 
     for at in range(2):
         landed(params_ref.at[at], param_sem.at[at])
+    for ref, sem in ffn_parts:
+        landed(ref, sem)
 
     @pl.when(target == core)
     def _():
@@ -862,7 +904,7 @@
                 landed(x_ref.at[seq, pl.ds(side * half, half)], row_out.at[seq * 2 + side])
 
 
-def spread(pack, following, shared, x_rows, small):
+def spread(pack, following, ups, downs, shared, x_rows, small):
     share, width = pack.shape
     narrow = following.shape[1]
     rest = shared.shape[2]
@@ -871,18 +913,377 @@
     any_space = pl.BlockSpec(memory_space=pl.ANY)
     return pl.pallas_call(
         spread_kernel,
-        in_specs=[any_space] * 5,
-        out_specs=[any_space] * 4,
+        in_specs=[any_space] * 7,
+        out_specs=[any_space] * 6,
         out_shape=[
             jax.ShapeDtypeStruct((8 * share, 2 * width + rest), pack.dtype),
             jax.ShapeDtypeStruct((8 * share, 2 * narrow), pack.dtype),
+            jax.ShapeDtypeStruct((2 * share, 4 * ups.shape[2]), pack.dtype),
+            jax.ShapeDtypeStruct((2 * share, 4 * downs.shape[2]), pack.dtype),
             jax.ShapeDtypeStruct((rows, x_rows.shape[2]), x_rows.dtype),
             jax.ShapeDtypeStruct((2,) + small.shape, small.dtype),
         ],
-        scratch_shapes=[dma((1,)), dma((8,))] + [dma((10,))] * 9 + [dma((4,))] * 6,
+        scratch_shapes=[dma((1,)), dma((8,))] + [dma((10,))] * 9 + [dma((4,))] * 6 + [dma((2, 8))] * 2,
         compiler_params=pltpu.CompilerParams(collective_id=1, has_side_effects=True),
         name="spread",
-    )(pack, following, shared, x_rows, small)
+    )(pack, following, ups, downs, shared, x_rows, small)
+
+
+def collect_kernel(
+    grad_ref,
+    next_ref,
+    small_ref,
+    rows_ref,
+    one_ref,
+    shared_ref,
+    total_ref,
+    back_ref,
+    mamba_out,
+    attn_out,
+    in_ref,
+    next_in,
+    sum_ref,
+    next_sum,
+    piece_ref,
+    next_buf,
+    pair_ref,
+    mix_ref,
+    near_ref,
+    far_ref,
+    in_sem,
+    out_sem,
+    piece_sem,
+    piece_out,
+    pair_sem,
+    mix_sem,
+    mix_out,
+    near_sem,
+    near_out,
+    far_sem,
+    far_out,
+    row_sem,
+    row_out,
+):
+    plane = lax.axis_index("plane")
+    core = lax.axis_index("core")
+    place = lax.axis_index("tensor")
+    xside = plane + 1 - 2 * (plane % 2)
+    yside = plane + 2 - 4 * (plane // 2)
+    across = xside + 2 - 4 * (xside // 2)
+    share, width = one_ref.shape
+    rest = grad_ref.shape[1] - 2 * width
+
+    barrier = pltpu.get_barrier_semaphore()
+    for step in range(4):
+        for side in range(2):
+            if step or side:
+                pl.semaphore_signal(
+                    barrier,
+                    inc=1,
+                    device_id={"core": (core + side) % 2, "tensor": (place + step) % 4},
+                    device_id_type=MESH,
+                )
+    for neighbour in (xside, yside):
+        pl.semaphore_signal(
+            barrier, inc=1, device_id={"plane": neighbour}, device_id_type=MESH
+        )
+    pl.semaphore_wait(barrier, 9)
+
+    started = []
+
+    def send(src, dst, send_sem, recv_sem, device):
+        pltpu.make_async_remote_copy(
+            src_ref=src,
+            dst_ref=dst,
+            send_sem=send_sem,
+            recv_sem=recv_sem,
+            device_id=device,
+            device_id_type=MESH,
+        ).start()
+        started.append((src, send_sem))
+
+    narrow = next_ref.shape[1] // 2
+    spans = [(0, 2 * width, rest), (0, 0, width), (0, width, width)]
+    spans += [(1, 0, narrow), (1, narrow, narrow)]
+
+    def block(at, part, span):
+        rows = pl.ds(pl.multiple_of(at * 2 * share + part * share, share), share)
+        return (grad_ref, next_ref)[span[0]].at[rows, pl.ds(*span[1:])]
+
+    def held(slot, span):
+        return (in_ref, next_in)[span[0]].at[slot, :, pl.ds(*span[1:])]
+
+    def summed(part, span):
+        return (sum_ref, next_sum)[span[0]].at[part, :, pl.ds(*span[1:])]
+
+    def begin(number):
+        span = spans[number]
+        send(
+            block(across, 0, span),
+            held(0, span),
+            out_sem.at[0, number],
+            in_sem.at[0, number],
+            {"plane": xside},
+        )
+        send(
+            block(across, 1, span),
+            held(1, span),
+            out_sem.at[1, number],
+            in_sem.at[1, number],
+            {"plane": yside},
+        )
+        send(
+            block(xside, 0, span),
+            held(2, span),
+            out_sem.at[2, number],
+            in_sem.at[2, number],
+            {"plane": xside},
+        )
+        send(
+            block(yside, 1, span),
+            held(3, span),
+            out_sem.at[3, number],
+            in_sem.at[3, number],
+            {"plane": yside},
+        )
+
+    send(small_ref, near_ref.at[0], near_out.at[0], near_sem.at[0], {"plane": xside})
+    begin(0)
+    begin(1)
+
+    seq = place % 2
+    owner = place // 2
+    dst_rows = back_ref.at[seq, pl.ds(pl.multiple_of(core * share, share), share)]
+    for step in (2, 1, 3):
+        at = (place + step) % 4
+        send(
+            rows_ref.at[at],
+            dst_rows,
+            row_out.at[step],
+            row_sem.at[seq * 2 + core],
+            {"core": owner, "tensor": at},
+        )
+
+    @pl.when(owner == core)
+    def _():
+        pltpu.make_async_copy(rows_ref.at[place], dst_rows, row_sem.at[seq * 2 + core]).start()
+
+    @pl.when(owner != core)
+    def _():
+        pltpu.make_async_remote_copy(
+            src_ref=rows_ref.at[place],
+            dst_ref=dst_rows,
+            send_sem=row_out.at[0],
+            recv_sem=row_sem.at[seq * 2 + core],
+            device_id={"core": 1 - core},
+            device_id_type=MESH,
+        ).start()
+
+    def pass_on(number):
+        span = spans[number]
+        landed(held(0, span), in_sem.at[0, number])
+        held(0, span)[...] = low(wide(held(0, span)[...]) + wide(block(yside, 0, span)[...]))
+        send(
+            held(0, span),
+            held(5, span),
+            out_sem.at[4, number],
+            in_sem.at[5, number],
+            {"plane": yside},
+        )
+        landed(held(1, span), in_sem.at[1, number])
+        held(1, span)[...] = low(wide(held(1, span)[...]) + wide(block(xside, 1, span)[...]))
+        send(
+            held(1, span),
+            held(4, span),
+            out_sem.at[5, number],
+            in_sem.at[4, number],
+            {"plane": xside},
+        )
+
+    def finish(number):
+        span = spans[number]
+        landed(held(2, span), in_sem.at[2, number])
+        landed(held(5, span), in_sem.at[5, number])
+        summed(0, span)[...] = low(
+            wide(block(plane, 0, span)[...]) + wide(held(2, span)[...]) + wide(held(5, span)[...])
+        )
+        landed(held(3, span), in_sem.at[3, number])
+        landed(held(4, span), in_sem.at[4, number])
+        summed(1, span)[...] = low(
+            wide(block(plane, 1, span)[...]) + wide(held(3, span)[...]) + wide(held(4, span)[...])
+        )
+
+    def send_pieces(number):
+        span = spans[number]
+        kind, col = span[0], span[1] // span[2]
+        buf = (piece_ref, next_buf)[kind]
+        goal = 2 * core + col
+        for part in range(2):
+            src = summed(part, span)
+            here = jnp.logical_and(core == part, goal == place)
+
+            @pl.when(here)
+            def _():
+                pltpu.make_async_copy(src, buf.at[place], piece_sem.at[kind, place]).start()
+
+            @pl.when(jnp.logical_not(here))
+            def _():
+                pltpu.make_async_remote_copy(
+                    src_ref=src,
+                    dst_ref=buf.at[place],
+                    send_sem=piece_out.at[kind, 2 * col + part],
+                    recv_sem=piece_sem.at[kind, place],
+                    device_id={"core": part, "tensor": goal},
+                    device_id_type=MESH,
+                ).start()
+
+    rest_cols = pl.ds(2 * width, rest)
+    state = rest * 2 // 3
+    pass_on(0)
+    landed(near_ref.at[0], near_sem.at[0])
+    near_ref[3] = small_ref[...] + near_ref[0]
+    send(near_ref.at[3], near_ref.at[1], near_out.at[1], near_sem.at[1], {"plane": yside})
+    begin(2)
+    finish(0)
+    send(
+        sum_ref.at[1 - core, :, rest_cols],
+        pair_ref,
+        pair_sem.at[0],
+        pair_sem.at[1],
+        {"core": 1 - core},
+    )
+    pass_on(1)
+    begin(3)
+    landed(near_ref.at[1], near_sem.at[1])
+    near_ref[4] = near_ref[3] + near_ref[1]
+    send(near_ref.at[4], near_ref.at[2], near_out.at[2], near_sem.at[2], {"core": 1 - core})
+    landed(pair_ref, pair_sem.at[1])
+    mine = sum_ref[core, :, rest_cols]
+    mix_ref[place, :, 0:state] = low(wide(mine[:, :state]) + wide(pair_ref[:, :state]))
+    first = core == 0
+    mix_ref[place, :, state:rest] = jnp.where(first, mine[:, state:], pair_ref[:, state:])
+    mix_ref[place, :, rest:] = jnp.where(first, pair_ref[:, state:], mine[:, state:])
+    own_mix = mix_ref.at[place]
+    for step in (2, 1, 3):
+        send(
+            own_mix,
+            own_mix,
+            mix_out.at[step],
+            mix_sem.at[place],
+            {"tensor": (place + step) % 4},
+        )
+    finish(1)
+    send_pieces(1)
+    pass_on(2)
+    begin(4)
+    landed(near_ref.at[2], near_sem.at[2])
+    far_ref[place] = near_ref[4] + near_ref[2]
+    own_far = far_ref.at[place]
+    for step in (2, 1, 3):
+        send(
+            own_far,
+            own_far,
+            far_out.at[step],
+            far_sem.at[place],
+            {"tensor": (place + step) % 4},
+        )
+    finish(2)
+    send_pieces(2)
+    pass_on(3)
+    finish(3)
+    send_pieces(3)
+    pass_on(4)
+    finish(4)
+    send_pieces(4)
+
+    for step in (1, 2, 3):
+        at = (place + step) % 4
+        landed(mix_ref.at[at], mix_sem.at[at])
+        landed(far_ref.at[at], far_sem.at[at])
+    shared_ref[...] = (
+        wide(mix_ref[0]) + wide(mix_ref[1]) + wide(mix_ref[2]) + wide(mix_ref[3])
+    )
+    total_ref[...] = (far_ref[0] + far_ref[1]) + (far_ref[2] + far_ref[3])
+    def gathered(buf, kind):
+        for at in range(4):
+            landed(buf.at[at], piece_sem.at[kind, at])
+        return wide(buf[0]) + wide(buf[1]) + wide(buf[2]) + wide(buf[3])
+
+    one_ref[...] = gathered(piece_ref, 0)
+    both = gathered(next_buf, 1).T
+    mamba_out[...] = both[: mamba_out.shape[0]]
+    attn_out[...] = both[mamba_out.shape[0] :]
+    for at in range(4):
+        landed(dst_rows, row_sem.at[at])
+    for src, sem in started:
+        landed(src, sem)
+
+    @pl.when(owner != core)
+    def _():
+        landed(rows_ref.at[place], row_out.at[0])
+
+    for span in spans[1:]:
+        col = span[1] // span[2]
+        for part in range(2):
+            here = jnp.logical_and(core == part, 2 * core + col == place)
+
+            @pl.when(jnp.logical_not(here))
+            def _():
+                landed(summed(part, span), piece_out.at[span[0], 2 * col + part])
+
+
+def collect(grad, following, small, rows, width, mamba_cols):
+    share = grad.shape[0] // 8
+    rest = grad.shape[1] - 2 * width
+    narrow = following.shape[1] // 2
+    dma = pltpu.SemaphoreType.DMA
+    any_space = pl.BlockSpec(memory_space=pl.ANY)
+    near = pl.BlockSpec(memory_space=pltpu.VMEM)
+    model = rows.shape[2]
+    shared_cols = rest + rest // 3
+    bf16, f32 = jnp.bfloat16, jnp.float32
+    return pl.pallas_call(
+        collect_kernel,
+        in_specs=[near, near, near, any_space],
+        out_specs=[near, near, near, any_space, near, near],
+        out_shape=[
+            jax.ShapeDtypeStruct((share, width), f32),
+            jax.ShapeDtypeStruct((share, shared_cols), f32),
+            jax.ShapeDtypeStruct(small.shape, f32),
+            jax.ShapeDtypeStruct((2, 2 * rows.shape[1], model), rows.dtype),
+            jax.ShapeDtypeStruct((mamba_cols, share), f32),
+            jax.ShapeDtypeStruct((narrow - mamba_cols, share), f32),
+        ],
+        scratch_shapes=[
+            pltpu.VMEM((6, share, grad.shape[1]), bf16),
+            pltpu.VMEM((6, share, following.shape[1]), bf16),
+            pltpu.VMEM((2, share, grad.shape[1]), bf16),
+            pltpu.VMEM((2, share, following.shape[1]), bf16),
+            pltpu.VMEM((4, share, width), bf16),
+            pltpu.VMEM((4, share, narrow), bf16),
+            pltpu.VMEM((share, rest), bf16),
+            pltpu.VMEM((4, share, shared_cols), bf16),
+            pltpu.VMEM((5,) + small.shape, f32),
+            pltpu.VMEM((4,) + small.shape, f32),
+            dma((6, 5)),
+            dma((6, 5)),
+            dma((2, 4)),
+            dma((2, 4)),
+            dma((2,)),
+            dma((4,)),
+            dma((4,)),
+            dma((3,)),
+            dma((3,)),
+            dma((4,)),
+            dma((4,)),
+            dma((4,)),
+            dma((4,)),
+        ],
+        compiler_params=pltpu.CompilerParams(
+            collective_id=2, has_side_effects=True, vmem_limit_bytes=BIG
+        ),
+        name="collect",
+    )(grad, following, small, rows)
 
 
 def rms_norm(values, gain_vec):
@@ -901,9 +1302,41 @@
 
 
 def swiglu(gate_up):
-    half_cols = gate_up.shape[1] // 2
-    gate = gate_up[:, :half_cols]
-    return gate * sigmoid(gate) * gate_up[:, half_cols:]
+    rows, columns = gate_up.shape
+    units = columns // 8
+    parts = []
+    for at in range(0, columns, 2 * units):
+        gate, up = gate_up[:, at : at + units], gate_up[:, at + units : at + 2 * units]
+        parts.append(gate * sigmoid(gate) * up)
+    return jnp.concatenate(parts, axis=1)
+
+
+def pairs_split(step):
+    return [
+        (core * 4 + place, (goal // 2) * 4 + 2 * core + goal % 2)
+        for core in range(2)
+        for place in range(4)
+        for goal in [(place + step) % 4]
+    ]
+
+
+def pairs_join(step):
+    return [
+        (core * 4 + place, (place // 2) * 4 + (2 * core + place % 2 + step) % 4)
+        for core in range(2)
+        for place in range(4)
+    ]
+
+
+def exchange(piece_at, mine, yours, pairs):
+    moved = [
+        lax.ppermute(piece_at((mine + step) % 4), ("core", "tensor"), pairs(step))
+        for step in range(4)
+    ]
+    stacked = jnp.stack(moved)
+    return [
+        lax.dynamic_index_in_dim(stacked, (yours - source) % 4, 0, False) for source in range(4)
+    ]
 
 
 def swapped(values):
@@ -963,12 +1396,15 @@
     def flat(values):
         return values.transpose(1, 0, 2).reshape(values.shape[1], -1)
 
+    spot = 2 * core + place % 2
+
     def positions_in(values):
         shaped = values.reshape(seq_dev, 2, half_rows, model_dim)
         keep = lax.dynamic_index_in_dim(shaped, core, 1, False)
         send = lax.dynamic_index_in_dim(shaped, 1 - core, 1, False)
-        four = in_order(keep, swapped(send), 0)
-        own = lax.all_to_all(four, "tensor", 0, 0, tiled=True)
+        return lax.all_to_all(in_order(keep, swapped(send), 0), "tensor", 0, 0, tiled=True)
+
+    def both_halves(own):
         both = in_order(own[:, None], swapped(own)[:, None], 1)
         return both.reshape(seq_total, model_dim)
 
@@ -987,6 +1423,12 @@
         shaped = values.reshape(groups, 2, half_rows, -1)
         return lax.dynamic_index_in_dim(shaped, 1 - core, 1, False)
 
+    out_dev = chans_dev + query_dev
+    pack_two = jnp.concatenate([mamba_proj.T, attn_proj.T], axis=1)
+    own_units = hidden_dev // 2
+    pack_ups = ffn_weight.reshape(share, 2, 2, own_units).transpose(2, 0, 1, 3)
+    pack_ups = pack_ups.reshape(2, share, hidden_dev)
+    pack_downs = ffn_down.reshape(2, own_units, share).transpose(0, 2, 1)
     out_dev = chans_dev + query_dev
     pack_two = jnp.concatenate([mamba_proj.T, attn_proj.T], axis=1)
     pack_one = jnp.concatenate(
@@ -1013,13 +1455,15 @@
     )
     small_pad = -(-small_in.shape[0] // 1024) * 1024
     small_in = jnp.pad(small_in, (0, small_pad - small_in.shape[0])).reshape(-1, 128)
-    if lax.axis_size("plane") == 4 and groups == 4 and share % 16 == 0:
+    quad = lax.axis_size("plane") == 4 and groups == 4 and share % 16 == 0
+    quad = quad and share == half_rows
+    if quad:
         shared = jnp.stack([shared_for(0), shared_for(1)])
-        weight_one, weight_two, x_low, small_mine = spread(
-            pack_one, pack_two, shared, layer_in, small_in
+        weight_one, weight_two, rows_up, rows_down, x_low, small_mine = spread(
+            pack_one, pack_two, pack_ups, pack_downs, shared, layer_in, small_in
         )
     else:
-        x_low = positions_in(layer_in)
+        x_low = both_halves(positions_in(layer_in))
         all_one = lax.all_gather(pack_one, "tensor", axis=0)
         own_one = jnp.concatenate([flat(mine(all_one)), shared_for(core)], axis=1)
         their_one = jnp.concatenate([flat(other(all_one)), shared_for(1 - core)], axis=1)
@@ -1033,21 +1477,22 @@
             axis=0,
             tiled=True,
         )
+        rows_up, rows_down = (
+            in_order(
+                lax.dynamic_index_in_dim(pack, core, 0, False),
+                swapped(lax.dynamic_index_in_dim(pack, 1 - core, 0, False)),
+                0,
+            )
+            for pack in (pack_ups, pack_downs)
+        )
+        rows_up, rows_down = (
+            lax.all_gather(rows, "tensor", axis=1, tiled=True) for rows in (rows_up, rows_down)
+        )
         small_mine = mine(lax.all_gather(small_in, "tensor", axis=0))
     small_mine = small_mine.reshape(held, -1)
 
-    pack_three = jnp.concatenate([ffn_weight.reshape(share, 2 * hidden_dev), ffn_down.T], axis=1)
-    all_three = lax.all_gather(pack_three, "tensor", axis=0)
-    all_three, weight_one = lax.optimization_barrier((all_three, weight_one))
-
-    def lay_three(pack):
-        cuts = [pack[:, :, at * hidden_dev : (at + 1) * hidden_dev] for at in range(3)]
-        return jnp.concatenate([flat(cut) for cut in cuts], axis=1)
-
-    rows_three = in_order(lay_three(mine(all_three)), swapped(lay_three(other(all_three))), 0)
-    weight_three = lax.all_gather(rows_three, "plane", axis=0, tiled=True)
-    gate_up_weight = weight_three[:, : 2 * held * hidden_dev]
-    down_weight = weight_three[:, 2 * held * hidden_dev :]
+    gate_up_weight = lax.all_gather(rows_up, "plane", axis=0, tiled=True)
+    down_weight = lax.all_gather(rows_down, "plane", axis=0, tiled=True)
 
     cuts = []
     at = 0
@@ -1074,6 +1519,8 @@
     attn, log_sums = attention_forward(len_one, proj, cosine, sine, group_cols)
     both_low, state_out, states = mamba_forward(proj, attn, taps, bias, decay, skip, gain)
 
+    grad_own = positions_in(lax.optimization_barrier((out_grad, proj))[0])
+    grad_own, both_low = lax.optimization_barrier((grad_own, both_low))
     mixed_part = low(dot_nt(both_low, weight_two))
     mixed = wide(mixed_part) + wide(swapped(mixed_part))
     hidden = x_rows + mixed
@@ -1086,54 +1533,52 @@
     out_own = own_half(valid_rows) * (own_half(hidden) + ffn_own)
     layer_out = positions_out(low(out_own))
 
-    grad_rows = valid_rows * wide(positions_in(out_grad))
+    grad_rows = valid_rows * wide(both_halves(grad_own))
     grad_low = low(grad_rows)
     grad_down = low(dot_tn(grad_low, act_low))
     (grad_gate_up,) = act_pull(dot(grad_low, down_weight))
     gate_up_low = low(grad_gate_up)
     grad_gate_up_weight = low(dot_tn(normed_two, gate_up_low))
     grad_two_part = low(dot_nt(gate_up_low, gate_up_weight))
-    grad_two = wide(grad_two_part) + wide(swapped(grad_two_part))
+    grad_n2 = wide(grad_two_part) + wide(swapped(grad_two_part))
     r_two = lax.rsqrt(jnp.mean(hidden * hidden, axis=-1, keepdims=True) + EPS)
-    scaled = grad_two * ffn_gain
+    scaled = grad_n2 * ffn_gain
     grad_hidden = (
         grad_rows
         + r_two * scaled
         - hidden * (r_two**3 * jnp.mean(hidden * scaled, axis=-1, keepdims=True))
     )
-    grad_ffn_gain = jnp.sum(own_half(hidden * r_two * grad_two), axis=(0, 1))
+    grad_ffn_gain = jnp.sum(own_half(hidden * r_two * grad_n2), axis=(0, 1))
     grad_mixed = low(grad_hidden)
 
     def scatter(values):
-        part = lax.psum_scatter(values, "plane", scatter_dimension=0, tiled=True)
-        part = part.reshape(2, share, -1)
-        return (
-            lax.dynamic_index_in_dim(part, core, 0, False),
-            lax.dynamic_index_in_dim(part, 1 - core, 0, False),
-        )
-
-    def by_group(values, widths):
-        pieces = []
-        at = 0
-        for width in widths:
-            piece = values[:, at : at + held * width]
-            pieces.append(piece.reshape(share, held, width).transpose(1, 0, 2))
-            at += held * width
-        return jnp.concatenate(pieces, axis=2)
-
-    def to_groups(own, theirs):
-        whole = in_order(own, theirs, 0)
-        return lax.psum_scatter(whole, "tensor", scatter_dimension=0, tiled=True)[0]
-
-    def sum_rest(parts, widths):
-        both = [scatter(part) for part in parts]
-        own = by_group(jnp.concatenate([pair[0] for pair in both], axis=1), widths)
-        theirs = by_group(jnp.concatenate([pair[1] for pair in both], axis=1), widths)
-        return to_groups(own, swapped(theirs))
-
-    sum_three = sum_rest((grad_gate_up_weight, grad_down), (hidden_dev,) * 3)
-    grad_both = low(dot_tn(grad_mixed, both_low))
-    sum_two = sum_rest((grad_both,), (out_dev,))
+        return lax.psum_scatter(values, "plane", scatter_dimension=0, tiled=True)
+
+    def to_groups(values):
+        rows, columns = values.shape
+
+        def piece_at(goal):
+            return lax.dynamic_slice(
+                values,
+                ((goal // 2) * (rows // 2), (goal % 2) * (columns // 2)),
+                (rows // 2, columns // 2),
+            )
+
+        parts = exchange(piece_at, place, spot, pairs_split)
+        return wide(parts[0]) + wide(parts[1]) + wide(parts[2]) + wide(parts[3])
+
+    def to_units(values):
+        part = lax.psum_scatter(values, "tensor", scatter_dimension=1, tiled=True)
+        by_part = part.reshape(2, share, -1)
+        own = lax.dynamic_index_in_dim(by_part, core, 0, False)
+        theirs = swapped(lax.dynamic_index_in_dim(by_part, 1 - core, 0, False))
+        return wide(in_order(own[None], theirs[None], 0))
+
+    units_down = to_units(scatter(grad_down))
+    units_up = to_units(scatter(grad_gate_up_weight))
+    sum_down = units_down.transpose(0, 2, 1).reshape(hidden_dev, share)
+    sum_up = units_up.reshape(2, share, 2, own_units).transpose(1, 2, 0, 3)
+    grad_two = low(dot_tn(grad_mixed, both_low))
 
     back = dot(grad_mixed, weight_two)
     attn_back = jnp.concatenate(
@@ -1146,32 +1591,18 @@
         proj, state_out, states, back, grad_q, grad_kv, taps, bias, decay, skip, gain
     )
     grad_one = low(dot_tn(normed, proj_grad))
-    own_grad, their_grad = scatter(grad_one)
-    their_grad = swapped(their_grad)
     edge = held * group_cols
-    shared_own = wide(own_grad[:, edge : edge + 2 * N]) + wide(their_grad[:, edge : edge + 2 * N])
-    kv_both = in_order(
-        own_grad[:, None, edge + 2 * N :], their_grad[:, None, edge + 2 * N :], 1
-    )
-    kv_both = kv_both.reshape(share, 2, 2, HEAD_SIZE).transpose(0, 2, 1, 3)
-    shared_low = jnp.concatenate([low(shared_own), kv_both.reshape(share, -1)], axis=1)
-    shared_sum = jnp.sum(wide(lax.all_gather(shared_low, "tensor", axis=0)), axis=0)
-    sum_one = to_groups(
-        by_group(own_grad[:, :edge], (group_cols,)), by_group(their_grad[:, :edge], (group_cols,))
-    )
-
     grad_norm_part = low(dot_nt(proj_grad, weight_one))
     grad_norm_own = wide(own_half(grad_norm_part)) + wide(swapped(other_half(grad_norm_part)))
     x_own = wide(own_half(x_low))
     r_one = lax.rsqrt(jnp.mean(x_own * x_own, axis=-1, keepdims=True) + EPS)
     scaled = grad_norm_own * norm_gain
-    grad_x = (
+    grad_x = low(
         own_half(grad_hidden)
         + r_one * scaled
         - x_own * (r_one**3 * jnp.mean(x_own * scaled, axis=-1, keepdims=True))
     )
     grad_norm_gain = jnp.sum(x_own * r_one * grad_norm_own, axis=(0, 1))
-    input_grad = positions_out(low(grad_x))
 
     grad_skip = jnp.sum(grad_skip_cols.reshape(held, heads_dev, HEAD_SIZE), axis=-1)
     chan_taps = grad_taps[:, : held * chans_dev].reshape(KCONV, held, chans_dev)
@@ -1194,7 +1625,33 @@
             small_groups.reshape(-1),
         ]
     )
-    small_sum = lax.psum(small_out, ("plane", "core", "tensor"))
+    if quad:
+        small_size = small_out.shape[0]
+        small_room = -(-small_size // 1024) * 1024
+        sum_one, shared_sum, small_sum, input_grad, sum_mamba, sum_attn = collect(
+            grad_one,
+            grad_two,
+            jnp.pad(small_out, (0, small_room - small_size)).reshape(-1, 128),
+            grad_x,
+            group_cols,
+            chans_dev,
+        )
+        small_sum = small_sum.reshape(-1)[:small_size]
+    else:
+        part_one = scatter(grad_one)
+        both_parts = part_one[:, edge:].reshape(2, share, -1)
+        own_rest = lax.dynamic_index_in_dim(both_parts, core, 0, False)
+        their_rest = swapped(lax.dynamic_index_in_dim(both_parts, 1 - core, 0, False))
+        shared_own = wide(own_rest[:, : 2 * N]) + wide(their_rest[:, : 2 * N])
+        kv_both = in_order(own_rest[:, 2 * N :], their_rest[:, 2 * N :], 1)
+        shared_low = jnp.concatenate([low(shared_own), kv_both], axis=1)
+        shared_sum = jnp.sum(wide(lax.all_gather(shared_low, "tensor", axis=0)), axis=0)
+        sum_one = to_groups(part_one[:, :edge])
+        sum_two = to_groups(scatter(grad_two)).T
+        sum_mamba, sum_attn = sum_two[:chans_dev], sum_two[chans_dev:]
+        input_grad = positions_out(grad_x)
+        small_sum = lax.psum(small_out, ("plane", "core", "tensor"))
+    kv_sum = shared_sum[:, 2 * N :].reshape(share, 2, 2, HEAD_SIZE).transpose(0, 2, 1, 3)
     group_sum = lax.dynamic_index_in_dim(
         small_sum[2 * model_dim + KCONV * 2 * N :].reshape(groups, -1), place, 0, False
     )
@@ -1204,7 +1661,7 @@
         pieces.append(group_sum[at : at + size])
         at += size
 
-    one, two, three = wide(sum_one), wide(sum_two), wide(sum_three)
+    one = sum_one
     return (
         layer_out,
         input_grad,
@@ -1213,18 +1670,18 @@
         one[:, 2 * chans_dev + query_dev :][:, :heads_dev],
         shared_sum[:, : 2 * N].reshape(share, 2, N),
         one[:, 2 * chans_dev : 2 * chans_dev + query_dev],
-        shared_sum[:, 2 * N :].reshape(share, 2, 2 * HEAD_SIZE),
+        kv_sum.reshape(share, 2, 2 * HEAD_SIZE),
         pieces[0].reshape(KCONV, chans_dev),
         small_sum[2 * model_dim : 2 * model_dim + KCONV * 2 * N].reshape(KCONV, 2, N),
         pieces[1],
         pieces[2],
         pieces[3],
         pieces[4],
-        two[:, :chans_dev].T,
-        two[:, chans_dev:].T,
+        sum_mamba,
+        sum_attn,
         small_sum[model_dim : 2 * model_dim],
-        three[:, : 2 * hidden_dev].reshape(share, 2, hidden_dev),
-        three[:, 2 * hidden_dev :].T,
+        sum_up.reshape(share, 2, hidden_dev),
+        sum_down,
     )
 
 

time: 549 us -> 508 us (0.925)
  Pallas kernels: 178 us -> 266 us
  blocking collectives: 63.9 us -> 0 us
  local copies, waits for them, and re-layouts: 66.6 us -> 46.2 us
  starting transfers between devices: 30.9 us -> 12.6 us
  waiting for transfers between devices: 35.6 us -> 17.8 us
    pallas_call x1 -> x2, Pallas kernels: 98.1 us -> 186 us  [the longest x1 96.5 us: spread(): pl.pallas_call(spread_kernel, in_specs=[any_space] * 7, out_specs=[any_sp...]
    psum x1 -> x0, blocking collectives: 39.1 us -> none  [body(): small_sum = lax.psum(small_out, ('plane', 'core', 'tensor'))]
    all_gather x1 -> x0, blocking collectives: 24.8 us -> none  [body(): lax.all_gather(shared_low, 'tensor', axis=0)]
    all_to_all x2 -> x1, waiting for transfers between devices: 20.8 us -> 0.01 us  [positions_out(): four = lax.all_to_all(own, 'tensor', 0, 0, tiled=True)]
    select_n x9 -> x5, other arithmetic: 19.1 us -> 2.95 us  [in_order(): jnp.where(first, jnp.concatenate([own, others], axis=axis), jnp.concatena...]
    all_gather x2, waiting for transfers between devices: 0.02 us -> 13.9 us  [the longest x1 13.9 us: body(): gate_up_weight = lax.all_gather(rows_up, 'plane', axis=0, tiled=True)]
    mul x1 -> x3, other arithmetic: 3.65 us -> 16.1 us  [the longest x2 11 us: swiglu(): parts.append(gate * sigmoid(gate) * up)]
    dynamic_slice x10 -> x3, local copies, waits for them, and re-layouts: 12 us -> 1.98 us  [the longest x2 1.87 us: to_units(): own = lax.dynamic_index_in_dim(by_part, core, 0, False)]
  transfers between devices with their start and end apart: 25 -> 18, of which waited for: 6 -> 3; matrix products, arithmetic and copies ran while one was open for 33% -> 30% of each run, Pallas kernels for 33% -> 34%
where the time goes in v3:
time: 508 us; the launch traced here: 501 us
  Pallas kernels  266 us (52%)
  matrix products  87.6 us (17%)
  other arithmetic  55.8 us (11%)
  local copies, waits for them, and re-layouts  46.2 us (9%)
  waiting for transfers between devices  17.8 us (4%)
  between operations  15 us (3%)
  starting transfers between devices  12.6 us (2%)
    pallas_call x1, Pallas kernels, spread(): pl.pallas_call(spread_kernel, in_specs=[any_space] * 7, out_specs=[any_sp...  96.5 us
    pallas_call x1, Pallas kernels, collect(): pl.pallas_call(collect_kernel, in_specs=[near, near, near, any_space], ou...  89.1 us
    pallas_call x1, Pallas kernels, mamba_backward(): pl.pallas_call(mamba_backward_kernel, grid=(chunks,), in_specs=[rows_of(c...  36.3 us
    dot_general x4, matrix products, dot(): return jnp.dot(left, right, preferred_element_type=jnp.float32)  30.9 us
    dot_general x4, matrix products, dot_tn(): lax.dot_general(left, right, (((0,), (0,)), ((), ())), preferred_element_...  29.6 us
    dot_general x4, matrix products, dot_nt(): lax.dot_general(left, right, (((1,), (1,)), ((), ())), preferred_element_...  27.1 us
    pallas_call x1, Pallas kernels, attention_backward(): pl.pallas_call(attention_backward_kernel, grid=(2,), in_specs=attention_s...  18.1 us
    unnamed x93, local copies, waits for them, and re-layouts  16.4 us
  transfers between devices with their start and end apart: 18, of which 3 were waited for; matrix products, arithmetic and copies ran while one was open for 30% of the time, Pallas kernels for 34%

profile of v3, /device:TPU:0, one launch (start us, length us, event | category | flops | bytes accessed | tf_op | source)
XLA Modules:
  0.0 500.9 jit_solution(3522196941945427803)
XLA Ops:
  21.7 96.5 %spread.1 = (bf16[1024,2432]{1,0:T(8,128)(2,1)}, bf16[1024,1024]{1,0:T(8,128)(2,1)}, bf16[256,2048]{1,0:T(8,128)(2,1)}, bf16[256,1024]{1,0:T(8,128)(2,1)}, bf16[...) custom-call(bf16[128,1024]{1,0:T(8,128)(2,1)} %fusion.37.pack_ref, bf16[128,512]{1,0:T(8,128)(2,1)} %pad_maximum_fusion.7.next_ref, ...), custom_call_target="tpu_custom_call" | custom-call | tf_op jit(solution)/shard_map/spread/pallas_call | solution.py:914
  121.0 11.2 %fusion.34.q_ref.kv_ref.proj_ref.before_ref = f32[1024,2432]{1,0:T(8,128)} fusion(bf16[1024,2432]{1,0:T(8,128)(2,1)} %get-tuple-element.48, bf16[1024,1024]{1,0:T(8,128)(2,1)} %get-tuple-element.47, f32[1024]{0:T(1024)S(1)} %copy-done.24, f32[1024]{0:T(1024)S(1)} %add_rsqrt_fusion.1), kind=kOutput, calls=%fused_computation.80 | convolution fusion | flops 5104467968 | bytes 17047552 | tf_op jit(solution)/shard_map/dot_general | solution.py:28
  135.5 4.2 all-to-all-start
  146.6 11.4 %attention_forward.1 = (bf16[1024,256]{1,0:T(8,128)(2,1)}, f32[1024,256]{1,0:T(8,128)}) custom-call(s32[1]{0:T(128)} %dynamic_slice.71.len_ref, f32[1024,2432]{1,0:T(8,128)} %fusion.34.q_ref.kv_ref.proj_ref.before_ref, f32[1024,2432]{1,0:T(8,128)} %fusion.34.q_ref.kv_ref.proj_ref.before_ref, f32[1024,128]{1,0:T(8,128)} %copy.85.cos_ref, ...), custom_call_target="tpu_custom_call" | custom-call | tf_op jit(solution)/shard_map/attention_forward/pallas_call | solution.py:181
  157.9 14.6 %mamba_forward.1 = (bf16[1024,1024]{1,0:T(8,128)(2,1)}, f32[1024,768]{1,0:T(8,128)}, f32[8,128,768]{2,1,0:T(8,128)}) custom-call(f32[1024,2432]{1,0:T(8,128)} %fusion.34.q_ref.kv_ref.proj_ref.before_ref, bf16[1024,256]{1,0:T(8,128)(2,1)} %get-tuple-element.50.attn_ref, f32[4,1024]{1,0:T(4,128)} %pad_maximum_fusion.10.taps_ref, f32[2,128]{1,0:T(2,128)} %pad.47.bias_ref, ...), custom_call_target="tpu_custom_call" | custom-call | tf_op jit(solution)/shard_map/mamba_forward/pallas_call | solution.py:356
  173.1 5.3 %convolution_convert_fusion.7 = bf16[1024,1024]{1,0:T(8,128)(2,1)} fusion(bf16[1024,1024]{1,0:T(8,128)(2,1)} %get-tuple-element.53, bf16[1024,1024]{1,0:T(8,128)(2,1)S(1)} %copy-done.34), kind=kOutput, calls=%fused_computation.44 | convolution fusion | flops 2148532224 | bytes 6291456 | tf_op jit(solution)/shard_map/dot_general | solution.py:32
  182.5 7.4 %fusion.57 = f32[1024,1024]{1,0:T(8,128)} fusion(bf16[1024,1024]{1,0:T(8,128)(2,1)} %fusion.4, bf16[1024,1024]{1,0:T(8,128)(2,1)} %all-gather.5.cloned.1.call-done), kind=kOutput, calls=%fused_computation.155 | convolution fusion | flops 2147483648 | bytes 8388608 | tf_op jit(solution)/shard_map/dot_general | solution.py:28
  189.9 5.1 %multiply_reduce_fusion.1 = (f32[1024]{0:T(1024)S(1)}, f32[1024,1024]{1,0:T(8,128)}) fusion(bf16[1024,1024]{1,0:T(8,128)(2,1)} %collective-permute-done.2, bf16[1024,1024]{1,0:T(8,128)(2,1)} %convolution_convert_fusion.7, bf16[1024,1024]{1,0:T(8,128)(2,1)S(1)} %copy-done.3), kind=kLoop, calls=%fused_computation.15 | loop fusion | flops 7339008 | bytes 10489856 | tf_op jit(solution)/shard_map/reduce_sum | solution.py:1290
  195.1 13.9 %all-gather.3.cloned.1.call-done = bf16[1024,2048]{1,0:T(8,128)(2,1)} async-done(((bf16[256,2048]{1,0:T(8,128)(2,1)}), bf16[1024,2048]{1,0:T(8,128)(2,1)}) %all-gather.3.cloned.1.call-update) | async-done | bytes 4194320 | tf_op jit(solution)/shard_map/all_gather | solution.py:1494
  208.9 8.0 %fusion.51 = f32[1024,2048]{1,0:T(8,128)S(1)} fusion(bf16[1024,2048]{1,0:T(8,128)(2,1)} %all-gather.3.cloned.1.call-done, f32[1024,1024]{1,0:T(8,128)} %get-tuple-element.135, f32[1024]{0:T(1024)S(1)} %copy-done.27, f32[1024]{0:T(1024)S(1)} %add_rsqrt_fusion), kind=kOutput, calls=%fused_computation.149 | convolution fusion | flops 4298113024 | bytes 16785408 | tf_op jit(solution)/shard_map/dot_general | solution.py:28
  226.1 7.4 %slice_multiply_fusion.3 = (f32[1024,256]{1,0:T(8,128)S(1)}, f32[1024,256]{1,0:T(8,128)S(1)}, f32[1024,256]{1,0:T(8,128)}, f32[1024,256]{1,0:T(8,128)}, f32[1024...) fusion(f32[1024,1024]{1,0:T(8,128)} %fusion.57, f32[1024,2048]{1,0:T(8,128)} %copy-done.2), kind=kLoop, calls=%fused_computation.79 | loop fusion | flops 15204352 | bytes 19922944 | tf_op jit(solution)/shard_map/transpose(jvp())/mul | solution.py:1310
  233.5 5.8 %add_convert_fusion = bf16[1024,2048]{1,0:T(8,128)(2,1)} fusion(f32[1024,256]{1,0:T(8,128)} %get-tuple-element.140, f32[1024,256]{1,0:T(8,128)} %get-tuple-element.141, f32[1024,256]{1,0:T(8,128)} %get-tuple-element.139, f32[1024,256]{1,0:T(8,128)} %get-tuple-element.142, f32[1024,256]{1,0:T(8,128)} %get-tuple-element.138, ...), kind=kLoop, calls=%fused_computation | loop fusion | flops 16777216 | bytes 12582912 | tf_op jit(solution)/shard_map/convert_element_type | solution.py:20
  239.4 8.8 %convolution_convert_fusion.1 = bf16[1024,2048]{1,0:T(8,128)(2,1)} fusion(bf16[1024,2048]{1,0:T(8,128)(2,1)} %add_convert_fusion, f32[1024,1024]{1,0:T(8,128)S(1)} %copy-done, f32[1024]{0:T(1024)S(1)} %copy-done.27, f32[1024]{0:T(1024)S(1)} %add_rsqrt_fusion), kind=kOutput, calls=%fused_computation.18 | convolution fusion | flops 4300210176 | bytes 12591104 | tf_op jit(solution)/shard_map/dot_general | solution.py:38
  248.2 9.4 %convolution_convert_fusion.5 = bf16[1024,1024]{1,0:T(8,128)(2,1)} fusion(bf16[1024,2048]{1,0:T(8,128)(2,1)} %add_convert_fusion, bf16[1024,2048]{1,0:T(8,128)(2,1)} %all-gather.3.cloned.1.call-done), kind=kOutput, calls=%fused_computation.42 | convolution fusion | flops 4296015872 | bytes 10485760 | tf_op jit(solution)/shard_map/dot_general | solution.py:32
  268.6 4.6 all-to-all-start.1
  273.2 4.5 multiply_reduce_fusion
  278.8 5.1 %fusion.6 = (f32[1024,1024]{1,0:T(8,128)}, f32[1024,1024]{1,0:T(8,128)S(1)}) fusion(bf16[1024,1024]{1,0:T(8,128)(2,1)} %collective-permute-done.6, bf16[1024,1024]{1,0:T(8,128)(2,1)} %convolution_convert_fusion.5, f32[1024,1024]{1,0:T(8,128)S(1)} %copy-done.1, f32[1024]{0:T(1024)S(1)} %add_rsqrt_fusion, f32[1024]{0:T(1024)S(1)} %fusion.44, ...), kind=kLoop, calls=%fused_computation.16 | loop fusion | flops 12582912 | bytes 18890752 | tf_op jit(solution)/shard_map/mul | solution.py:1551
  283.9 4.3 fusion.56
  289.2 18.1 %attention_backward.1 = (bf16[1024,256]{1,0:T(8,128)(2,1)}, bf16[1024,128]{1,0:T(8,128)(2,1)}) custom-call(s32[1]{0:T(128)} %dynamic_slice.71.len_ref, f32[1024,2432]{1,0:T(8,128)} %fusion.34.q_ref.kv_ref.proj_ref.before_ref, f32[1024,2432]{1,0:T(8,128)} %fusion.34.q_ref.kv_ref.proj_ref.before_ref, f32[1024,128]{1,0:T(8,128)} %copy.85.cos_ref, ...), custom_call_target="tpu_custom_call" | custom-call | tf_op jit(solution)/shard_map/attention_backward/pallas_call | solution.py:198
  307.3 36.3 %mamba_backward.1 = (bf16[1024,2432]{1,0:T(8,128)(2,1)}, f32[4,1024]{1,0:T(4,128)}, f32[1,768]{1,0:T(1,128)}, f32[1,768]{1,0:T(1,128)}, f32[2,128]{1,0:T(2,128)}, /*index=5*/f32[2,128]{1,0:T(2,128)}) custom-call(f32[1024,2432]{1,0:T(8,128)} %fusion.34.q_ref.kv_ref.proj_ref.before_ref, f32[1024,2432]{1,0:T(8,128)} %fusion.34.q_ref.kv_ref.proj_ref.before_ref, ...), custom_call_target="tpu_custom_call" | custom-call | tf_op jit(solution)/shard_map/mamba_backward/pallas_call | solution.py:569
  343.6 10.0 %convolution_convert_fusion.3 = bf16[1024,1024]{1,0:T(8,128)(2,1)} fusion(bf16[1024,2432]{1,0:T(8,128)(2,1)} %get-tuple-element.63, bf16[1024,2432]{1,0:T(8,128)(2,1)} %get-tuple-element.48), kind=kOutput, calls=%fused_computation.40 | convolution fusion | flops 5101322240 | bytes 12058624 | tf_op jit(solution)/shard_map/dot_general | solution.py:32
  353.7 10.4 %convolution_convert_fusion.grad_ref = bf16[1024,2432]{1,0:T(8,128)(2,1)} fusion(bf16[1024,2432]{1,0:T(8,128)(2,1)} %get-tuple-element.63, bf16[1024,1024]{1,0:T(8,128)(2,1)S(1)} %copy-done.3, f32[1024]{0:T(1024)S(1)} %copy-done.24, f32[1024]{0:T(1024)S(1)} %add_rsqrt_fusion.1), kind=kOutput, calls=%fused_computation.4 | convolution fusion | flops 5106958336 | bytes 12066816 | tf_op jit(solution)/shard_map/dot_general | solution.py:38
  368.0 6.7 %convolution_convert_fusion.4.next_ref = bf16[1024,1024]{1,0:T(8,128)(2,1)} fusion(bf16[1024,1024]{1,0:T(8,128)(2,1)} %get-tuple-element.53, f32[1024,1024]{1,0:T(8,128)} %copy-done.6), kind=kOutput, calls=%fused_computation.41 | convolution fusion | flops 2149580800 | bytes 8388608 | tf_op jit(solution)/shard_map/dot_general | solution.py:38
  382.7 89.1 %collect.1 = (f32[128,1024]{1,0:T(8,128)}, f32[128,512]{1,0:T(8,128)}, f32[88,128]{1,0:T(8,128)}, bf16[2,256,1024]{2,1,0:T(8,128)(2,1)}, f32[384,128]{1,0:T(8,128)}, /*index=5*/f32[128,128]{1,0:T(8,128)}) custom-call(bf16[1024,2432]{1,0:T(8,128)(2,1)} %convolution_convert_fusion.grad_ref, bf16[1024,1024]{1,0:T(8,128)(2,1)} %convolution_convert_fusion.4.next_ref, ...), custom_call_target="tpu_custom_call" | custom-call | tf_op jit(solution)/shard_map/collect/pallas_call | solution.py:1245
  (223 shorter events, 87.9 us)
Async XLA Ops:
  7.2 175.3 %all-gather.5.cloned.1.call-start = ((), (), s32[]{:S(2)}) async-start(), calls=%async_computation.7 | async-start | bytes 2621440 | tf_op jit(solution)/shard_map/all_gather | solution.py:1495
  11.3 109.7 %copy-start.24 = (f32[1024]{0:T(1024)S(1)}, f32[1024]{0:T(1024)}, u32[]{:S(2)}) copy-start(f32[1024]{0:T(1024)} %param.23) | copy-start | bytes 12292
  118.2 90.7 %all-gather.3.cloned.1.call-start = ((), (), s32[]{:S(2)}) async-start(), calls=%async_computation.6 | async-start | bytes 5242880 | tf_op jit(solution)/shard_map/all_gather | solution.py:1494
  132.3 2.1 collective-permute-start.1
  135.5 37.0 %all-to-all-start = ((bf16[4,128,1024]{2,1,0:T(8,128)(2,1)}), bf16[4,128,1024]{2,1,0:T(8,128)(2,1)S(1)}, u32[]{:S(2)}, u32[]{:S(2)}) async-start(bf16[4,128,1024]{2,1,0:T(8,128)(2,1)} %maximum_select_fusion.1), calls=%async_computation | async-start | bytes 2097152 | tf_op jit(solution)/shard_map/all_to_all | solution.py:1405
  139.7 213.9 %reduce-scatter.9.cloned.1.call-start = ((), (), s32[]{:S(2)}) async-start(), calls=%async_computation.10 | async-start | bytes 2621440 | tf_op jit(solution)/shard_map/reduce_scatter | solution.py:1555
  139.7 6.2 %collective-permute-start = (s32[2]{0:T(128)S(1)}, s32[2]{0:T(128)S(1)}, u32[]{:S(2)}, u32[]{:S(2)}) collective-permute-start(s32[2]{0:T(128)S(1)} %copy-done.33), channel_id=1, source_target_pairs={{0,4},{4,0},{1,5},{5,1},{2,6},{6,2},{3,7},{7,3},{8,12},{12,8},{9,1... | collective-permute-start | bytes 32 | tf_op jit(solution)/shard_map/ppermute | solution.py:1343
  157.9 15.1 %copy-start.34 = (bf16[1024,1024]{1,0:T(8,128)(2,1)S(1)}, bf16[1024,1024]{1,0:T(8,128)(2,1)}, u32[]{:S(2)}) copy-start(bf16[1024,1024]{1,0:T(8,128)(2,1)} %get-tuple-element.54) | copy-start | bytes 6291460
  172.6 6.5 %collective-permute-start.5 = (bf16[4,128,1024]{2,1,0:T(8,128)(2,1)S(1)}, bf16[4,128,1024]{2,1,0:T(8,128)(2,1)S(1)}, u32[]{:S(2)}, u32[]{:S(2)}) collective-permute-start(bf16[4,128,1024]{2,1,0:T(8,128)(2,1)S(1)} %all-to-all-done), channel_id=1, source_target_pairs={{0,4},{4,0},{1,5},{5,1},{2,6},{6,2},{3,7},{7,3},{8,12},{12,8},{9,1... | collective-permute-start | bytes 3145736 | tf_op jit(solution)/shard_map/ppermute | solution.py:1343
  178.3 11.6 %collective-permute-start.2 = (bf16[1024,1024]{1,0:T(8,128)(2,1)}, bf16[1024,1024]{1,0:T(8,128)(2,1)}, u32[]{:S(2)}, u32[]{:S(2)}) collective-permute-start(bf16[1024,1024]{1,0:T(8,128)(2,1)} %convolution_convert_fusion.7), channel_id=1, source_target_pairs={{0,4},{4,0},{1,5},{5,1},{2,6},{6,2},{3,7},{7,3},{8,12},{12,8},{9,1... | collective-permute-start | bytes 6291464 | tf_op jit(solution)/shard_map/ppermute | solution.py:1343
  189.9 19.0 %copy-start.27 = (f32[1024]{0:T(1024)S(1)}, f32[1024]{0:T(1024)}, u32[]{:S(2)}) copy-start(f32[1024]{0:T(1024)} %param.37) | copy-start | bytes 12292
  226.1 141.9 %reduce-scatter.5.cloned.1.call-start = ((), (), s32[]{:S(2)}) async-start(), calls=%async_computation.8 | async-start | bytes 5242880 | tf_op jit(solution)/shard_map/reduce_scatter | solution.py:1555
  257.7 15.6 %collective-permute-start.6 = (bf16[1024,1024]{1,0:T(8,128)(2,1)}, bf16[1024,1024]{1,0:T(8,128)(2,1)}, u32[]{:S(2)}, u32[]{:S(2)}) collective-permute-start(bf16[1024,1024]{1,0:T(8,128)(2,1)} %convolution_convert_fusion.5), channel_id=1, source_target_pairs={{0,4},{4,0},{1,5},{5,1},{2,6},{6,2},{3,7},{7,3},{8,12},{12,8},{9,1... | collective-permute-start | bytes 6291464 | tf_op jit(solution)/shard_map/ppermute | solution.py:1343
  262.4 3.0 collective-permute-start.3
  268.6 106.0 %all-to-all-start.1 = ((bf16[4,128,1024]{2,1,0:T(8,128)(2,1)}), bf16[4,128,1024]{2,1,0:T(8,128)(2,1)}, u32[]{:S(2)}, u32[]{:S(2)}) async-start(bf16[4,128,1024]{2,1,0:T(8,128)(2,1)} %fusion.16), calls=%async_computation.1 | async-start | bytes 2097152 | tf_op jit(solution)/shard_map/all_to_all | solution.py:1412
  273.2 210.3 %reduce-scatter.11.cloned.1.call-start = ((), (), s32[]{:S(2)}) async-start(), calls=%async_computation.11 | async-start | bytes 655360 | tf_op jit(solution)/shard_map/reduce_scatter | solution.py:1571
  353.6 12.3 %copy-start.31 = (f32[2,128]{1,0:T(2,128)S(1)}, f32[2,128]{1,0:T(2,128)}, u32[]{:S(2)}) copy-start(f32[2,128]{1,0:T(2,128)} %get-tuple-element.65) | copy-start | bytes 3076
  353.7 12.3 %copy-start.32 = (f32[2,128]{1,0:T(2,128)S(1)}, f32[2,128]{1,0:T(2,128)}, u32[]{:S(2)}) copy-start(f32[2,128]{1,0:T(2,128)} %get-tuple-element.66) | copy-start | bytes 3076
  353.7 132.0 %reduce-scatter.7.cloned.1.call-start = ((), (), s32[]{:S(2)}) async-start(), calls=%async_computation.9 | async-start | bytes 1310720 | tf_op jit(solution)/shard_map/reduce_scatter | solution.py:1571
  365.2 11.9 %collective-permute-start.7 = (bf16[4,128,1024]{2,1,0:T(8,128)(2,1)}, bf16[4,128,1024]{2,1,0:T(8,128)(2,1)S(1)}, u32[]{:S(2)}, u32[]{:S(2)}) collective-permute-start(bf16[4,128,1024]{2,1,0:T(8,128)(2,1)} %dynamic-slice_bitcast_fusion), channel_id=1, source_target_pairs={{0,4},{4,0},{1,5},{5,1},{2,6},{6,2},{3,7},{7,3},{8,12},{12,8},{9,1... | collective-permute-start | bytes 3145736 | tf_op jit(solution)/shard_map/ppermute | solution.py:1343
  377.0 109.9 %collective-permute-start.4 = (bf16[2,128,1024]{2,1,0:T(8,128)(2,1)}, bf16[2,128,1024]{2,1,0:T(8,128)(2,1)}, u32[]{:S(2)}, u32[]{:S(2)}) collective-permute-start(bf16[2,128,1024]{2,1,0:T(8,128)(2,1)} %get-tuple-element.153), channel_id=1, source_target_pairs={{0,4},{4,0},{1,5},{5,1},{2,6},{6,2},{3,7},{7,3},{8,12},{12,8},{9,1... | collective-permute-start | bytes 1572872 | tf_op jit(solution)/shard_map/ppermute | solution.py:1343
  471.9 15.1 %copy-start.11 = (bf16[2,1,128,1024]{3,2,0,1:T(8,128)(2,1)S(1)}, bf16[2,1,128,1024]{3,2,0,1:T(8,128)(2,1)}, u32[]{:S(2)}) copy-start(bf16[2,1,128,1024]{3,2,0,1:T(8,128)(2,1)} %get-tuple-element.152) | copy-start | bytes 1572868
  484.4 5.0 %collective-permute-start.9 = (bf16[128,256]{1,0:T(8,128)(2,1)S(1)}, bf16[128,256]{1,0:T(8,128)(2,1)S(1)}, u32[]{:S(2)}, u32[]{:S(2)}) collective-permute-start(bf16[128,256]{1,0:T(8,128)(2,1)S(1)} %get-tuple-element.161), channel_id=1, source_target_pairs={{0,4},{4,0},{1,5},{5,1},{2,6},{6,2},{3,7},{7,3},{8,12},{12,8},{9,1... | collective-permute-start | bytes 196616 | tf_op jit(solution)/shard_map/ppermute | solution.py:1343
  486.8 3.6 collective-permute-start.8
  (31 other events, 199.1 us)
Sparse Core Ops, SparseCore 0:
  118.3 35.9 all-gather.4
  156.2 52.6 all-gather.2
  226.2 35.1 reduce-scatter.8
  264.5 52.6 reduce-scatter.4
  353.7 22.5 reduce-scatter.10
  378.5 40.6 reduce-scatter.6

commit v4 on v3

--- a/solution.py
+++ b/solution.py
@@ -1,5 +1,6 @@
 import jax
 import jax.numpy as jnp
+import numpy as np
 from jax import lax
 from jax.experimental import pallas as pl
 from jax.experimental.pallas import tpu as pltpu
@@ -75,6 +76,10 @@
     up = pltpu.roll(turned, 128 - half, 1)
     down = pltpu.roll(turned, half, 1)
     return values * cosine + jnp.where(lane % HEAD_SIZE < half, up, down)
+
+
+def cost(micros):
+    return pl.CostEstimate(flops=int(micros * 1e9), bytes_accessed=0, transcendentals=0)
 
 
 SCALE = HEAD_SIZE ** (-0.5)
@@ -188,6 +193,7 @@
             jax.ShapeDtypeStruct((rows, 256), jnp.float32),
         ],
         compiler_params=pltpu.CompilerParams(vmem_limit_bytes=BIG),
+        cost_estimate=cost(11),
         name="attention_forward",
     )(seq_len, proj, proj, cosine, sine)
 
@@ -210,6 +216,7 @@
             pltpu.VMEM((HEAD_SIZE, rows), jnp.float32),
         ],
         compiler_params=pltpu.CompilerParams(vmem_limit_bytes=BIG),
+        cost_estimate=cost(18),
         name="attention_backward",
     )(seq_len, proj, proj, cosine, sine, sums, grad)
 
@@ -376,6 +383,7 @@
             pltpu.VMEM((N, 2 * GROUP), jnp.float32),
         ],
         compiler_params=pltpu.CompilerParams(vmem_limit_bytes=BIG),
+        cost_estimate=cost(14),
         name="mamba_forward",
     )(proj, attn, taps, bias, decay, skip, gain)
 
@@ -596,6 +604,7 @@
             pltpu.VMEM((8, 128), jnp.float32),
         ],
         compiler_params=pltpu.CompilerParams(vmem_limit_bytes=BIG),
+        cost_estimate=cost(36),
         name="mamba_backward",
     )(proj, proj, out, states, back, dq, dkv, *params)
 
@@ -618,7 +627,7 @@
     w_ref,
     v_ref,
     up_rows,
-    down_rows,
+    d_ref,
     full_ref,
     params_ref,
     near_sem,
@@ -764,6 +773,37 @@
     def rows_at(at, side):
         return full_ref.at[pl.ds(pl.multiple_of(at * rows_dev + side * half, half), half)]
 
+    wide_up, wide_down = ups_ref.shape[2], downs_ref.shape[2]
+
+    def down_piece(at, part, place_at):
+        cols = pl.ds(pl.multiple_of(place_at * wide_down, wide_down), wide_down)
+        return d_ref.at[block(at, part), cols]
+
+    def up_piece(part, place_at):
+        return up_rows.at[
+            pl.ds(pl.multiple_of(part * share, share), share),
+            pl.ds(pl.multiple_of(place_at * wide_up, wide_up), wide_up),
+        ]
+
+    def send_halves(number, src, goal_ref, recv_sem):
+        for step in (2, 1, 3):
+            for side in range(2):
+                send(
+                    src.at[side],
+                    goal_ref,
+                    ffn_out.at[number, 2 * step + side],
+                    recv_sem,
+                    {"core": side, "tensor": (place + step) % 4},
+                )
+        send(
+            src.at[1 - core], goal_ref, ffn_out.at[number, 0], recv_sem, {"core": 1 - core}
+        )
+        pltpu.make_async_copy(src.at[core], goal_ref, recv_sem).start()
+
+    send_halves(
+        0, downs_ref, down_piece(plane, core, place), part_sem.at[10 + 2 * place + core]
+    )
+
     for seq in range(2):
         for side in range(2):
             goal = 2 * core + seq
@@ -786,40 +826,7 @@
                     device_id_type=MESH,
                 ).start()
 
-    wide_up, wide_down = ups_ref.shape[2], downs_ref.shape[2]
-    ffn_parts = []
-    for number, (src, dst, size) in enumerate(
-        ((ups_ref, up_rows, wide_up), (downs_ref, down_rows, wide_down))
-    ):
-        goal_ref = dst.at[
-            pl.ds(pl.multiple_of(core * share, share), share),
-            pl.ds(pl.multiple_of(place * size, size), size),
-        ]
-        for step in (2, 1, 3):
-            for side in range(2):
-                send(
-                    src.at[side],
-                    goal_ref,
-                    ffn_out.at[number, 2 * step + side],
-                    ffn_sem.at[number, 2 * place + core],
-                    {"core": side, "tensor": (place + step) % 4},
-                )
-        send(
-            src.at[1 - core],
-            goal_ref,
-            ffn_out.at[number, 0],
-            ffn_sem.at[number, 2 * place + core],
-            {"core": 1 - core},
-        )
-        pltpu.make_async_copy(src.at[core], goal_ref, ffn_sem.at[number, 2 * place + core]).start()
-        for at in range(4):
-            for part in range(2):
-                ffn_parts.append(
-                    (
-                        dst.at[pl.ds(part * share, share), pl.ds(at * size, size)],
-                        ffn_sem.at[number, 2 * at + part],
-                    )
-                )
+    send_halves(1, ups_ref, up_piece(core, place), ffn_sem.at[2 * place + core])
 
     first_col = jnp.where(place // 2 == core, place % 2, 1 - core)
     order = [(0, None, 0), (0, None, 1)]
@@ -828,14 +835,22 @@
             for part in range(2):
                 order.append((kind, (first_col + turn) % 2, part))
 
+    for step in (0, 1, 3, 2):
+        for part in range(2):
+            order.append((3, (place + step) % 4, part))
+
     def at_piece(at, item):
         kind, col, part = item
+        if kind == 3:
+            return down_piece(at, part, col)
         if kind == 0:
             return rest_piece(at, part)
         return piece(at, part, col) if kind == 1 else next_piece(at, part, col)
 
     def index(item):
         kind, col, part = item
+        if kind == 3:
+            return 10 + 2 * col + part
         return 4 + part if kind == 0 else (kind - 1) * 6 + part * 2 + col
 
     def relay(item):
@@ -857,7 +872,7 @@
         send(ref, ref, toy_sem.at[at], fromy_sem.at[at], {"plane": yside})
         if number >= 2:
             relay(order[number - 2])
-        if number == 9:
+        if number == 13:
             for step in range(4):
                 at = (place + step) % 4
                 ref = rows_at(at, core)
@@ -882,8 +897,9 @@
 
     for at in range(2):
         landed(params_ref.at[at], param_sem.at[at])
-    for ref, sem in ffn_parts:
-        landed(ref, sem)
+    for at in range(4):
+        for part in range(2):
+            landed(up_piece(part, at), ffn_sem.at[2 * at + part])
 
     @pl.when(target == core)
     def _():
@@ -919,59 +935,50 @@
             jax.ShapeDtypeStruct((8 * share, 2 * width + rest), pack.dtype),
             jax.ShapeDtypeStruct((8 * share, 2 * narrow), pack.dtype),
             jax.ShapeDtypeStruct((2 * share, 4 * ups.shape[2]), pack.dtype),
-            jax.ShapeDtypeStruct((2 * share, 4 * downs.shape[2]), pack.dtype),
+            jax.ShapeDtypeStruct((8 * share, 4 * downs.shape[2]), pack.dtype),
             jax.ShapeDtypeStruct((rows, x_rows.shape[2]), x_rows.dtype),
             jax.ShapeDtypeStruct((2,) + small.shape, small.dtype),
         ],
-        scratch_shapes=[dma((1,)), dma((8,))] + [dma((10,))] * 9 + [dma((4,))] * 6 + [dma((2, 8))] * 2,
+        scratch_shapes=[dma((1,)), dma((8,))] + [dma((18,))] * 9 + [dma((4,))] * 6 + [dma((8,)), dma((2, 8))],
         compiler_params=pltpu.CompilerParams(collective_id=1, has_side_effects=True),
+        cost_estimate=cost(80),
         name="spread",
     )(pack, following, ups, downs, shared, x_rows, small)
 
 
-def collect_kernel(
-    grad_ref,
-    next_ref,
-    small_ref,
-    rows_ref,
-    one_ref,
-    shared_ref,
-    total_ref,
-    back_ref,
-    mamba_out,
-    attn_out,
-    in_ref,
-    next_in,
-    sum_ref,
-    next_sum,
-    piece_ref,
-    next_buf,
-    pair_ref,
-    mix_ref,
-    near_ref,
-    far_ref,
-    in_sem,
-    out_sem,
-    piece_sem,
-    piece_out,
-    pair_sem,
-    mix_sem,
-    mix_out,
-    near_sem,
-    near_out,
-    far_sem,
-    far_out,
-    row_sem,
-    row_out,
-):
+def collect_kernel(*refs):
+    (mixed_ref, both_ref, normed_hbm, dproj_hbm, weight_hbm, x_hbm, hidden_hbm) = refs[:7]
+    (gain_ref, small_ref) = refs[7:9]
+    (mixer_out, query_out, step_out, shared_ref, total_ref, back_ref) = refs[9:15]
+    (mamba_out, attn_out) = refs[15:17]
+    (normed_ref, dproj_ref, weight_ref, x_ref, hidden_ref, grad_ref, next_ref) = refs[17:24]
+    (norm_ref, norm_in, rows_ref, in_ref, next_in, sum_ref, next_sum) = refs[24:31]
+    (piece_ref, next_buf, pair_ref, mix_ref, near_ref, far_ref) = refs[31:37]
+    (in_sem, out_sem, piece_sem, piece_out, pair_sem, mix_sem, mix_out) = refs[37:44]
+    (near_sem, near_out, far_sem, far_out, row_sem, row_out, load_sem, norm_sem) = refs[44:]
     plane = lax.axis_index("plane")
     core = lax.axis_index("core")
     place = lax.axis_index("tensor")
     xside = plane + 1 - 2 * (plane % 2)
     yside = plane + 2 - 4 * (plane // 2)
     across = xside + 2 - 4 * (xside // 2)
-    share, width = one_ref.shape
+    share = pair_ref.shape[0]
+    width = piece_ref.shape[2]
     rest = grad_ref.shape[1] - 2 * width
+
+    loads = [
+        (dproj_hbm, dproj_ref),
+        (weight_hbm, weight_ref),
+        (normed_hbm, normed_ref),
+        (x_hbm.at[:, core], x_ref),
+        (hidden_hbm.at[:, core], hidden_ref),
+    ]
+    for number, (src, dst) in enumerate(loads):
+        pltpu.make_async_copy(src, dst, load_sem.at[number]).start()
+
+    def loaded(number):
+        src, dst = loads[number]
+        pltpu.make_async_copy(src, dst, load_sem.at[number]).wait()
 
     barrier = pltpu.get_barrier_semaphore()
     for step in range(4):
@@ -1047,37 +1054,85 @@
             {"plane": yside},
         )
 
-    send(small_ref, near_ref.at[0], near_out.at[0], near_sem.at[0], {"plane": xside})
-    begin(0)
-    begin(1)
+    def work(number):
+        kind, begin_at, size = spans[number]
+        left = (normed_ref, mixed_ref)[kind]
+        right = (dproj_ref, both_ref)[kind]
+        result = (grad_ref, next_ref)[kind]
+        tile = 256 if size % 256 == 0 else size
+
+        @pl.loop(0, size // tile)
+        def _(at):
+            cols = pl.ds(pl.multiple_of(begin_at + at * tile, 128), tile)
+            result[:, cols] = low(dot_tn(left[...], right[:, cols]))
 
     seq = place % 2
     owner = place // 2
     dst_rows = back_ref.at[seq, pl.ds(pl.multiple_of(core * share, share), share)]
-    for step in (2, 1, 3):
-        at = (place + step) % 4
+
+    def send_back():
+        for step in (2, 1, 3):
+            at = (place + step) % 4
+            send(
+                rows_ref.at[at],
+                dst_rows,
+                row_out.at[step],
+                row_sem.at[seq * 2 + core],
+                {"core": owner, "tensor": at},
+            )
+
+        @pl.when(owner == core)
+        def _():
+            pltpu.make_async_copy(
+                rows_ref.at[place], dst_rows, row_sem.at[seq * 2 + core]
+            ).start()
+
+        @pl.when(owner != core)
+        def _():
+            pltpu.make_async_remote_copy(
+                src_ref=rows_ref.at[place],
+                dst_ref=dst_rows,
+                send_sem=row_out.at[0],
+                recv_sem=row_sem.at[seq * 2 + core],
+                device_id={"core": 1 - core},
+                device_id_type=MESH,
+            ).start()
+
+    def norm_product():
+        loaded(0)
+        loaded(1)
+        for at in range(4):
+            rows = pl.ds(at * 2 * share, 2 * share)
+            part = low(dot_nt(dproj_ref[rows, :], weight_ref[...]))
+            norm_ref[at, 0] = part[:share]
+            norm_ref[at, 1] = part[share:]
         send(
-            rows_ref.at[at],
-            dst_rows,
-            row_out.at[step],
-            row_sem.at[seq * 2 + core],
-            {"core": owner, "tensor": at},
-        )
-
-    @pl.when(owner == core)
-    def _():
-        pltpu.make_async_copy(rows_ref.at[place], dst_rows, row_sem.at[seq * 2 + core]).start()
-
-    @pl.when(owner != core)
-    def _():
-        pltpu.make_async_remote_copy(
-            src_ref=rows_ref.at[place],
-            dst_ref=dst_rows,
-            send_sem=row_out.at[0],
-            recv_sem=row_sem.at[seq * 2 + core],
-            device_id={"core": 1 - core},
-            device_id_type=MESH,
-        ).start()
+            norm_ref.at[:, 1 - core],
+            norm_in,
+            norm_sem.at[0],
+            norm_sem.at[1],
+            {"core": 1 - core},
+        )
+
+    def norm_back():
+        loaded(3)
+        loaded(4)
+        landed(norm_in, norm_sem.at[1])
+        gain_total = jnp.zeros((1, x_ref.shape[2]), jnp.float32)
+        for at in range(4):
+            grad = wide(norm_ref[at, core]) + wide(norm_in[at])
+            values = wide(x_ref[at])
+            size = 1.0 / values.shape[1]
+            root = lax.rsqrt(jnp.sum(values * values, axis=1, keepdims=True) * size + EPS)
+            scaled = grad * gain_ref[...]
+            inner = jnp.sum(values * scaled, axis=1, keepdims=True) * size
+            rows_ref[at] = low(
+                hidden_ref[at] + root * scaled - values * (root * root * root * inner)
+            )
+            gain_total = gain_total + jnp.sum(values * root * grad, axis=0, keepdims=True)
+        near_ref[5] = small_ref[...]
+        for at in range(gain_total.shape[1] // 128):
+            near_ref[5, at : at + 1, :] = gain_total[:, at * 128 : (at + 1) * 128]
 
     def pass_on(number):
         span = spans[number]
@@ -1139,43 +1194,67 @@
 
     rest_cols = pl.ds(2 * width, rest)
     state = rest * 2 // 3
+
+    def pair_up():
+        send(
+            sum_ref.at[1 - core, :, rest_cols],
+            pair_ref,
+            pair_sem.at[0],
+            pair_sem.at[1],
+            {"core": 1 - core},
+        )
+
+    def mix():
+        landed(pair_ref, pair_sem.at[1])
+        mine = sum_ref[core, :, rest_cols]
+        mix_ref[place, :, 0:state] = low(wide(mine[:, :state]) + wide(pair_ref[:, :state]))
+        first = core == 0
+        mix_ref[place, :, state:rest] = jnp.where(first, mine[:, state:], pair_ref[:, state:])
+        mix_ref[place, :, rest:] = jnp.where(first, pair_ref[:, state:], mine[:, state:])
+        own_mix = mix_ref.at[place]
+        for step in (2, 1, 3):
+            send(
+                own_mix,
+                own_mix,
+                mix_out.at[step],
+                mix_sem.at[place],
+                {"tensor": (place + step) % 4},
+            )
+
+    work(3)
+    begin(3)
+    work(4)
+    begin(4)
+    norm_product()
+    pass_on(3)
+    loaded(2)
+    work(0)
+    begin(0)
+    finish(3)
+    send_pieces(3)
+    pass_on(4)
+    norm_back()
+    send_back()
+    send(near_ref.at[5], near_ref.at[0], near_out.at[0], near_sem.at[0], {"plane": xside})
+    work(1)
+    begin(1)
+    finish(4)
+    send_pieces(4)
     pass_on(0)
+    work(2)
     landed(near_ref.at[0], near_sem.at[0])
-    near_ref[3] = small_ref[...] + near_ref[0]
+    near_ref[3] = near_ref[5] + near_ref[0]
     send(near_ref.at[3], near_ref.at[1], near_out.at[1], near_sem.at[1], {"plane": yside})
+    finish(0)
+    pair_up()
+    pass_on(1)
     begin(2)
-    finish(0)
-    send(
-        sum_ref.at[1 - core, :, rest_cols],
-        pair_ref,
-        pair_sem.at[0],
-        pair_sem.at[1],
-        {"core": 1 - core},
-    )
-    pass_on(1)
-    begin(3)
     landed(near_ref.at[1], near_sem.at[1])
     near_ref[4] = near_ref[3] + near_ref[1]
     send(near_ref.at[4], near_ref.at[2], near_out.at[2], near_sem.at[2], {"core": 1 - core})
-    landed(pair_ref, pair_sem.at[1])
-    mine = sum_ref[core, :, rest_cols]
-    mix_ref[place, :, 0:state] = low(wide(mine[:, :state]) + wide(pair_ref[:, :state]))
-    first = core == 0
-    mix_ref[place, :, state:rest] = jnp.where(first, mine[:, state:], pair_ref[:, state:])
-    mix_ref[place, :, rest:] = jnp.where(first, pair_ref[:, state:], mine[:, state:])
-    own_mix = mix_ref.at[place]
-    for step in (2, 1, 3):
-        send(
-            own_mix,
-            own_mix,
-            mix_out.at[step],
-            mix_sem.at[place],
-            {"tensor": (place + step) % 4},
-        )
+    mix()
     finish(1)
     send_pieces(1)
-    pass_on(2)
-    begin(4)
     landed(near_ref.at[2], near_sem.at[2])
     far_ref[place] = near_ref[4] + near_ref[2]
     own_far = far_ref.at[place]
@@ -1187,14 +1266,9 @@
             far_sem.at[place],
             {"tensor": (place + step) % 4},
         )
+    pass_on(2)
     finish(2)
     send_pieces(2)
-    pass_on(3)
-    finish(3)
-    send_pieces(3)
-    pass_on(4)
-    finish(4)
-    send_pieces(4)
 
     for step in (1, 2, 3):
         at = (place + step) % 4
@@ -1209,7 +1283,11 @@
             landed(buf.at[at], piece_sem.at[kind, at])
         return wide(buf[0]) + wide(buf[1]) + wide(buf[2]) + wide(buf[3])
 
-    one_ref[...] = gathered(piece_ref, 0)
+    one = gathered(piece_ref, 0)
+    cut = mixer_out.shape[1]
+    mixer_out[...] = one[:, :cut]
+    query_out[...] = one[:, cut : cut + query_out.shape[1]]
+    step_out[...] = one[:, cut + query_out.shape[1] :]
     both = gathered(next_buf, 1).T
     mamba_out[...] = both[: mamba_out.shape[0]]
     attn_out[...] = both[mamba_out.shape[0] :]
@@ -1232,38 +1310,54 @@
                 landed(summed(part, span), piece_out.at[span[0], 2 * col + part])
 
 
-def collect(grad, following, small, rows, width, mamba_cols):
-    share = grad.shape[0] // 8
-    rest = grad.shape[1] - 2 * width
-    narrow = following.shape[1] // 2
+def collect(normed, dproj, weight, mixed, both, x_rows, hidden, gain, small, sizes):
+    chans, queries, width = sizes
+    share = weight.shape[0] // 8
+    model = weight.shape[0]
+    columns = weight.shape[1]
+    rest = columns - 2 * width
+    narrow = both.shape[1] // 2
     dma = pltpu.SemaphoreType.DMA
     any_space = pl.BlockSpec(memory_space=pl.ANY)
     near = pl.BlockSpec(memory_space=pltpu.VMEM)
-    model = rows.shape[2]
     shared_cols = rest + rest // 3
     bf16, f32 = jnp.bfloat16, jnp.float32
+    split = (4, 2, x_rows.shape[0] // 8, model)
+    half = (4, x_rows.shape[0] // 8, model)
     return pl.pallas_call(
         collect_kernel,
-        in_specs=[near, near, near, any_space],
-        out_specs=[near, near, near, any_space, near, near],
+        in_specs=[near, near] + [any_space] * 5 + [near, near],
+        out_specs=[near] * 5 + [any_space] + [near] * 2,
         out_shape=[
-            jax.ShapeDtypeStruct((share, width), f32),
+            jax.ShapeDtypeStruct((share, 2 * chans), f32),
+            jax.ShapeDtypeStruct((share, queries), f32),
+            jax.ShapeDtypeStruct((share, width - 2 * chans - queries), f32),
             jax.ShapeDtypeStruct((share, shared_cols), f32),
             jax.ShapeDtypeStruct(small.shape, f32),
-            jax.ShapeDtypeStruct((2, 2 * rows.shape[1], model), rows.dtype),
-            jax.ShapeDtypeStruct((mamba_cols, share), f32),
-            jax.ShapeDtypeStruct((narrow - mamba_cols, share), f32),
+            jax.ShapeDtypeStruct((2, 2 * half[1], model), bf16),
+            jax.ShapeDtypeStruct((chans, share), f32),
+            jax.ShapeDtypeStruct((narrow - chans, share), f32),
         ],
         scratch_shapes=[
-            pltpu.VMEM((6, share, grad.shape[1]), bf16),
-            pltpu.VMEM((6, share, following.shape[1]), bf16),
-            pltpu.VMEM((2, share, grad.shape[1]), bf16),
-            pltpu.VMEM((2, share, following.shape[1]), bf16),
+            pltpu.VMEM(normed.shape, bf16),
+            pltpu.VMEM(dproj.shape, bf16),
+            pltpu.VMEM(weight.shape, bf16),
+            pltpu.VMEM(half, bf16),
+            pltpu.VMEM(half, f32),
+            pltpu.VMEM((model, columns), bf16),
+            pltpu.VMEM((model, 2 * narrow), bf16),
+            pltpu.VMEM(split, bf16),
+            pltpu.VMEM(half, bf16),
+            pltpu.VMEM(half, bf16),
+            pltpu.VMEM((6, share, columns), bf16),
+            pltpu.VMEM((6, share, 2 * narrow), bf16),
+            pltpu.VMEM((2, share, columns), bf16),
+            pltpu.VMEM((2, share, 2 * narrow), bf16),
             pltpu.VMEM((4, share, width), bf16),
             pltpu.VMEM((4, share, narrow), bf16),
             pltpu.VMEM((share, rest), bf16),
             pltpu.VMEM((4, share, shared_cols), bf16),
-            pltpu.VMEM((5,) + small.shape, f32),
+            pltpu.VMEM((6,) + small.shape, f32),
             pltpu.VMEM((4,) + small.shape, f32),
             dma((6, 5)),
             dma((6, 5)),
@@ -1278,12 +1372,25 @@
             dma((4,)),
             dma((4,)),
             dma((4,)),
+            dma((5,)),
+            dma((2,)),
         ],
         compiler_params=pltpu.CompilerParams(
             collective_id=2, has_side_effects=True, vmem_limit_bytes=BIG
         ),
+        cost_estimate=cost(80),
         name="collect",
-    )(grad, following, small, rows)
+    )(
+        mixed,
+        both,
+        normed,
+        dproj,
+        weight,
+        x_rows.reshape(split),
+        hidden.reshape(split),
+        gain.reshape(1, -1),
+        small,
+    )
 
 
 def rms_norm(values, gain_vec):
@@ -1292,12 +1399,12 @@
 
 def turn_tables(seq_count, head_count):
     half_dim = HEAD_SIZE // 2
-    freqs = THETA ** (-jnp.arange(half_dim, dtype=jnp.float32) * 2.0 / HEAD_SIZE)
-    angles = jnp.arange(seq_count, dtype=jnp.float32)[:, None] * freqs[None, :]
-    cosine, sine = jnp.cos(angles), jnp.sin(angles)
+    freqs = np.float32(THETA) ** (-np.arange(half_dim, dtype=np.float32) * 2.0 / HEAD_SIZE)
+    angles = np.arange(seq_count, dtype=np.float32)[:, None] * freqs.astype(np.float32)[None, :]
+    cosine, sine = np.cos(angles), np.sin(angles)
     return (
-        jnp.tile(jnp.concatenate([cosine, cosine], axis=1), (1, head_count)),
-        jnp.tile(jnp.concatenate([-sine, sine], axis=1), (1, head_count)),
+        jnp.asarray(np.tile(np.concatenate([cosine, cosine], axis=1), (1, head_count))),
+        jnp.asarray(np.tile(np.concatenate([-sine, sine], axis=1), (1, head_count))),
     )
 
 
@@ -1309,34 +1416,6 @@
         gate, up = gate_up[:, at : at + units], gate_up[:, at + units : at + 2 * units]
         parts.append(gate * sigmoid(gate) * up)
     return jnp.concatenate(parts, axis=1)
-
-
-def pairs_split(step):
-    return [
-        (core * 4 + place, (goal // 2) * 4 + 2 * core + goal % 2)
-        for core in range(2)
-        for place in range(4)
-        for goal in [(place + step) % 4]
-    ]
-
-
-def pairs_join(step):
-    return [
-        (core * 4 + place, (place // 2) * 4 + (2 * core + place % 2 + step) % 4)
-        for core in range(2)
-        for place in range(4)
-    ]
-
-
-def exchange(piece_at, mine, yours, pairs):
-    moved = [
-        lax.ppermute(piece_at((mine + step) % 4), ("core", "tensor"), pairs(step))
-        for step in range(4)
-    ]
-    stacked = jnp.stack(moved)
-    return [
-        lax.dynamic_index_in_dim(stacked, (yours - source) % 4, 0, False) for source in range(4)
-    ]
 
 
 def swapped(values):
@@ -1459,7 +1538,7 @@
     quad = quad and share == half_rows
     if quad:
         shared = jnp.stack([shared_for(0), shared_for(1)])
-        weight_one, weight_two, rows_up, rows_down, x_low, small_mine = spread(
+        weight_one, weight_two, rows_up, down_weight, x_low, small_mine = spread(
             pack_one, pack_two, pack_ups, pack_downs, shared, layer_in, small_in
         )
     else:
@@ -1488,11 +1567,11 @@
         rows_up, rows_down = (
             lax.all_gather(rows, "tensor", axis=1, tiled=True) for rows in (rows_up, rows_down)
         )
+        down_weight = lax.all_gather(rows_down, "plane", axis=0, tiled=True)
         small_mine = mine(lax.all_gather(small_in, "tensor", axis=0))
     small_mine = small_mine.reshape(held, -1)
 
     gate_up_weight = lax.all_gather(rows_up, "plane", axis=0, tiled=True)
-    down_weight = lax.all_gather(rows_down, "plane", axis=0, tiled=True)
 
     cuts = []
     at = 0
@@ -1555,30 +1634,24 @@
         return lax.psum_scatter(values, "plane", scatter_dimension=0, tiled=True)
 
     def to_groups(values):
-        rows, columns = values.shape
-
-        def piece_at(goal):
-            return lax.dynamic_slice(
-                values,
-                ((goal // 2) * (rows // 2), (goal % 2) * (columns // 2)),
-                (rows // 2, columns // 2),
-            )
-
-        parts = exchange(piece_at, place, spot, pairs_split)
-        return wide(parts[0]) + wide(parts[1]) + wide(parts[2]) + wide(parts[3])
-
-    def to_units(values):
-        part = lax.psum_scatter(values, "tensor", scatter_dimension=1, tiled=True)
-        by_part = part.reshape(2, share, -1)
+        by_part = values.reshape(2, share, held, -1).transpose(0, 2, 1, 3)
         own = lax.dynamic_index_in_dim(by_part, core, 0, False)
         theirs = swapped(lax.dynamic_index_in_dim(by_part, 1 - core, 0, False))
-        return wide(in_order(own[None], theirs[None], 0))
-
-    units_down = to_units(scatter(grad_down))
-    units_up = to_units(scatter(grad_gate_up_weight))
-    sum_down = units_down.transpose(0, 2, 1).reshape(hidden_dev, share)
-    sum_up = units_up.reshape(2, share, 2, own_units).transpose(1, 2, 0, 3)
-    grad_two = low(dot_tn(grad_mixed, both_low))
+        whole = in_order(own, theirs, 0)
+        return wide(lax.psum_scatter(whole, "tensor", scatter_dimension=0, tiled=True)[0])
+
+    def to_units(values):
+        return lax.psum_scatter(values, "tensor", scatter_dimension=1, tiled=True)
+
+    units = jnp.concatenate(
+        [to_units(scatter(grad_gate_up_weight)), to_units(scatter(grad_down))], axis=1
+    )
+    units = units.reshape(2, share, -1)
+    own_part = lax.dynamic_index_in_dim(units, core, 0, True)
+    their_part = swapped(lax.dynamic_index_in_dim(units, 1 - core, 0, True))
+    units = wide(in_order(own_part, their_part, 0))
+    sum_up = units[:, :, :hidden_dev].reshape(2, share, 2, own_units).transpose(1, 2, 0, 3)
+    sum_down = units[:, :, hidden_dev:].transpose(0, 2, 1).reshape(hidden_dev, share)
 
     back = dot(grad_mixed, weight_two)
     attn_back = jnp.concatenate(
@@ -1590,20 +1663,7 @@
     proj_grad, grad_taps, grad_gain, grad_skip_cols, grad_bias, grad_decay = mamba_backward(
         proj, state_out, states, back, grad_q, grad_kv, taps, bias, decay, skip, gain
     )
-    grad_one = low(dot_tn(normed, proj_grad))
     edge = held * group_cols
-    grad_norm_part = low(dot_nt(proj_grad, weight_one))
-    grad_norm_own = wide(own_half(grad_norm_part)) + wide(swapped(other_half(grad_norm_part)))
-    x_own = wide(own_half(x_low))
-    r_one = lax.rsqrt(jnp.mean(x_own * x_own, axis=-1, keepdims=True) + EPS)
-    scaled = grad_norm_own * norm_gain
-    grad_x = low(
-        own_half(grad_hidden)
-        + r_one * scaled
-        - x_own * (r_one**3 * jnp.mean(x_own * scaled, axis=-1, keepdims=True))
-    )
-    grad_norm_gain = jnp.sum(x_own * r_one * grad_norm_own, axis=(0, 1))
-
     grad_skip = jnp.sum(grad_skip_cols.reshape(held, heads_dev, HEAD_SIZE), axis=-1)
     chan_taps = grad_taps[:, : held * chans_dev].reshape(KCONV, held, chans_dev)
     group_small = jnp.concatenate(
@@ -1619,7 +1679,7 @@
     small_groups = in_order(group_small, jnp.zeros_like(group_small), 0)
     small_out = jnp.concatenate(
         [
-            grad_norm_gain,
+            jnp.zeros_like(norm_gain),
             grad_ffn_gain,
             grad_taps[:, held * chans_dev :].reshape(-1),
             small_groups.reshape(-1),
@@ -1628,16 +1688,42 @@
     if quad:
         small_size = small_out.shape[0]
         small_room = -(-small_size // 1024) * 1024
-        sum_one, shared_sum, small_sum, input_grad, sum_mamba, sum_attn = collect(
-            grad_one,
-            grad_two,
+        (
+            sum_mixer,
+            sum_query,
+            sum_step,
+            shared_sum,
+            small_sum,
+            input_grad,
+            sum_mamba,
+            sum_attn,
+        ) = collect(
+            normed,
+            proj_grad,
+            weight_one,
+            grad_mixed,
+            both_low,
+            x_low,
+            grad_hidden,
+            norm_gain,
             jnp.pad(small_out, (0, small_room - small_size)).reshape(-1, 128),
-            grad_x,
-            group_cols,
-            chans_dev,
+            (chans_dev, query_dev, group_cols),
         )
         small_sum = small_sum.reshape(-1)[:small_size]
     else:
+        grad_one = low(dot_tn(normed, proj_grad))
+        grad_norm_part = low(dot_nt(proj_grad, weight_one))
+        grad_norm_own = wide(own_half(grad_norm_part)) + wide(swapped(other_half(grad_norm_part)))
+        x_own = wide(own_half(x_low))
+        r_one = lax.rsqrt(jnp.mean(x_own * x_own, axis=-1, keepdims=True) + EPS)
+        scaled = grad_norm_own * norm_gain
+        grad_x = low(
+            own_half(grad_hidden)
+            + r_one * scaled
+            - x_own * (r_one**3 * jnp.mean(x_own * scaled, axis=-1, keepdims=True))
+        )
+        grad_norm_gain = jnp.sum(x_own * r_one * grad_norm_own, axis=(0, 1))
+        small_out = small_out.at[:model_dim].set(grad_norm_gain)
         part_one = scatter(grad_one)
         both_parts = part_one[:, edge:].reshape(2, share, -1)
         own_rest = lax.dynamic_index_in_dim(both_parts, core, 0, False)
@@ -1647,7 +1733,10 @@
         shared_low = jnp.concatenate([low(shared_own), kv_both], axis=1)
         shared_sum = jnp.sum(wide(lax.all_gather(shared_low, "tensor", axis=0)), axis=0)
         sum_one = to_groups(part_one[:, :edge])
-        sum_two = to_groups(scatter(grad_two)).T
+        sum_mixer = sum_one[:, : 2 * chans_dev]
+        sum_query = sum_one[:, 2 * chans_dev : 2 * chans_dev + query_dev]
+        sum_step = sum_one[:, 2 * chans_dev + query_dev :]
+        sum_two = to_groups(scatter(low(dot_tn(grad_mixed, both_low)))).T
         sum_mamba, sum_attn = sum_two[:chans_dev], sum_two[chans_dev:]
         input_grad = positions_out(grad_x)
         small_sum = lax.psum(small_out, ("plane", "core", "tensor"))
@@ -1661,15 +1750,14 @@
         pieces.append(group_sum[at : at + size])
         at += size
 
-    one = sum_one
     return (
         layer_out,
         input_grad,
         small_sum[:model_dim],
-        one[:, : 2 * chans_dev].reshape(share, 2, chans_dev),
-        one[:, 2 * chans_dev + query_dev :][:, :heads_dev],
+        sum_mixer.reshape(share, 2, chans_dev),
+        sum_step[:, :heads_dev],
         shared_sum[:, : 2 * N].reshape(share, 2, N),
-        one[:, 2 * chans_dev : 2 * chans_dev + query_dev],
+        sum_query,
         kv_sum.reshape(share, 2, 2 * HEAD_SIZE),
         pieces[0].reshape(KCONV, chans_dev),
         small_sum[2 * model_dim : 2 * model_dim + KCONV * 2 * N].reshape(KCONV, 2, N),

time: 508 us -> 466 us (0.917)
  the two profiles are of different devices: /device:TPU:0 before, /device:TPU:9 now
where the time goes in v4:
time: 466 us; the launch traced here: 459 us
  Pallas kernels  284 us (61%)
  other arithmetic  50.8 us (11%)
  matrix products  50.7 us (11%)
  local copies, waits for them, and re-layouts  44.2 us (9%)
  between operations  14.6 us (3%)
  starting transfers between devices  11.9 us (3%)
    pallas_call x1, Pallas kernels, spread(): pl.pallas_call(spread_kernel, in_specs=[any_space] * 7, out_specs=[any_sp...  104 us
    pallas_call x1, Pallas kernels, collect(): pl.pallas_call(collect_kernel, in_specs=[near, near] + [any_space] * 5 +...  99.6 us
    pallas_call x1, Pallas kernels, mamba_backward(): pl.pallas_call(mamba_backward_kernel, grid=(chunks,), in_specs=[rows_of(c...  36.5 us
    dot_general x4, matrix products, dot(): return jnp.dot(left, right, preferred_element_type=jnp.float32)  24.5 us
    unnamed x86, local copies, waits for them, and re-layouts  19.5 us
    pallas_call x1, Pallas kernels, attention_backward(): pl.pallas_call(attention_backward_kernel, grid=(2,), in_specs=attention_s...  18.1 us
    convert_element_type x5, other arithmetic, low(): return values.astype(jnp.bfloat16)  16.3 us
    dot_general x3, matrix products, dot_nt(): lax.dot_general(left, right, (((1,), (1,)), ((), ())), preferred_element_...  15.8 us
  transfers between devices with their start and end apart: 15, of which 2 were waited for; matrix products, arithmetic and copies ran while one was open for 20% of the time, Pallas kernels for 39%

profile of v4, /device:TPU:9, one launch (start us, length us, event | category | flops | bytes accessed | tf_op | source)
XLA Modules:
  0.0 459.3 jit_solution(18137560552513140749)
XLA Ops:
  21.6 104.1 %spread.1 = (bf16[1024,2432]{1,0:T(8,128)(2,1)}, bf16[1024,1024]{1,0:T(8,128)(2,1)}, bf16[256,2048]{1,0:T(8,128)(2,1)}, bf16[1024,1024]{1,0:T(8,128)(2,1)}, bf16...) custom-call(bf16[128,1024]{1,0:T(8,128)(2,1)} %fusion.25.pack_ref, bf16[128,512]{1,0:T(8,128)(2,1)} %pad_maximum_fusion.6.next_ref, ...), custom_call_target="tpu_custom_call" | custom-call | flops 80000000000 | tf_op jit(solution)/shard_map/spread/pallas_call | solution.py:930
  131.4 8.0 %fusion.43.q_ref.kv_ref.proj_ref.before_ref = f32[1024,2432]{1,0:T(8,128)} fusion(bf16[1024,1024]{1,0:T(8,128)(2,1)S(1)} %fusion.2.refs_2_, bf16[1024,2432]{1,0:T(8,128)(2,1)S(1)} %copy-done.33), kind=kOutput, calls=%fused_computation.124 | convolution fusion | flops 5100273664 | bytes 17039360 | tf_op jit(solution)/shard_map/dot_general | solution.py:29
  145.3 4.6 %all-to-all-start = ((bf16[4,128,1024]{2,1,0:T(8,128)(2,1)}), bf16[4,128,1024]{2,1,0:T(8,128)(2,1)S(1)}, u32[]{:S(2)}, u32[]{:S(2)}) async-start(bf16[4,128,1024]{2,1,0:T(8,128)(2,1)} %maximum_select_fusion.1), calls=%async_computation | async-start | bytes 2097152 | tf_op jit(solution)/shard_map/all_to_all | solution.py:1484
  150.1 11.2 %attention_forward.1 = (bf16[1024,256]{1,0:T(8,128)(2,1)}, f32[1024,256]{1,0:T(8,128)}) custom-call(s32[1]{0:T(128)} %dynamic_slice.52.len_ref, f32[1024,2432]{1,0:T(8,128)} %fusion.43.q_ref.kv_ref.proj_ref.before_ref, f32[1024,2432]{1,0:T(8,128)} %fusion.43.q_ref.kv_ref.proj_ref.before_ref, f32[1024,128]{1,0:T(8,128)} %constant.83.clone.cos_ref, ...), custom_call_target="tpu_custom_call" | custom-call | flops 11000000512 | tf_op jit(solution)/shard_map/attention_forward/pallas_call | solution.py:186
  161.3 14.7 %mamba_forward.1 = (bf16[1024,1024]{1,0:T(8,128)(2,1)}, f32[1024,768]{1,0:T(8,128)}, f32[8,128,768]{2,1,0:T(8,128)}) custom-call(f32[1024,2432]{1,0:T(8,128)} %fusion.43.q_ref.kv_ref.proj_ref.before_ref, bf16[1024,256]{1,0:T(8,128)(2,1)} %get-tuple-element.52.attn_ref, f32[4,1024]{1,0:T(4,128)} %pad_maximum_fusion.9.taps_ref, f32[2,128]{1,0:T(2,128)} %pad.47.bias_ref, ...), custom_call_target="tpu_custom_call" | custom-call | flops 14000000000 | tf_op jit(solution)/shard_map/mamba_forward/pallas_call | solution.py:363
  176.5 4.0 convolution_convert_fusion.4
  183.6 4.3 fusion.44
  188.0 3.0 multiply_reduce_fusion.1
  191.7 7.8 %fusion.35 = f32[1024,2048]{1,0:T(8,128)S(1)} fusion(bf16[1024,2048]{1,0:T(8,128)(2,1)} %all-gather.2.cloned.1.call-done, f32[1024,1024]{1,0:T(8,128)} %get-tuple-element.120, f32[1024]{0:T(1024)S(1)} %copy-done.24, f32[1024]{0:T(1024)S(1)} %add_rsqrt_fusion), kind=kOutput, calls=%fused_computation.117 | convolution fusion | flops 4298113024 | bytes 16785408 | tf_op jit(solution)/shard_map/dot_general | solution.py:29
  199.5 3.6 slice_multiply_fusion.2
  204.7 3.8 convolution_convert_fusion.1
  208.6 8.5 %slice_multiply_fusion.3 = (f32[1024,256]{1,0:T(8,128)}, f32[1024,256]{1,0:T(8,128)}, f32[1024,256]{1,0:T(8,128)}, f32[1024,256]{1,0:T(8,128)}, f32[1024,256]{1,...) fusion(f32[1024,1024]{1,0:T(8,128)} %fusion.44, f32[1024,2048]{1,0:T(8,128)} %copy-done.2), kind=kLoop, calls=%fused_computation.59 | loop fusion | flops 15204352 | bytes 19922944 | tf_op jit(solution)/shard_map/transpose(jvp())/mul | solution.py:1417
  217.1 4.2 add_convert_fusion
  223.3 6.6 %convolution_convert_fusion = bf16[1024,2048]{1,0:T(8,128)(2,1)} fusion(bf16[1024,2048]{1,0:T(8,128)(2,1)S(1)} %add_convert_fusion, f32[1024,1024]{1,0:T(8,128)S(1)} %copy-done, f32[1024]{0:T(1024)S(1)} %copy-done.24, f32[1024]{0:T(1024)S(1)} %add_rsqrt_fusion), kind=kOutput, calls=%fused_computation.17 | convolution fusion | flops 4300210176 | bytes 12591104 | tf_op jit(solution)/shard_map/dot_general | solution.py:39
  230.0 9.4 %convolution_convert_fusion.2 = bf16[1024,1024]{1,0:T(8,128)(2,1)} fusion(bf16[1024,2048]{1,0:T(8,128)(2,1)} %copy-done.6, bf16[1024,2048]{1,0:T(8,128)(2,1)} %all-gather.2.cloned.1.call-done), kind=kOutput, calls=%fused_computation.26 | convolution fusion | flops 4296015872 | bytes 10485760 | tf_op jit(solution)/shard_map/dot_general | solution.py:33
  240.1 2.4 convolution_convert_fusion.3
  246.4 2.9 fusion.10
  249.3 4.5 all-to-all-start.1
  253.9 4.9 %multiply_reduce_fusion = f32[1024]{0:T(1024)S(1)} fusion(f32[1024,1024]{1,0:T(8,128)} %get-tuple-element.120, bf16[1024,1024]{1,0:T(8,128)(2,1)} %collective-permute-done.6, bf16[1024,1024]{1,0:T(8,128)(2,1)} %convolution_convert_fusion.2, f32[1024]{0:T(1024)S(1)} %copy-done.24), kind=kLoop, calls=%fused_computation.11 | loop fusion | flops 6290432 | bytes 8396800 | tf_op jit(solution)/shard_map/reduce_sum | solution.py:1628
  259.6 6.6 %fusion.36 = (bf16[1024,1024]{1,0:T(8,128)(2,1)S(1)}, f32[1024,1024]{1,0:T(8,128)}, f32[1024,1024]{1,0:T(8,128)}) fusion(f32[1024,1024]{1,0:T(8,128)S(1)} %copy-done.1, f32[1024]{0:T(1024)S(1)} %fusion.29, f32[1024]{0:T(1024)S(1)} %copy-done.24, bf16[1024,1024]{1,0:T(8,128)(2,1)} %collective-permute-done.6, ...), kind=kLoop, calls=%fused_computation.118 | loop fusion | flops 13631488 | bytes 20987904 | tf_op jit(solution)/shard_map/convert_element_type | solution.py:21
  266.2 4.4 fusion.42
  271.5 18.1 %attention_backward.1 = (bf16[1024,256]{1,0:T(8,128)(2,1)}, bf16[1024,128]{1,0:T(8,128)(2,1)}) custom-call(s32[1]{0:T(128)} %dynamic_slice.52.len_ref, f32[1024,2432]{1,0:T(8,128)} %fusion.43.q_ref.kv_ref.proj_ref.before_ref, f32[1024,2432]{1,0:T(8,128)} %fusion.43.q_ref.kv_ref.proj_ref.before_ref, f32[1024,128]{1,0:T(8,128)} %constant.83.clone.cos_ref, ...), custom_call_target="tpu_custom_call" | custom-call | flops 17999998976 | tf_op jit(solution)/shard_map/attention_backward/pallas_call | solution.py:204
  289.7 36.5 %mamba_backward.1 = (bf16[1024,2432]{1,0:T(8,128)(2,1)}, f32[4,1024]{1,0:T(4,128)}, f32[1,768]{1,0:T(1,128)}, f32[1,768]{1,0:T(1,128)}, f32[2,128]{1,0:T(2,128)}, /*index=5*/f32[2,128]{1,0:T(2,128)}) custom-call(f32[1024,2432]{1,0:T(8,128)} %fusion.43.q_ref.kv_ref.proj_ref.before_ref, f32[1024,2432]{1,0:T(8,128)} %fusion.43.q_ref.kv_ref.proj_ref.before_ref, ...), custom_call_target="tpu_custom_call" | custom-call | flops 35999997952 | tf_op jit(solution)/shard_map/mamba_backward/pallas_call | solution.py:577
  332.5 99.6 %collect.1 = (f32[128,768]{1,0:T(8,128)}, f32[128,128]{1,0:T(8,128)}, f32[128,128]{1,0:T(8,128)}, f32[128,512]{1,0:T(8,128)}, f32[88,128]{1,0:T(8,128)}, /*index...) custom-call(bf16[1024,1024]{1,0:T(8,128)(2,1)} %copy-done.7, ...), custom_call_target="tpu_custom_call" | custom-call | flops 80000000000 | tf_op jit(solution)/shard_map/collect/pallas_call | solution.py:1327
  (194 shorter events, 67.0 us)
Async XLA Ops:
  7.2 184.5 %all-gather.2.cloned.1.call-start = ((), (), s32[]{:S(2)}) async-start(), calls=%async_computation.6 | async-start | bytes 5242880 | tf_op jit(solution)/shard_map/all_gather | solution.py:1574
  21.6 106.3 %copy-start.27 = (f32[1024]{0:T(1024)S(1)}, f32[1024]{0:T(1024)}, u32[]{:S(2)}) copy-start(f32[1024]{0:T(1024)} %param.25) | copy-start | bytes 12292
  131.4 8.7 %copy-start.25 = (f32[2,16,128]{2,1,0:T(8,128)S(1)}, f32[2,16,128]{2,1,0:T(8,128)}, u32[]{:S(2)}) copy-start(f32[2,16,128]{2,1,0:T(8,128)} %get-tuple-element.53) | copy-start | bytes 49156
  131.4 8.8 %copy-start.26 = (f32[4,2,128]{2,1,0:T(2,128)S(1)}, f32[4,2,128]{2,1,0:T(2,128)}, u32[]{:S(2)}) copy-start(f32[4,2,128]{2,1,0:T(2,128)} %param.32) | copy-start | bytes 12292
  139.6 4.6 %collective-permute-start.1 = (bf16[2,128,1024]{2,1,0:T(8,128)(2,1)S(1)}, bf16[2,128,1024]{2,1,0:T(8,128)(2,1)S(1)}, u32[]{:S(2)}, u32[]{:S(2)}) collective-permute-start(bf16[2,128,1024]{2,1,0:T(8,128)(2,1)S(1)} %get-tuple-element.139), channel_id=1, source_target_pairs={{0,4},{4,0},{1,5},{5,1},{2,6},{6,2},{3,7},{7,3},{8,12},{12,8},{9,1... | collective-permute-start | bytes 1572872 | tf_op jit(solution)/shard_map/ppermute | solution.py:1422
  139.7 3.9 collective-permute-start
  145.3 30.7 %all-to-all-start = ((bf16[4,128,1024]{2,1,0:T(8,128)(2,1)}), bf16[4,128,1024]{2,1,0:T(8,128)(2,1)S(1)}, u32[]{:S(2)}, u32[]{:S(2)}) async-start(bf16[4,128,1024]{2,1,0:T(8,128)(2,1)} %maximum_select_fusion.1), calls=%async_computation | async-start | bytes 2097152 | tf_op jit(solution)/shard_map/all_to_all | solution.py:1484
  149.9 139.7 %reduce-scatter.9.cloned.1.call-start = ((), (), s32[]{:S(2)}) async-start(), calls=%async_computation.9 | async-start | bytes 2621440 | tf_op jit(solution)/shard_map/reduce_scatter | solution.py:1634
  161.3 15.3 %copy-start.29 = (bf16[1024,1024]{1,0:T(8,128)(2,1)S(1)}, bf16[1024,1024]{1,0:T(8,128)(2,1)}, u32[]{:S(2)}) copy-start(bf16[1024,1024]{1,0:T(8,128)(2,1)} %get-tuple-element.56) | copy-start | bytes 6291460
  176.0 5.3 %collective-permute-start.5 = (bf16[4,128,1024]{2,1,0:T(8,128)(2,1)S(1)}, bf16[4,128,1024]{2,1,0:T(8,128)(2,1)S(1)}, u32[]{:S(2)}, u32[]{:S(2)}) collective-permute-start(bf16[4,128,1024]{2,1,0:T(8,128)(2,1)S(1)} %all-to-all-done), channel_id=1, source_target_pairs={{0,4},{4,0},{1,5},{5,1},{2,6},{6,2},{3,7},{7,3},{8,12},{12,8},{9,1... | collective-permute-start | bytes 3145736 | tf_op jit(solution)/shard_map/ppermute | solution.py:1422
  180.5 7.4 %collective-permute-start.2 = (bf16[1024,1024]{1,0:T(8,128)(2,1)S(1)}, bf16[1024,1024]{1,0:T(8,128)(2,1)S(1)}, u32[]{:S(2)}, u32[]{:S(2)}) collective-permute-start(bf16[1024,1024]{1,0:T(8,128)(2,1)S(1)} %convolution_convert_fusion.4), channel_id=1, source_target_pairs={{0,4},{4,0},{1,5},{5,1},{2,6},{6,2},{3,7},{7,3},{8,12},{12,8},{9,1... | collective-permute-start | bytes 6291464 | tf_op jit(solution)/shard_map/ppermute | solution.py:1422
  208.5 123.9 %reduce-scatter.5.cloned.1.call-start = ((), (), s32[]{:S(2)}) async-start(), calls=%async_computation.7 | async-start | bytes 5242880 | tf_op jit(solution)/shard_map/reduce_scatter | solution.py:1634
  230.0 10.1 %copy-start.14 = (bf16[1024,256]{1,0:T(8,128)(2,1)S(1)}, bf16[1024,256]{1,0:T(8,128)(2,1)}, u32[]{:S(2)}) copy-start(bf16[1024,256]{1,0:T(8,128)(2,1)} %copy-done.13) | copy-start | bytes 1572868
  230.0 10.1 %copy-start.16 = (bf16[1024,256]{1,0:T(8,128)(2,1)S(1)}, bf16[1024,256]{1,0:T(8,128)(2,1)}, u32[]{:S(2)}) copy-start(bf16[1024,256]{1,0:T(8,128)(2,1)} %copy-done.15) | copy-start | bytes 1572868
  230.0 10.1 %copy-start.18 = (bf16[1024,256]{1,0:T(8,128)(2,1)S(1)}, bf16[1024,256]{1,0:T(8,128)(2,1)}, u32[]{:S(2)}) copy-start(bf16[1024,256]{1,0:T(8,128)(2,1)} %copy-done.17) | copy-start | bytes 1572868
  230.0 10.1 %copy-start.20 = (bf16[1024,256]{1,0:T(8,128)(2,1)S(1)}, bf16[1024,256]{1,0:T(8,128)(2,1)}, u32[]{:S(2)}) copy-start(bf16[1024,256]{1,0:T(8,128)(2,1)} %copy-done.19) | copy-start | bytes 1572868
  230.0 10.1 %copy-start.32 = (bf16[1024,1024]{1,0:T(8,128)(2,1)S(1)}, bf16[1024,1024]{1,0:T(8,128)(2,1)}, u32[]{:S(2)}) copy-start(bf16[1024,1024]{1,0:T(8,128)(2,1)} %get-tuple-element.58) | copy-start | bytes 6291460
  239.5 14.4 %collective-permute-start.6 = (bf16[1024,1024]{1,0:T(8,128)(2,1)}, bf16[1024,1024]{1,0:T(8,128)(2,1)}, u32[]{:S(2)}, u32[]{:S(2)}) collective-permute-start(bf16[1024,1024]{1,0:T(8,128)(2,1)} %convolution_convert_fusion.2), channel_id=1, source_target_pairs={{0,4},{4,0},{1,5},{5,1},{2,6},{6,2},{3,7},{7,3},{8,12},{12,8},{9,1... | collective-permute-start | bytes 6291464 | tf_op jit(solution)/shard_map/ppermute | solution.py:1422
  243.5 2.9 collective-permute-start.3
  249.3 190.9 %all-to-all-start.1 = ((bf16[4,128,1024]{2,1,0:T(8,128)(2,1)}), bf16[4,128,1024]{2,1,0:T(8,128)(2,1)}, u32[]{:S(2)}, u32[]{:S(2)}) async-start(bf16[4,128,1024]{2,1,0:T(8,128)(2,1)} %fusion.10), calls=%async_computation.1 | async-start | bytes 2097152 | tf_op jit(solution)/shard_map/all_to_all | solution.py:1491
  253.9 189.0 %reduce-scatter.11.cloned.1.call-start = ((), (), s32[]{:S(2)}) async-start(), calls=%async_computation.10 | async-start | bytes 655360 | tf_op jit(solution)/shard_map/reduce_scatter | solution.py:1644
  289.7 153.3 %reduce-scatter.7.cloned.1.call-start = ((), (), s32[]{:S(2)}) async-start(), calls=%async_computation.8 | async-start | bytes 1310720 | tf_op jit(solution)/shard_map/reduce_scatter | solution.py:1644
  441.6 3.6 collective-permute-start.4
  444.0 2.4 collective-permute-start.7
  (25 other events, 107.7 us)
Sparse Core Ops, SparseCore 0:
  140.3 51.3 all-gather.1
  208.7 35.2 reduce-scatter.8
  247.2 52.6 reduce-scatter.4
  302.0 17.7 reduce-scatter.10
  332.6 25.1 reduce-scatter.6
